TPU v7x, 32 devices: a whole 2x2x4 slice. The times are simulated.
32 devices in a mesh: row: 4 (over z), col: 8 (over y, x, core).
Axes of the slice: x: 2, y: 2, z: 4, core: 2. Of those that a mesh axis runs over, the one named last changes fastest.
Arguments:
- vectors: float32 [1536, 48, 128], P('row', 'col'), may hold values from -0.078125 to 0.078125
- hblocks: float32 [48, 7, 128, 128], P('col'), may hold values from -1 to 1, as said below
- coupling: int32 [48, 6], P('col'), may hold values from 0 to 1, as said below
Outputs:
- projected_ham: float32 [1536, 1536], P('row', 'col')
- intersection: float32 [1536, 1536], P('row', 'col')
Inputs may be any that keep to these rules, and one draw needn't show every extreme that they name: For 1 <= k <= 3 and a >= k, hblocks[a, 3 - k] is the transpose of hblocks[a - k, 3 + k], and hblocks[a, 3] is symmetric, so the Hamiltonian is symmetric. coupling[a, 3 + k - 1] equals coupling[a + k, 3 - k] for 1 <= k <= 3; entries that name an atom outside the chain are 0.
All inputs are finite; a program needn't handle non-finite values.
Results may differ from a plain program's by a relative error of at most 0.0001.
Values sent between devices are 32-bit elements; how exact they have to be, the bound alone decides.
No kernel may reach another device: no remote copies, remote signals or barrier semaphores. Data moves between devices by JAX's collectives and lax.ppermute only.
A program may use at most 64 MiB of HBM per device.

v0:
```python
import jax
import jax.numpy as jnp
from jax import lax
from jax.sharding import PartitionSpec as P

REACH = 3
DEGREE = 3


CENTER = 0.5
HALF_WIDTH = 1.5
HSCALE = 0.1


def with_halo(block, sides, width):
    for axis, dim in sides:
        count = lax.axis_size(axis)
        forward = [(i, i + 1) for i in range(count - 1)]
        backward = [(target, source) for source, target in forward]
        low = lax.ppermute(
            lax.slice_in_dim(block, block.shape[dim] - width, None, axis=dim), axis, forward
        )
        high = lax.ppermute(lax.slice_in_dim(block, 0, width, axis=dim), axis, backward)
        block = jnp.concatenate([low, block, high], axis=dim)
    return block


def masked_blocks(hblocks, coupling):
    ones = jnp.ones((coupling.shape[0], 1), jnp.int32)
    presence = jnp.concatenate([coupling[:, :REACH], ones, coupling[:, REACH:]], axis=1)
    return HSCALE * hblocks * presence.astype(jnp.float32)[:, :, None, None]


def apply_ham(field, blocks):
    atoms = field.shape[1]
    padded = with_halo(field, (("col", 1),), REACH)
    stacked = jnp.stack(
        [padded[:, offset : offset + atoms, :] for offset in range(2 * REACH + 1)], axis=2
    )
    return jnp.einsum("sakj,akij->sai", stacked, blocks, precision=lax.Precision.HIGHEST)


def block_product(left, piece):
    flat_piece = piece.reshape(piece.shape[0], -1)
    return jnp.einsum("sn,tn->st", left, flat_piece, precision=lax.Precision.HIGHEST)


def per_device(vectors, hblocks, coupling):
    blocks = masked_blocks(hblocks, coupling)
    y_prev = vectors
    y_now = (apply_ham(vectors, blocks) - CENTER * vectors) / HALF_WIDTH
    for section in range(DEGREE - 1):
        y_next = 2.0 * (apply_ham(y_now, blocks) - CENTER * y_now) / HALF_WIDTH - y_prev
        y_prev = y_now
        y_now = y_next
    own_rows = y_now.reshape(y_now.shape[0], -1)
    image = apply_ham(y_now, blocks)
    first = block_product(own_rows, lax.all_gather(image, "row", axis=0, tiled=True))
    second = block_product(own_rows, lax.all_gather(y_now, "row", axis=0, tiled=True))
    projected_ham, intersection = (
        lax.psum_scatter(first, "col", scatter_dimension=1, tiled=True),
        lax.psum_scatter(second, "col", scatter_dimension=1, tiled=True),
    )
    return (projected_ham, intersection)


def solution(mesh):
    in_specs = (P("row", "col", None), P("col", None, None, None), P("col", None))
    out_specs = (P("row", "col"), P("row", "col"))
    return jax.shard_map(
        per_device, mesh=mesh, in_specs=in_specs, out_specs=out_specs, check_vma=False
    )
```

profile of v0, /device:TPU:0, one launch (start us, length us, event | category | flops | bytes accessed | tf_op | source)
XLA Modules:
  0.0 362.4 jit_solution(3092274974082693468)
XLA Ops:
  7.2 2.5 fusion.124
  9.7 2.5 collective-permute-start
  12.2 1.3 collective-permute-start.1
  13.5 0.4 copy.9
  14.2 0.2 constant_dynamic-update-slice_fusion.3
  14.7 3.7 %collective-permute-done.1 = f32[384,3,128]{2,0,1:T(8,128)S(1)} collective-permute-done((f32[384,3,128]{2,0,1:T(8,128)}, f32[384,3,128]{2,0,1:T(8,128)S(1)}, u32[]{:S(2)}, u32[]{:S(2)}) %collective-permute-start.1) | collective-permute-done | bytes 589856 | tf_op jit(solution)/shard_map/ppermute | solution.py:23
  18.7 1.6 copy-done.1
  20.3 7.5 %broadcast_multiply_fusion = (f32[384,6,128]{0,2,1:T(8,128)S(1)}, f32[384,6,128]{0,2,1:T(8,128)S(1)}) fusion(f32[384,6,128]{0,2,1:T(8,128)S(1)} %copy.9, f32[384,6,7,128]{3,0,2,1:T(8,128)S(1)} %fusion.114, f32[6,7,128,128]{3,2,1,0:T(8,128)S(1)} %copy-done.1, f32[6,7]{1,0:T(8,128)S(1)} %fusion.120), kind=kOutput, calls=%fused_computation.122 | convolution fusion | flops 3172466688 | bytes 14549160 | tf_op jit(solution)/shard_map/sakj,akij->sai/dot_general | solution.py:40
  27.9 13.3 %collective-permute-start.2 = (f32[384,3,128]{0,2,1:T(8,128)S(1)}, f32[384,3,128]{0,2,1:T(8,128)S(1)}, u32[]{:S(2)}, u32[]{:S(2)}) collective-permute-start(f32[384,3,128]{0,2,1:T(8,128)S(1)} %get-tuple-element.7), channel_id=1, source_target_pairs={{0,1},{1,2},{2,3},{3,4},{4,5},{5,6},{6,7},{8,9},{9,10},{10,11},{11... | collective-permute-start | bytes 1769480 | tf_op jit(solution)/shard_map/ppermute | solution.py:20
  41.2 1.5 collective-permute-start.3
  42.7 0.1 collective-permute-done.2
  43.1 0.1 bitcast_dynamic-update-slice_fusion.2
  43.2 2.0 collective-permute-done.3
  45.4 6.2 %fusion.61 = f32[384,6,128]{0,2,1:T(8,128)S(1)} fusion(f32[384,6,128]{0,2,1:T(8,128)S(1)} %copy.9, f32[384,6,7,128]{0,3,1,2:T(8,128)S(1)} %fusion.111, f32[6,7,128,128]{3,2,1,0:T(8,128)S(1)} %copy-done.1, f32[6,7]{1,0:T(8,128)S(1)} %fusion.120, f32[384,6,128]{0,2,1:T(8,128)S(1)} %get-tuple-element.15), kind=kOutput, calls=%fused_computation.51 | convolution fusion | flops 3172761600 | bytes 14549160 | tf_op jit(solution)/shard_map/sakj,akij->sai/dot_general | solution.py:40
  51.7 12.8 %collective-permute-start.4 = (f32[384,3,128]{0,2,1:T(8,128)S(1)}, f32[384,3,128]{0,2,1:T(8,128)S(1)}, u32[]{:S(2)}, u32[]{:S(2)}) collective-permute-start(f32[384,3,128]{0,2,1:T(8,128)S(1)} %get-tuple-element.5), channel_id=1, source_target_pairs={{0,1},{1,2},{2,3},{3,4},{4,5},{5,6},{6,7},{8,9},{9,10},{10,11},{11... | collective-permute-start | bytes 1769480 | tf_op jit(solution)/shard_map/ppermute | solution.py:20
  64.5 1.5 collective-permute-start.5
  66.4 2.0 collective-permute-done.5
  68.7 7.2 %fusion.46 = f32[384,6,128]{0,2,1:T(8,128)} fusion(f32[384,6,7,128]{0,3,1,2:T(8,128)S(1)} %fusion.107, f32[6,7,128,128]{3,2,1,0:T(8,128)S(1)} %copy-done.1, f32[6,7]{1,0:T(8,128)S(1)} %fusion.120, f32[384,6,128]{0,2,1:T(8,128)S(1)} %fusion.61, f32[384,6,128]{0,2,1:T(8,128)S(1)} %get-tuple-element.15), kind=kOutput, calls=%fused_computation.48 | convolution fusion | flops 3173056512 | bytes 14549160 | tf_op jit(solution)/shard_map/sakj,akij->sai/dot_general | solution.py:40
  75.9 1.2 copy-done
  77.2 12.1 %collective-permute-start.6 = (f32[384,3,128]{0,2,1:T(8,128)S(1)}, f32[384,3,128]{0,2,1:T(8,128)S(1)}, u32[]{:S(2)}, u32[]{:S(2)}) collective-permute-start(f32[384,3,128]{0,2,1:T(8,128)S(1)} %get-tuple-element.3), channel_id=1, source_target_pairs={{0,1},{1,2},{2,3},{3,4},{4,5},{5,6},{6,7},{8,9},{9,10},{10,11},{11... | collective-permute-start | bytes 1769480 | tf_op jit(solution)/shard_map/ppermute | solution.py:20
  89.3 1.7 collective-permute-start.7
  91.4 1.8 collective-permute-done.7
  93.3 0.1 fusion.68
  93.5 0.1 fusion.103
  93.6 1.8 copy-done.2
  95.4 15.0 %fusion.14 = f32[384,6,128]{2,0,1:T(8,128)} fusion(f32[384,6,7,128]{0,3,1,2:T(8,128)S(1)} %fusion.103, f32[6,7,128,128]{3,2,1,0:T(8,128)S(1)} %copy-done.2, f32[6,7]{1,0:T(8,128)S(1)} %fusion.120), kind=kOutput, calls=%fused_computation.38 | convolution fusion | flops 3171581952 | bytes 12189864 | tf_op jit(solution)/shard_map/sakj,akij->sai/dot_general | solution.py:40
  110.5 64.2 %all-gather.5.cloned.1.call-done = f32[1536,6,128]{0,2,1:T(8,128)} async-done(((f32[384,6,128]{0,2,1:T(8,128)}), f32[1536,6,128]{0,2,1:T(8,128)}) %all-gather.5.cloned.1.call-update) | async-done | bytes 4718608 | tf_op jit(solution)/shard_map/all_gather | solution.py:59
  174.6 10.4 %convolution_bitcast_fusion = f32[384,1536]{0,1:T(8,128)} fusion(f32[384,6,128]{0,2,1:T(8,128)S(1)} %copy-done, f32[1536,6,128]{0,2,1:T(8,128)} %all-gather.5.cloned.1.call-done), kind=kOutput, calls=%fused_computation.6 | convolution fusion | flops 5435817984 | bytes 8257536 | tf_op jit(solution)/shard_map/sn,tn->st/dot_general | solution.py:45
  185.1 78.9 %all-gather.3.cloned.1.call-done = f32[1536,6,128]{2,0,1:T(8,128)} async-done(((f32[384,6,128]{2,0,1:T(8,128)}), f32[1536,6,128]{2,0,1:T(8,128)}) %all-gather.3.cloned.1.call-update) | async-done | bytes 4718608 | tf_op jit(solution)/shard_map/all_gather | solution.py:58
  264.0 10.4 %convolution_bitcast_fusion.1 = f32[384,1536]{0,1:T(8,128)} fusion(f32[384,6,128]{0,2,1:T(8,128)S(1)} %copy-done, f32[1536,6,128]{2,0,1:T(8,128)} %all-gather.3.cloned.1.call-done), kind=kOutput, calls=%fused_computation.7 | convolution fusion | flops 5435817984 | bytes 8257536 | tf_op jit(solution)/shard_map/sn,tn->st/dot_general | solution.py:45
  274.5 34.5 %reduce-scatter.5.cloned.1.call-done = f32[384,192]{0,1:T(8,128)} async-done(((f32[384,1536]{0,1:T(8,128)}), f32[384,192]{0,1:T(8,128)}) %reduce-scatter.5.cloned.1.call-update) | async-done | bytes 294928 | tf_op jit(solution)/shard_map/reduce_scatter | solution.py:62
  309.0 46.7 %reduce-scatter.3.cloned.1.call-done = f32[384,192]{0,1:T(8,128)} async-done(((f32[384,1536]{0,1:T(8,128)}), f32[384,192]{0,1:T(8,128)}) %reduce-scatter.3.cloned.1.call-update) | async-done | bytes 294928 | tf_op jit(solution)/shard_map/reduce_scatter | solution.py:61
  (51 shorter events, 2.9 us)
Async XLA Ops:
  7.2 6.3 %copy-start.3 = (f32[384,6,128]{2,0,1:T(8,128)S(1)}, f32[384,6,128]{2,0,1:T(8,128)}, u32[]{:S(2)}) copy-start(f32[384,6,128]{2,0,1:T(8,128)} %param.3) | copy-start | bytes 3538948
  7.2 167.4 %all-gather.5.cloned.1.call-start = ((), (), s32[]{:S(2)}) async-start(), calls=%async_computation.4 | async-start | bytes 5898240 | tf_op jit(solution)/shard_map/all_gather | solution.py:59
  9.7 4.3 %copy-start.4 = (s32[6,6]{1,0:T(8,128)S(1)}, s32[6,6]{1,0:T(8,128)}, u32[]{:S(2)}) copy-start(s32[6,6]{1,0:T(8,128)} %param.5) | copy-start | bytes 436
  9.7 4.4 %collective-permute-start = (f32[384,3,128]{2,0,1:T(8,128)}, f32[384,3,128]{2,0,1:T(8,128)S(1)}, u32[]{:S(2)}, u32[]{:S(2)}) collective-permute-start(f32[384,3,128]{2,0,1:T(8,128)} %get-tuple-element.9), channel_id=1, source_target_pairs={{0,1},{1,2},{2,3},{3,4},{4,5},{5,6},{6,7},{8,9},{9,10},{10,11},{11... | collective-permute-start | bytes 1769480 | tf_op jit(solution)/shard_map/ppermute | solution.py:20
  12.2 6.2 %collective-permute-start.1 = (f32[384,3,128]{2,0,1:T(8,128)}, f32[384,3,128]{2,0,1:T(8,128)S(1)}, u32[]{:S(2)}, u32[]{:S(2)}) collective-permute-start(f32[384,3,128]{2,0,1:T(8,128)} %get-tuple-element.8), channel_id=1, source_target_pairs={{1,0},{2,1},{3,2},{4,3},{5,4},{6,5},{7,6},{9,8},{10,9},{11,10},{12... | collective-permute-start | bytes 1769480 | tf_op jit(solution)/shard_map/ppermute | solution.py:23
  18.5 1.8 copy-start.1
  27.9 14.9 %collective-permute-start.2 = (f32[384,3,128]{0,2,1:T(8,128)S(1)}, f32[384,3,128]{0,2,1:T(8,128)S(1)}, u32[]{:S(2)}, u32[]{:S(2)}) collective-permute-start(f32[384,3,128]{0,2,1:T(8,128)S(1)} %get-tuple-element.7), channel_id=1, source_target_pairs={{0,1},{1,2},{2,3},{3,4},{4,5},{5,6},{6,7},{8,9},{9,10},{10,11},{11... | collective-permute-start | bytes 1769480 | tf_op jit(solution)/shard_map/ppermute | solution.py:20
  41.2 3.9 %collective-permute-start.3 = (f32[384,3,128]{0,2,1:T(8,128)S(1)}, f32[384,3,128]{0,2,1:T(8,128)S(1)}, u32[]{:S(2)}, u32[]{:S(2)}) collective-permute-start(f32[384,3,128]{0,2,1:T(8,128)S(1)} %get-tuple-element.6), channel_id=1, source_target_pairs={{1,0},{2,1},{3,2},{4,3},{5,4},{6,5},{7,6},{9,8},{10,9},{11,10},{12... | collective-permute-start | bytes 1769480 | tf_op jit(solution)/shard_map/ppermute | solution.py:23
  51.7 14.4 %collective-permute-start.4 = (f32[384,3,128]{0,2,1:T(8,128)S(1)}, f32[384,3,128]{0,2,1:T(8,128)S(1)}, u32[]{:S(2)}, u32[]{:S(2)}) collective-permute-start(f32[384,3,128]{0,2,1:T(8,128)S(1)} %get-tuple-element.5), channel_id=1, source_target_pairs={{0,1},{1,2},{2,3},{3,4},{4,5},{5,6},{6,7},{8,9},{9,10},{10,11},{11... | collective-permute-start | bytes 1769480 | tf_op jit(solution)/shard_map/ppermute | solution.py:20
  64.5 3.9 %collective-permute-start.5 = (f32[384,3,128]{0,2,1:T(8,128)S(1)}, f32[384,3,128]{0,2,1:T(8,128)S(1)}, u32[]{:S(2)}, u32[]{:S(2)}) collective-permute-start(f32[384,3,128]{0,2,1:T(8,128)S(1)} %get-tuple-element.4), channel_id=1, source_target_pairs={{1,0},{2,1},{3,2},{4,3},{5,4},{6,5},{7,6},{9,8},{10,9},{11,10},{12... | collective-permute-start | bytes 1769480 | tf_op jit(solution)/shard_map/ppermute | solution.py:23
  75.9 1.3 copy-start
  75.9 188.1 %all-gather.3.cloned.1.call-start = ((), (), s32[]{:S(2)}) async-start(), calls=%async_computation.2 | async-start | bytes 5898240 | tf_op jit(solution)/shard_map/all_gather | solution.py:58
  77.2 13.8 %collective-permute-start.6 = (f32[384,3,128]{0,2,1:T(8,128)S(1)}, f32[384,3,128]{0,2,1:T(8,128)S(1)}, u32[]{:S(2)}, u32[]{:S(2)}) collective-permute-start(f32[384,3,128]{0,2,1:T(8,128)S(1)} %get-tuple-element.3), channel_id=1, source_target_pairs={{0,1},{1,2},{2,3},{3,4},{4,5},{5,6},{6,7},{8,9},{9,10},{10,11},{11... | collective-permute-start | bytes 1769480 | tf_op jit(solution)/shard_map/ppermute | solution.py:20
  89.3 3.9 %collective-permute-start.7 = (f32[384,3,128]{0,2,1:T(8,128)S(1)}, f32[384,3,128]{0,2,1:T(8,128)S(1)}, u32[]{:S(2)}, u32[]{:S(2)}) collective-permute-start(f32[384,3,128]{0,2,1:T(8,128)S(1)} %get-tuple-element.2), channel_id=1, source_target_pairs={{1,0},{2,1},{3,2},{4,3},{5,4},{6,5},{7,6},{9,8},{10,9},{11,10},{12... | collective-permute-start | bytes 1769480 | tf_op jit(solution)/shard_map/ppermute | solution.py:23
  93.4 1.9 copy-start.2
  110.4 198.6 %reduce-scatter.5.cloned.1.call-start = ((), (), s32[]{:S(2)}) async-start(), calls=%async_computation.5 | async-start | bytes 2654208 | tf_op jit(solution)/shard_map/reduce_scatter | solution.py:62
  185.1 170.6 %reduce-scatter.3.cloned.1.call-start = ((), (), s32[]{:S(2)}) async-start(), calls=%async_computation.3 | async-start | bytes 2654208 | tf_op jit(solution)/shard_map/reduce_scatter | solution.py:61
Sparse Core Ops, SparseCore 0:
  76.0 98.5 all-gather.4
  176.2 87.8 all-gather.2
  268.0 40.9 reduce-scatter.4
  313.1 42.4 reduce-scatter.2
where the time goes:
time: 369 us; the launch traced here: 362 us
  waiting for transfers between devices  234 us (63%)
  matrix products  56.8 us (15%)
  starting transfers between devices  46.8 us (13%)
  between operations  14.3 us (4%)
  local copies, waits for them, and re-layouts  8.73 us (2%)
    all_gather x1, waiting for transfers between devices, per_device(): lax.all_gather(image, 'row', axis=0, tiled=True)  78.9 us
    all_gather x1, waiting for transfers between devices, per_device(): lax.all_gather(y_now, 'row', axis=0, tiled=True)  64.2 us
    reduce_scatter x1, waiting for transfers between devices, per_device(): lax.psum_scatter(first, 'col', scatter_dimension=1, tiled=True)  46.7 us
    ppermute x4, starting transfers between devices, with_halo(): lax.ppermute(lax.slice_in_dim(block, block.shape[dim] - width, None, axis...  40.7 us
    dot_general x4, matrix products, apply_ham(): jnp.einsum('sakj,akij->sai', stacked, blocks, precision=lax.Precision.HIG...  35.9 us
    reduce_scatter x1, waiting for transfers between devices, per_device(): lax.psum_scatter(second, 'col', scatter_dimension=1, tiled=True)  34.5 us
    dot_general x2, matrix products, block_product(): jnp.einsum('sn,tn->st', left, flat_piece, precision=lax.Precision.HIGHEST)  20.9 us
    ppermute x4, waiting for transfers between devices, with_halo(): lax.ppermute(lax.slice_in_dim(block, 0, width, axis=dim), axis, backward)  9.48 us
  transfers between devices with their start and end apart: 12, of which 10 were waited for; matrix products, arithmetic and copies ran while one was open for 11% of the time, Pallas kernels for 0%

commit v1 on v0

v1 whole, which is shorter than its diff:
```python
import functools

import jax
import jax.numpy as jnp
from jax import lax
from jax.experimental import pallas as pl
from jax.experimental.pallas import tpu as pltpu
from jax.sharding import PartitionSpec as P

REACH = 3
DEGREE = 3
CENTER = 0.5
HALF_WIDTH = 1.5
HSCALE = 0.1
PARTS = 2

WHOLE = pl.BlockSpec(memory_space=pltpu.VMEM)
SCALARS = pl.BlockSpec(memory_space=pltpu.SMEM)
ANYWHERE = pl.BlockSpec(memory_space=pl.ANY)
NN = ((1,), (0,))


def call(kernel, out_shape, arrays, specs, name, mib, flops=0, scratch=(), after=()):
    outs = list(out_shape)
    moved = sum(a.size * a.dtype.itemsize for a in list(arrays) + outs)
    count, made, late = len(arrays), len(outs), len(after)

    def body(*refs):
        inner = refs[count + late :]
        kernel(*refs[:count], *inner[:made], *inner[made + late :])

    return list(pl.pallas_call(
        body,
        out_shape=outs + [jax.ShapeDtypeStruct(a.shape, a.dtype) for a in after],
        in_specs=[*specs] + [ANYWHERE] * late,
        out_specs=[WHOLE] * made + [ANYWHERE] * late,
        scratch_shapes=list(scratch),
        input_output_aliases={count + i: made + i for i in range(late)},
        compiler_params=pltpu.CompilerParams(vmem_limit_bytes=mib * 1024 * 1024),
        cost_estimate=pl.CostEstimate(flops=int(flops), bytes_accessed=moved, transcendentals=0),
        name=name,
    )(*arrays, *after))


def f32(*shape):
    return jax.ShapeDtypeStruct(shape, jnp.float32)


def bf16(*shape):
    return jax.ShapeDtypeStruct(shape, jnp.bfloat16)


def split(x):
    high = x.astype(jnp.bfloat16)
    low = (x - high.astype(jnp.float32)).astype(jnp.bfloat16)
    return high, low


def dot(a, b):
    return lax.dot_general(a, b, (NN, ((), ())), preferred_element_type=jnp.float32)


def dot3(a, b):
    rows = a[0].shape[0]
    both = dot(jnp.concatenate(a, axis=0), b[0])
    return both[:rows] + (both[rows:] + dot(a[0], b[1]))


def arrange_kernel(groups, width, odd_ref, v_ref, mine_ref, theirs_ref, *parts):
    odd = odd_ref[0]
    atoms, states, size = v_ref.shape
    half = atoms // 2
    rows = states // PARTS
    for k in range(atoms):
        column = v_ref[jnp.where(odd == 1, atoms - 1 - k, k)]
        at = slice((k % half) * size, (k % half + 1) * size)
        for part in range(PARTS):
            parts[2 * part + k // half][:, at] = column[part * rows : (part + 1) * rows]
        for group in range(groups):
            low = column[2 * group * width : (2 * group + 1) * width]
            high = column[(2 * group + 1) * width : (2 * group + 2) * width]
            to = slice(group * width, (group + 1) * width)
            mine_ref[to, k * size : (k + 1) * size] = jnp.where(odd == 1, high, low)
            theirs_ref[to, k * size : (k + 1) * size] = jnp.where(odd == 1, low, high)


def arrange(odd, vectors, width):
    states, atoms, size = vectors.shape
    out = [f32(states // 2, atoms * size)] * 2 + [f32(states // PARTS, atoms // 2 * size)] * (2 * PARTS)
    kernel = functools.partial(arrange_kernel, states // (2 * width), width)
    by_atom = jnp.transpose(vectors, (1, 0, 2))
    mine, theirs, *parts = call(kernel, out, [odd, by_atom], [SCALARS, WHOLE], "arrange", 8)
    return mine, theirs, [parts[2 * p : 2 * p + 2] for p in range(PARTS)]


def weights_kernel(atoms, odd_ref, coupling_ref, h_ref, own_h, own_l, far_h, far_l, near_h, near_l):
    odd = odd_ref[0]
    size = h_ref.shape[-1]

    def block(k, d):
        a = jnp.where(odd == 1, atoms - 1 - k, k)
        s = jnp.where(odd == 1, -d, d)
        h = HSCALE * h_ref[a, s + REACH]
        if d != 0:
            place = jnp.where(s < 0, s + REACH, s + REACH - 1)
            h = h * coupling_ref[a, place].astype(jnp.float32)
        return split(h.T)

    def put(high_ref, low_ref, row, column, value):
        rows = slice(row * size, (row + 1) * size)
        columns = slice(column * size, (column + 1) * size)
        high_ref[rows, columns], low_ref[rows, columns] = value

    zero = jnp.zeros((size, size), jnp.bfloat16)
    for m in range(atoms):
        for k in range(atoms):
            put(own_h, own_l, m, k, block(k, m - k) if abs(m - k) <= REACH else (zero, zero))
    for n in range(REACH):
        for j in range(REACH):
            d = -1 - n - j
            put(far_h, far_l, n, j, block(j, d) if d >= -REACH else (zero, zero))
            k = atoms - REACH + j
            d = atoms + REACH - 1 - n - k
            put(near_h, near_l, n, j, block(k, d) if d <= REACH else (zero, zero))


def make_weights(odd, coupling, hblocks):
    atoms, size = hblocks.shape[0], hblocks.shape[-1]
    full, edge = atoms * size, REACH * size
    out = [bf16(full, full)] * 2 + [bf16(edge, edge)] * 4
    kernel = functools.partial(weights_kernel, atoms)
    return call(kernel, out, [odd, coupling, hblocks], [SCALARS, SCALARS, WHOLE], "weights", 10)


def base_kernel(scales, high_ref, low_ref, *rest):
    out_ref = rest[-1]
    fields = [(rest[2 * i], rest[2 * i + 1]) for i in range((len(rest) - 1) // 2)]
    edge = rest[0].shape[1]
    halves = [split(ref[...]) for ref in fields[0]]
    operand = [jnp.concatenate([halves[0][term], halves[1][term]], axis=1) for term in range(2)]
    for side in range(2):
        columns = slice(side * edge, (side + 1) * edge)
        value = scales[0] * dot3(operand, (high_ref[:, columns], low_ref[:, columns]))
        for scale, field in zip(scales[1:], fields):
            if scale:
                value = value + scale * field[side][...]
        out_ref[:, columns] = value


def make_base(scales, weights, fields, after):
    arrays = list(weights[:2]) + [half for field in fields for half in field]
    rows, edge = fields[0][0].shape
    flops = 6 * rows * 4 * edge * edge
    return call(functools.partial(base_kernel, scales), [f32(rows, 2 * edge)], arrays, [WHOLE] * len(arrays), "base", 10, flops, (), after)


def tail_kernel(scale, base, got_far, got_near, fh, fl, nh, nl, *outs):
    edge = got_far.shape[1]
    for side, (got, high, low) in enumerate(((got_far, fh, fl), (got_near, nh, nl))):
        columns = slice(side * edge, (side + 1) * edge)
        value = base[:, columns] + scale * dot3(split(got[...]), (high[...], low[...]))
        if len(outs) == 2:
            outs[side][...] = value
        else:
            outs[0][:, columns] = value


def make_tail(scale, base, got, weights, joined, after):
    arrays = [base, *got, *weights[2:]]
    rows, edge = got[0].shape
    out = [f32(rows, 2 * edge)] if joined else [f32(rows, edge)] * 2
    flops = 6 * rows * 2 * edge * edge
    return call(functools.partial(tail_kernel, scale), out, arrays, [WHOLE] * len(arrays), "tail", 8, flops, (), after)


def assemble_kernel(all_ref, *outs):
    planes, _, rows, depth = all_ref.shape
    step = 128
    for side in range(2):
        for at in range(0, depth, step):
            columns = [all_ref[plane, side, :, at : at + step] for plane in range(planes)]
            term = split(jnp.concatenate(columns, axis=0).T)
            outs[2 * side][at : at + step], outs[2 * side + 1][at : at + step] = term


def assemble(gathered, after):
    planes, _, rows, depth = gathered.shape
    out = [bf16(depth, planes * rows)] * 4
    return call(assemble_kernel, out, [gathered], [WHOLE], "assemble", 10, 0, (), after)


def product_kernel(own_h, own_l, other_h, other_l, *rest):
    out_ref = rest[-1]
    half = len(rest) // 2
    value = dot3(split(joined(rest[:half])), (own_h[...], own_l[...]))
    value = value + dot3(split(joined(rest[half:-1])), (other_h[...], other_l[...]))
    out_ref[...] = value.T


def joined(refs):
    parts = len(refs) // PARTS
    rows = [
        jnp.concatenate([ref[...] for ref in refs[parts * p : parts * (p + 1)]], axis=1) for p in range(PARTS)
    ]
    return jnp.concatenate(rows, axis=0)


def product(everything, own, other):
    depth, width = everything[0].shape
    arrays = [*everything] + [half for part in own + other for half in part]
    rows = sum(part[0].shape[0] for part in own)
    flops = 12 * rows * depth * width
    return call(product_kernel, [f32(width, rows)], arrays, [WHOLE] * len(arrays), "product", 14, flops)[0]


def halve(part, axis_at, mine, count, bit):
    other = lax.dynamic_index_in_dim(part, 1 - mine, axis_at, keepdims=False)
    kept = lax.dynamic_index_in_dim(part, mine, axis_at, keepdims=False)
    return kept + lax.ppermute(other, "col", [(i, i ^ (1 << bit)) for i in range(count)])


def reduce_step(part, step, low_first):
    count = lax.axis_size("col")
    me = lax.axis_index("col").astype(jnp.int32)
    bits = count.bit_length() - 1
    if step == 1:
        part = part.reshape((2,) * (bits - 1) + (part.shape[0] * 2 // count, part.shape[1]))
    bit = step if low_first else bits - step
    return halve(part, bits - 1 - step if low_first else 0, (me >> bit) % 2, count, bit)


def reduce_rest(part, done, low_first):
    bits = lax.axis_size("col").bit_length() - 1
    for step in range(done + 1, bits):
        part = reduce_step(part, step, low_first)
    return part


def per_device(vectors, hblocks, coupling):
    count = lax.axis_size("col")
    me = lax.axis_index("col").astype(jnp.int32)
    odd = (me % 2).reshape(1)
    width = vectors.shape[0] * lax.axis_size("row") // count
    inner = [(i, i ^ 1) for i in range(count)]
    outer = [(i, i + 1) for i in range(1, count - 1, 2)]
    outer = outer + [(b, a) for a, b in outer]

    mine, theirs, start = arrange(odd, vectors, width)
    weights = make_weights(odd, coupling, hblocks)
    groups = mine.shape[0] // width
    cut = width // 24 * 16 or width
    payload = [x.reshape(groups, width, -1) for x in (mine, lax.ppermute(theirs, "col", inner))]

    def gather(at, to):
        slab = jnp.stack([x[:, at:to].reshape(groups * (to - at), -1) for x in payload])
        return lax.all_gather(slab, "row", axis=0)

    gathered = [gather(0, cut), gather(cut, width)]

    def send(now):
        return [lax.ppermute(now[0], "col", outer), lax.ppermute(now[1], "col", inner)]

    scale = 1.0 / HALF_WIDTH
    plans = [(scale, -CENTER * scale)] + [(2.0 * scale, -2.0 * CENTER * scale, -1.0)] * (2 * DEGREE - 2)
    plans.append((scale, -CENTER * scale, -0.5, 0.5))
    plans.append((1.0, 0.0))
    fields = [[part] for part in start]
    for at, plan in enumerate(plans):
        got = [send(fields[p][-1]) for p in range(PARTS)]
        for p in range(PARTS):
            now = fields[p][-1]
            used = [now] + (fields[p][-2:-1] if len(plan) > 2 else []) + ([start[p]] if len(plan) > 3 else [])
            (base,) = make_base(plan, weights, used, [])
            fields[p].append(make_tail(plan[0], base, got[p], weights, at == len(plans) - 1, []))
    filtered = [field[-2] for field in fields]
    image = [field[-1] for field in fields]
    other_filtered = [[lax.ppermute(filtered[p][0], "col", inner), got[p][1]] for p in range(PARTS)]
    other_image = [[lax.ppermute(image[p][0], "col", inner)] for p in range(PARTS)]

    everything = assemble(gathered[0], [])
    sums = reduce_step(product(everything, filtered, other_filtered), 1, True)
    image_sums = product(everything, image, other_image)
    *everything, sums, image_sums = assemble(gathered[1], [sums, image_sums])
    more = product(everything, filtered, other_filtered)
    more_image = product(everything, image, other_image)
    intersection = [reduce_rest(sums, 1, True), reduce_rest(more, 0, True)]
    projected_ham = [reduce_rest(image_sums, 0, False), reduce_rest(more_image, 0, False)]
    return jnp.concatenate(projected_ham, axis=0).T, jnp.concatenate(intersection, axis=0).T


def solution(mesh):
    in_specs = (P("row", "col", None), P("col", None, None, None), P("col", None))
    out_specs = (P("row", "col"), P("row", "col"))
    return jax.shard_map(
        per_device, mesh=mesh, in_specs=in_specs, out_specs=out_specs, check_vma=False
    )
```

time: 369 us -> 184 us (0.50); the launches traced: 362 us -> 182 us
  waiting for transfers between devices: 234 us -> 19.1 us
  matrix products: 56.8 us -> 0 us
  Pallas kernels: 0 us -> 56.5 us
  starting transfers between devices: 46.8 us -> 64.8 us
  local copies, waits for them, and re-layouts: 8.73 us -> 22.4 us
    all_gather x2, waiting for transfers between devices: 143 us -> 0.02 us  [gather(): return lax.all_gather(slab, 'row', axis=0)]
    reduce_scatter x2 -> x0, waiting for transfers between devices: 81.1 us -> none  [the longest x1 46.7 us: per_device(): lax.psum_scatter(first, 'col', scatter_dimension=1, tiled=True)]
    dot_general x6 -> x0, matrix products: 56.8 us -> none  [the longest x4 35.9 us: apply_ham(): jnp.einsum('sakj,akij->sai', stacked, blocks, precision=lax.Precision.HIG...]
    pallas_call x0 -> x36, Pallas kernels: none -> 56.5 us  [call(): pl.pallas_call(body, out_shape=outs + [jax.ShapeDtypeStruct(a.shape, a.dt...]
    ppermute x8 -> x41, starting transfers between devices: 46.7 us -> 64.7 us  [the longest x14 37.9 us: send(): lax.ppermute(now[1], 'col', inner)]
    unnamed x21 -> x78, local copies, waits for them, and re-layouts: 5.78 us -> 19.5 us
    ppermute x8 -> x41, waiting for transfers between devices: 9.65 us -> 19 us  [the longest x8 17.7 us: halve(): lax.ppermute(other, 'col', [(i, i ^ 1 << bit) for i in range(count)])]
  transfers between devices with their start and end apart: 12 -> 43, of which waited for: 10 -> 6; matrix products, arithmetic and copies ran while one was open for 11% -> 3% of each run, Pallas kernels for 0% -> 30%
where the time goes in v1:
time: 184 us; the launch traced here: 182 us
  starting transfers between devices  64.8 us (35%)
  Pallas kernels  56.5 us (31%)
  local copies, waits for them, and re-layouts  22.4 us (12%)
  waiting for transfers between devices  19.1 us (10%)
  between operations  14.9 us (8%)
  other arithmetic  4.41 us (2%)
    pallas_call x36, Pallas kernels, call(): pl.pallas_call(body, out_shape=outs + [jax.ShapeDtypeStruct(a.shape, a.dt...  56.5 us
    ppermute x14, starting transfers between devices, send(): lax.ppermute(now[1], 'col', inner)  37.9 us
    unnamed x78, local copies, waits for them, and re-layouts  19.5 us
    ppermute x8, waiting for transfers between devices, halve(): lax.ppermute(other, 'col', [(i, i ^ 1 << bit) for i in range(count)])  17.7 us
    ppermute x14, starting transfers between devices, send(): lax.ppermute(now[0], 'col', outer)  11.1 us
    ppermute x8, starting transfers between devices, halve(): lax.ppermute(other, 'col', [(i, i ^ 1 << bit) for i in range(count)])  8.51 us
    ppermute x2, starting transfers between devices, per_device(): lax.ppermute(image[p][0], 'col', inner)  4.24 us
  transfers between devices with their start and end apart: 43, of which 6 were waited for; matrix products, arithmetic and copies ran while one was open for 3% of the time, Pallas kernels for 30%

profile of v1, /device:TPU:0, one launch (start us, length us, event | category | flops | bytes accessed | tf_op | source)
XLA Modules:
  0.0 182.1 jit_solution(11177459375245705267)
XLA Ops:
  14.3 4.3 %collective-permute-start.14 = (f32[192,384]{1,0:T(8,128)}, f32[192,384]{1,0:T(8,128)S(1)}, u32[]{:S(2)}, u32[]{:S(2)}) collective-permute-start(f32[192,384]{1,0:T(8,128)} %get-tuple-element.75.refs_3_.refs_5_.refs_7_), channel_id=1, source_target_pairs={{0,1},{1,0},{2,3},{3,2},{4,5},{5,4},{6,7},{7,6},{8,9},{9,8},{10,11... | collective-permute-start | bytes 884744 | tf_op jit(solution)/shard_map/ppermute | solution.py:261
  19.2 2.9 %collective-permute-start.2 = (f32[192,384]{1,0:T(8,128)}, f32[192,384]{1,0:T(8,128)S(1)}, u32[]{:S(2)}, u32[]{:S(2)}) collective-permute-start(f32[192,384]{1,0:T(8,128)} %get-tuple-element.57.refs_3_.refs_5_.refs_7_), channel_id=1, source_target_pairs={{0,1},{1,0},{2,3},{3,2},{4,5},{5,4},{6,7},{7,6},{8,9},{9,8},{10,11... | collective-permute-start | bytes 884744 | tf_op jit(solution)/shard_map/ppermute | solution.py:261
  25.6 2.2 %base.20.refs_0_ = f32[192,768]{1,0:T(8,128)S(1)} custom-call(bf16[768,768]{1,0:T(8,128)(2,1)S(1)} %get-tuple-element.54.refs_0_, bf16[768,768]{1,0:T(8,128)(2,1)S(1)} %get-tuple-element.55.refs_1_, f32[192,384]{1,0:T(8,128)} %get-tuple-element.74.refs_2_.refs_4_.refs_6_, f32[192,384]{1,0:T(8,128)} %get-tuple-element.75.refs_3_.refs_5_.refs_7_), custom_call_target="tpu_custom_call" | custom-call | flops 679477248 | bytes 3538944 | tf_op jit(solution)/shard_map/base/pallas_call | solution.py:32
  29.2 2.9 %collective-permute-start.16 = (f32[192,384]{1,0:T(8,128)S(1)}, f32[192,384]{1,0:T(8,128)S(1)}, u32[]{:S(2)}, u32[]{:S(2)}) collective-permute-start(f32[192,384]{1,0:T(8,128)S(1)} %get-tuple-element.77.refs_3_.refs_5_), channel_id=1, source_target_pairs={{0,1},{1,0},{2,3},{3,2},{4,5},{5,4},{6,7},{7,6},{8,9},{9,8},{10,11... | collective-permute-start | bytes 884744 | tf_op jit(solution)/shard_map/ppermute | solution.py:261
  32.1 2.1 %base.14.refs_0_ = f32[192,768]{1,0:T(8,128)S(1)} custom-call(bf16[768,768]{1,0:T(8,128)(2,1)S(1)} %get-tuple-element.54.refs_0_, bf16[768,768]{1,0:T(8,128)(2,1)S(1)} %get-tuple-element.55.refs_1_, f32[192,384]{1,0:T(8,128)} %get-tuple-element.56.refs_2_.refs_4_.refs_6_, f32[192,384]{1,0:T(8,128)} %get-tuple-element.57.refs_3_.refs_5_.refs_7_), custom_call_target="tpu_custom_call" | custom-call | flops 679477248 | bytes 3538944 | tf_op jit(solution)/shard_map/base/pallas_call | solution.py:32
  35.7 2.3 %collective-permute-start.4 = (f32[192,384]{1,0:T(8,128)S(1)}, f32[192,384]{1,0:T(8,128)S(1)}, u32[]{:S(2)}, u32[]{:S(2)}) collective-permute-start(f32[192,384]{1,0:T(8,128)S(1)} %get-tuple-element.63.refs_3_.refs_5_), channel_id=1, source_target_pairs={{0,1},{1,0},{2,3},{3,2},{4,5},{5,4},{6,7},{7,6},{8,9},{9,8},{10,11... | collective-permute-start | bytes 884744 | tf_op jit(solution)/shard_map/ppermute | solution.py:261
  38.0 2.2 %base.21.refs_0_ = f32[192,768]{1,0:T(8,128)S(1)} custom-call(bf16[768,768]{1,0:T(8,128)(2,1)S(1)} %get-tuple-element.54.refs_0_, bf16[768,768]{1,0:T(8,128)(2,1)S(1)} %get-tuple-element.55.refs_1_, f32[192,384]{1,0:T(8,128)S(1)} %get-tuple-element.76.refs_2_.refs_4_, f32[192,384]{1,0:T(8,128)S(1)} %get-tuple-element.77.refs_3_.refs_5_, ...), custom_call_target="tpu_custom_call" | custom-call | flops 679477248 | bytes 4128768 | tf_op jit(solution)/shard_map/base/pallas_call | solution.py:32
  41.7 2.9 %collective-permute-start.18 = (f32[192,384]{1,0:T(8,128)S(1)}, f32[192,384]{1,0:T(8,128)S(1)}, u32[]{:S(2)}, u32[]{:S(2)}) collective-permute-start(f32[192,384]{1,0:T(8,128)S(1)} %get-tuple-element.79.refs_3_.refs_5_), channel_id=1, source_target_pairs={{0,1},{1,0},{2,3},{3,2},{4,5},{5,4},{6,7},{7,6},{8,9},{9,8},{10,11... | collective-permute-start | bytes 884744 | tf_op jit(solution)/shard_map/ppermute | solution.py:261
  44.6 2.2 %base.15.refs_0_ = f32[192,768]{1,0:T(8,128)S(1)} custom-call(bf16[768,768]{1,0:T(8,128)(2,1)S(1)} %get-tuple-element.54.refs_0_, bf16[768,768]{1,0:T(8,128)(2,1)S(1)} %get-tuple-element.55.refs_1_, f32[192,384]{1,0:T(8,128)S(1)} %get-tuple-element.62.refs_2_.refs_4_, f32[192,384]{1,0:T(8,128)S(1)} %get-tuple-element.63.refs_3_.refs_5_, ...), custom_call_target="tpu_custom_call" | custom-call | flops 679477248 | bytes 4128768 | tf_op jit(solution)/shard_map/base/pallas_call | solution.py:32
  57.5 2.5 %collective-permute-start.20 = (f32[192,384]{1,0:T(8,128)}, f32[192,384]{1,0:T(8,128)}, u32[]{:S(2)}, u32[]{:S(2)}) collective-permute-start(f32[192,384]{1,0:T(8,128)} %get-tuple-element.81.refs_3_.refs_5_), channel_id=1, source_target_pairs={{0,1},{1,0},{2,3},{3,2},{4,5},{5,4},{6,7},{7,6},{8,9},{9,8},{10,11... | collective-permute-start | bytes 884744 | tf_op jit(solution)/shard_map/ppermute | solution.py:261
  62.7 2.2 %base.16.refs_0_ = f32[192,768]{1,0:T(8,128)S(1)} custom-call(bf16[768,768]{1,0:T(8,128)(2,1)S(1)} %get-tuple-element.54.refs_0_, bf16[768,768]{1,0:T(8,128)(2,1)S(1)} %get-tuple-element.55.refs_1_, f32[192,384]{1,0:T(8,128)} %get-tuple-element.64.refs_2_.refs_4_, f32[192,384]{1,0:T(8,128)} %get-tuple-element.65.refs_3_.refs_5_, f32[192,384]{1,0:T(8,128)S(1)} %copy-done.16, ...), custom_call_target="tpu_custom_call" | custom-call | flops 679477248 | bytes 4128768 | tf_op jit(solution)/shard_map/base/pallas_call | solution.py:32
  67.4 2.5 %collective-permute-start.8 = (f32[192,384]{1,0:T(8,128)S(1)}, f32[192,384]{1,0:T(8,128)S(1)}, u32[]{:S(2)}, u32[]{:S(2)}) collective-permute-start(f32[192,384]{1,0:T(8,128)S(1)} %get-tuple-element.67.refs_3_.refs_5_), channel_id=1, source_target_pairs={{0,1},{1,0},{2,3},{3,2},{4,5},{5,4},{6,7},{7,6},{8,9},{9,8},{10,11... | collective-permute-start | bytes 884744 | tf_op jit(solution)/shard_map/ppermute | solution.py:261
  69.9 2.2 %base.23.refs_0_ = f32[192,768]{1,0:T(8,128)S(1)} custom-call(bf16[768,768]{1,0:T(8,128)(2,1)S(1)} %get-tuple-element.54.refs_0_, bf16[768,768]{1,0:T(8,128)(2,1)S(1)} %get-tuple-element.55.refs_1_, f32[192,384]{1,0:T(8,128)} %get-tuple-element.80.refs_2_.refs_4_, f32[192,384]{1,0:T(8,128)} %get-tuple-element.81.refs_3_.refs_5_, f32[192,384]{1,0:T(8,128)S(1)} %copy-done.12, ...), custom_call_target="tpu_custom_call" | custom-call | flops 679477248 | bytes 4128768 | tf_op jit(solution)/shard_map/base/pallas_call | solution.py:32
  74.6 2.8 %collective-permute-start.22 = (f32[192,384]{1,0:T(8,128)S(1)}, f32[192,384]{1,0:T(8,128)S(1)}, u32[]{:S(2)}, u32[]{:S(2)}) collective-permute-start(f32[192,384]{1,0:T(8,128)S(1)} %get-tuple-element.83.refs_3_.refs_5_), channel_id=1, source_target_pairs={{0,1},{1,0},{2,3},{3,2},{4,5},{5,4},{6,7},{7,6},{8,9},{9,8},{10,11... | collective-permute-start | bytes 884744 | tf_op jit(solution)/shard_map/ppermute | solution.py:261
  77.4 2.2 %base.17.refs_0_ = f32[192,768]{1,0:T(8,128)S(1)} custom-call(bf16[768,768]{1,0:T(8,128)(2,1)S(1)} %get-tuple-element.54.refs_0_, bf16[768,768]{1,0:T(8,128)(2,1)S(1)} %get-tuple-element.55.refs_1_, f32[192,384]{1,0:T(8,128)S(1)} %get-tuple-element.66.refs_2_.refs_4_, f32[192,384]{1,0:T(8,128)S(1)} %get-tuple-element.67.refs_3_.refs_5_, ...), custom_call_target="tpu_custom_call" | custom-call | flops 679477248 | bytes 4128768 | tf_op jit(solution)/shard_map/base/pallas_call | solution.py:32
  81.1 2.2 %base.24.refs_0_ = f32[192,768]{1,0:T(8,128)S(1)} custom-call(bf16[768,768]{1,0:T(8,128)(2,1)S(1)} %get-tuple-element.54.refs_0_, bf16[768,768]{1,0:T(8,128)(2,1)S(1)} %get-tuple-element.55.refs_1_, f32[192,384]{1,0:T(8,128)S(1)} %get-tuple-element.82.refs_2_.refs_4_, f32[192,384]{1,0:T(8,128)S(1)} %get-tuple-element.83.refs_3_.refs_5_, ...), custom_call_target="tpu_custom_call" | custom-call | flops 679477248 | bytes 4128768 | tf_op jit(solution)/shard_map/base/pallas_call | solution.py:32
  84.7 4.8 %collective-permute-start.24 = (f32[192,384]{1,0:T(8,128)S(1)}, f32[192,384]{1,0:T(8,128)S(1)}, u32[]{:S(2)}, u32[]{:S(2)}) collective-permute-start(f32[192,384]{1,0:T(8,128)S(1)} %get-tuple-element.85.refs_3_), channel_id=1, source_target_pairs={{0,1},{1,0},{2,3},{3,2},{4,5},{5,4},{6,7},{7,6},{8,9},{9,8},{10,11... | collective-permute-start | bytes 884744 | tf_op jit(solution)/shard_map/ppermute | solution.py:261
  92.0 3.4 %collective-permute-start.12 = (f32[192,384]{1,0:T(8,128)S(1)}, f32[192,384]{1,0:T(8,128)S(1)}, u32[]{:S(2)}, u32[]{:S(2)}) collective-permute-start(f32[192,384]{1,0:T(8,128)S(1)} %get-tuple-element.71.refs_3_), channel_id=1, source_target_pairs={{0,1},{1,0},{2,3},{3,2},{4,5},{5,4},{6,7},{7,6},{8,9},{9,8},{10,11... | collective-permute-start | bytes 884744 | tf_op jit(solution)/shard_map/ppermute | solution.py:261
  95.4 2.2 %base.25.refs_0_ = f32[192,768]{1,0:T(8,128)S(1)} custom-call(bf16[768,768]{1,0:T(8,128)(2,1)S(1)} %get-tuple-element.54.refs_0_, bf16[768,768]{1,0:T(8,128)(2,1)S(1)} %get-tuple-element.55.refs_1_, f32[192,384]{1,0:T(8,128)S(1)} %get-tuple-element.84.refs_2_, f32[192,384]{1,0:T(8,128)S(1)} %get-tuple-element.85.refs_3_, ...), custom_call_target="tpu_custom_call" | custom-call | flops 679477248 | bytes 4718592 | tf_op jit(solution)/shard_map/base/pallas_call | solution.py:32
  99.8 2.2 %base.19.refs_0_ = f32[192,768]{1,0:T(8,128)S(1)} custom-call(bf16[768,768]{1,0:T(8,128)(2,1)S(1)} %get-tuple-element.54.refs_0_, bf16[768,768]{1,0:T(8,128)(2,1)S(1)} %get-tuple-element.55.refs_1_, f32[192,384]{1,0:T(8,128)S(1)} %get-tuple-element.70.refs_2_, f32[192,384]{1,0:T(8,128)S(1)} %get-tuple-element.71.refs_3_, ...), custom_call_target="tpu_custom_call" | custom-call | flops 679477248 | bytes 4718592 | tf_op jit(solution)/shard_map/base/pallas_call | solution.py:32
  104.2 3.6 %collective-permute-start.26 = (f32[192,384]{1,0:T(8,128)S(1)}, f32[192,384]{1,0:T(8,128)S(1)}, u32[]{:S(2)}, u32[]{:S(2)}) collective-permute-start(f32[192,384]{1,0:T(8,128)S(1)} %get-tuple-element.73.refs_5_.refs_3_), channel_id=1, source_target_pairs={{0,1},{1,0},{2,3},{3,2},{4,5},{5,4},{6,7},{7,6},{8,9},{9,8},{10,11... | collective-permute-start | bytes 884744 | tf_op jit(solution)/shard_map/ppermute | solution.py:261
  108.5 2.4 %collective-permute-start.27 = (f32[192,384]{1,0:T(8,128)}, f32[192,384]{1,0:T(8,128)}, u32[]{:S(2)}, u32[]{:S(2)}) collective-permute-start(f32[192,384]{1,0:T(8,128)} %get-tuple-element.86.refs_6_.refs_2_), channel_id=1, source_target_pairs={{0,1},{1,0},{2,3},{3,2},{4,5},{5,4},{6,7},{7,6},{8,9},{9,8},{10,11... | collective-permute-start | bytes 884744 | tf_op jit(solution)/shard_map/ppermute | solution.py:277
  111.0 2.1 %base.27.refs_0_ = f32[192,768]{1,0:T(8,128)S(1)} custom-call(bf16[768,768]{1,0:T(8,128)(2,1)S(1)} %get-tuple-element.54.refs_0_, bf16[768,768]{1,0:T(8,128)(2,1)S(1)} %get-tuple-element.55.refs_1_, f32[192,384]{1,0:T(8,128)} %get-tuple-element.86.refs_6_.refs_2_, f32[192,384]{1,0:T(8,128)S(1)} %get-tuple-element.87.refs_7_.refs_3_), custom_call_target="tpu_custom_call" | custom-call | flops 679477248 | bytes 3538944 | tf_op jit(solution)/shard_map/base/pallas_call | solution.py:32
  117.1 3.8 %collective-permute-start.32 = (f32[192,768]{1,0:T(8,128)S(1)}, f32[192,768]{1,0:T(8,128)S(1)}, u32[]{:S(2)}, u32[]{:S(2)}) collective-permute-start(f32[192,768]{1,0:T(8,128)S(1)} %tail.26.refs_4_), channel_id=1, source_target_pairs={{0,1},{1,0},{2,3},{3,2},{4,5},{5,4},{6,7},{7,6},{8,9},{9,8},{10,11... | collective-permute-start | bytes 1769480 | tf_op jit(solution)/shard_map/ppermute | solution.py:278
  124.0 4.2 %product.4 = f32[512,384]{1,0:T(8,128)S(1)} custom-call(bf16[768,512]{1,0:T(8,128)(2,1)S(1)} %get-tuple-element.50.refs_0_, bf16[768,512]{1,0:T(8,128)(2,1)S(1)} %get-tuple-element.51.refs_1_, bf16[768,512]{1,0:T(8,128)(2,1)S(1)} %get-tuple-element.52.refs_2_, bf16[768,512]{1,0:T(8,128)(2,1)S(1)} %get-tuple-element.53.refs_3_, ...), custom_call_target="tpu_custom_call" | custom-call | flops 1811939328 | bytes 6291456 | tf_op jit(solution)/shard_map/product/pallas_call | solution.py:32
  139.2 2.1 %product.5.refs_2_ = f32[512,384]{1,0:T(8,128)S(1)} custom-call(bf16[768,512]{1,0:T(8,128)(2,1)S(1)} %copy-done.31, bf16[768,512]{1,0:T(8,128)(2,1)S(1)} %copy-done.33, bf16[768,512]{1,0:T(8,128)(2,1)S(1)} %copy-done.35, bf16[768,512]{1,0:T(8,128)(2,1)S(1)} %copy-done.37, f32[192,768]{1,0:T(8,128)S(1)} %tail.26.refs_4_, f32[192,768]{1,0:T(8,128)S(1)} %tail.27.refs_5_, ...), custom_call_target="tpu_custom_call" | custom-call | flops 1811939328 | bytes 6291456 | tf_op jit(solution)/shard_map/product/pallas_call | solution.py:32
  144.4 2.3 %collective-permute-start.38 = (f32[128,384]{1,0:T(8,128)S(1)}, f32[128,384]{1,0:T(8,128)S(1)}, u32[]{:S(2)}, u32[]{:S(2)}) collective-permute-start(f32[128,384]{1,0:T(8,128)S(1)} %dynamic-slice_bitcast_fusion.3), channel_id=1, source_target_pairs={{0,4},{1,5},{2,6},{3,7},{4,0},{5,1},{6,2},{7,3},{8,12},{9,13},{10,... | collective-permute-start | bytes 589832 | tf_op jit(solution)/shard_map/ppermute | solution.py:219
  146.7 2.4 %product.7 = f32[256,384]{1,0:T(8,128)S(1)} custom-call(bf16[768,256]{1,0:T(8,128)(2,1)S(1)} %get-tuple-element.89.refs_0_, bf16[768,256]{1,0:T(8,128)(2,1)S(1)} %get-tuple-element.90.refs_1_, bf16[768,256]{1,0:T(8,128)(2,1)S(1)} %get-tuple-element.91.refs_2_, bf16[768,256]{1,0:T(8,128)(2,1)S(1)} %get-tuple-element.92.refs_3_, ...), custom_call_target="tpu_custom_call" | custom-call | flops 905969664 | bytes 4325376 | tf_op jit(solution)/shard_map/product/pallas_call | solution.py:32
  153.4 2.1 %collective-permute-done.39 = f32[2,64,384]{2,1,0:T(8,128)S(1)} collective-permute-done((f32[2,64,384]{2,1,0:T(8,128)S(1)}, f32[2,64,384]{2,1,0:T(8,128)S(1)}, u32[]{:S(2)}, u32[]{:S(2)}) %collective-permute-start.39) | collective-permute-done | bytes 196640 | tf_op jit(solution)/shard_map/ppermute | solution.py:219
  155.8 10.1 %collective-permute-done.36 = f32[2,64,384]{2,1,0:T(8,128)S(1)} collective-permute-done((f32[2,64,384]{2,1,0:T(8,128)S(1)}, f32[2,64,384]{2,1,0:T(8,128)S(1)}, u32[]{:S(2)}, u32[]{:S(2)}) %collective-permute-start.36) | collective-permute-done | bytes 196640 | tf_op jit(solution)/shard_map/ppermute | solution.py:219
  169.1 2.6 %collective-permute-done.37 = f32[64,384]{1,0:T(8,128)S(1)} collective-permute-done((f32[64,384]{1,0:T(8,128)S(1)}, f32[64,384]{1,0:T(8,128)S(1)}, u32[]{:S(2)}, u32[]{:S(2)}) %collective-permute-start.37) | collective-permute-done | bytes 98336 | tf_op jit(solution)/shard_map/ppermute | solution.py:219
  171.7 2.8 %collective-permute-done.35 = f32[128,384]{1,0:T(8,128)S(1)} collective-permute-done((f32[128,384]{1,0:T(8,128)S(1)}, f32[128,384]{1,0:T(8,128)S(1)}, u32[]{:S(2)}, u32[]{:S(2)}) %collective-permute-start.35) | collective-permute-done | bytes 196640 | tf_op jit(solution)/shard_map/ppermute | solution.py:219
  (194 shorter events, 73.6 us)
Async XLA Ops:
  7.2 113.7 %all-gather.7.cloned.1.call-start = ((), (), s32[]{:S(2)}) async-start(), calls=%async_computation.1 | async-start | bytes 3932160 | tf_op jit(solution)/shard_map/all_gather | solution.py:256
  13.5 129.0 %all-gather.5.cloned.1.call-start = ((), (), s32[]{:S(2)}) async-start(), calls=%async_computation | async-start | bytes 1966080 | tf_op jit(solution)/shard_map/all_gather | solution.py:256
  13.6 14.2 %collective-permute-start.13 = (f32[192,384]{1,0:T(8,128)}, f32[192,384]{1,0:T(8,128)S(1)}, u32[]{:S(2)}, u32[]{:S(2)}) collective-permute-start(f32[192,384]{1,0:T(8,128)} %get-tuple-element.74.refs_2_.refs_4_.refs_6_), channel_id=1, source_target_pairs={{1,2},{3,4},{5,6},{2,1},{4,3},{6,5},{9,10},{11,12},{13,14},{10,9},... | collective-permute-start | bytes 884744 | tf_op jit(solution)/shard_map/ppermute | solution.py:261
  14.3 13.5 %collective-permute-start.14 = (f32[192,384]{1,0:T(8,128)}, f32[192,384]{1,0:T(8,128)S(1)}, u32[]{:S(2)}, u32[]{:S(2)}) collective-permute-start(f32[192,384]{1,0:T(8,128)} %get-tuple-element.75.refs_3_.refs_5_.refs_7_), channel_id=1, source_target_pairs={{0,1},{1,0},{2,3},{3,2},{4,5},{5,4},{6,7},{7,6},{8,9},{9,8},{10,11... | collective-permute-start | bytes 884744 | tf_op jit(solution)/shard_map/ppermute | solution.py:261
  18.5 15.7 %collective-permute-start.1 = (f32[192,384]{1,0:T(8,128)}, f32[192,384]{1,0:T(8,128)S(1)}, u32[]{:S(2)}, u32[]{:S(2)}) collective-permute-start(f32[192,384]{1,0:T(8,128)} %get-tuple-element.56.refs_2_.refs_4_.refs_6_), channel_id=1, source_target_pairs={{1,2},{3,4},{5,6},{2,1},{4,3},{6,5},{9,10},{11,12},{13,14},{10,9},... | collective-permute-start | bytes 884744 | tf_op jit(solution)/shard_map/ppermute | solution.py:261
  19.2 15.0 %collective-permute-start.2 = (f32[192,384]{1,0:T(8,128)}, f32[192,384]{1,0:T(8,128)S(1)}, u32[]{:S(2)}, u32[]{:S(2)}) collective-permute-start(f32[192,384]{1,0:T(8,128)} %get-tuple-element.57.refs_3_.refs_5_.refs_7_), channel_id=1, source_target_pairs={{0,1},{1,0},{2,3},{3,2},{4,5},{5,4},{6,7},{7,6},{8,9},{9,8},{10,11... | collective-permute-start | bytes 884744 | tf_op jit(solution)/shard_map/ppermute | solution.py:261
  28.5 11.7 %collective-permute-start.15 = (f32[192,384]{1,0:T(8,128)S(1)}, f32[192,384]{1,0:T(8,128)S(1)}, u32[]{:S(2)}, u32[]{:S(2)}) collective-permute-start(f32[192,384]{1,0:T(8,128)S(1)} %get-tuple-element.76.refs_2_.refs_4_), channel_id=1, source_target_pairs={{1,2},{3,4},{5,6},{2,1},{4,3},{6,5},{9,10},{11,12},{13,14},{10,9},... | collective-permute-start | bytes 884744 | tf_op jit(solution)/shard_map/ppermute | solution.py:261
  35.0 11.8 %collective-permute-start.3 = (f32[192,384]{1,0:T(8,128)S(1)}, f32[192,384]{1,0:T(8,128)S(1)}, u32[]{:S(2)}, u32[]{:S(2)}) collective-permute-start(f32[192,384]{1,0:T(8,128)S(1)} %get-tuple-element.62.refs_2_.refs_4_), channel_id=1, source_target_pairs={{1,2},{3,4},{5,6},{2,1},{4,3},{6,5},{9,10},{11,12},{13,14},{10,9},... | collective-permute-start | bytes 884744 | tf_op jit(solution)/shard_map/ppermute | solution.py:261
  35.7 11.1 %collective-permute-start.4 = (f32[192,384]{1,0:T(8,128)S(1)}, f32[192,384]{1,0:T(8,128)S(1)}, u32[]{:S(2)}, u32[]{:S(2)}) collective-permute-start(f32[192,384]{1,0:T(8,128)S(1)} %get-tuple-element.63.refs_3_.refs_5_), channel_id=1, source_target_pairs={{0,1},{1,0},{2,3},{3,2},{4,5},{5,4},{6,7},{7,6},{8,9},{9,8},{10,11... | collective-permute-start | bytes 884744 | tf_op jit(solution)/shard_map/ppermute | solution.py:261
  41.0 13.7 %collective-permute-start.17 = (f32[192,384]{1,0:T(8,128)S(1)}, f32[192,384]{1,0:T(8,128)S(1)}, u32[]{:S(2)}, u32[]{:S(2)}) collective-permute-start(f32[192,384]{1,0:T(8,128)S(1)} %get-tuple-element.78.refs_2_.refs_4_), channel_id=1, source_target_pairs={{1,2},{3,4},{5,6},{2,1},{4,3},{6,5},{9,10},{11,12},{13,14},{10,9},... | collective-permute-start | bytes 884744 | tf_op jit(solution)/shard_map/ppermute | solution.py:261
  41.7 13.0 %collective-permute-start.18 = (f32[192,384]{1,0:T(8,128)S(1)}, f32[192,384]{1,0:T(8,128)S(1)}, u32[]{:S(2)}, u32[]{:S(2)}) collective-permute-start(f32[192,384]{1,0:T(8,128)S(1)} %get-tuple-element.79.refs_3_.refs_5_), channel_id=1, source_target_pairs={{0,1},{1,0},{2,3},{3,2},{4,5},{5,4},{6,7},{7,6},{8,9},{9,8},{10,11... | collective-permute-start | bytes 884744 | tf_op jit(solution)/shard_map/ppermute | solution.py:261
  48.2 16.7 %collective-permute-start.5 = (f32[192,384]{1,0:T(8,128)}, f32[192,384]{1,0:T(8,128)}, u32[]{:S(2)}, u32[]{:S(2)}) collective-permute-start(f32[192,384]{1,0:T(8,128)} %get-tuple-element.64.refs_2_.refs_4_), channel_id=1, source_target_pairs={{1,2},{3,4},{5,6},{2,1},{4,3},{6,5},{9,10},{11,12},{13,14},{10,9},... | collective-permute-start | bytes 884744 | tf_op jit(solution)/shard_map/ppermute | solution.py:261
  49.6 15.3 %collective-permute-start.6 = (f32[192,384]{1,0:T(8,128)}, f32[192,384]{1,0:T(8,128)}, u32[]{:S(2)}, u32[]{:S(2)}) collective-permute-start(f32[192,384]{1,0:T(8,128)} %get-tuple-element.65.refs_3_.refs_5_), channel_id=1, source_target_pairs={{0,1},{1,0},{2,3},{3,2},{4,5},{5,4},{6,7},{7,6},{8,9},{9,8},{10,11... | collective-permute-start | bytes 884744 | tf_op jit(solution)/shard_map/ppermute | solution.py:261
  56.1 16.0 %collective-permute-start.19 = (f32[192,384]{1,0:T(8,128)}, f32[192,384]{1,0:T(8,128)}, u32[]{:S(2)}, u32[]{:S(2)}) collective-permute-start(f32[192,384]{1,0:T(8,128)} %get-tuple-element.80.refs_2_.refs_4_), channel_id=1, source_target_pairs={{1,2},{3,4},{5,6},{2,1},{4,3},{6,5},{9,10},{11,12},{13,14},{10,9},... | collective-permute-start | bytes 884744 | tf_op jit(solution)/shard_map/ppermute | solution.py:261
  57.5 14.6 %collective-permute-start.20 = (f32[192,384]{1,0:T(8,128)}, f32[192,384]{1,0:T(8,128)}, u32[]{:S(2)}, u32[]{:S(2)}) collective-permute-start(f32[192,384]{1,0:T(8,128)} %get-tuple-element.81.refs_3_.refs_5_), channel_id=1, source_target_pairs={{0,1},{1,0},{2,3},{3,2},{4,5},{5,4},{6,7},{7,6},{8,9},{9,8},{10,11... | collective-permute-start | bytes 884744 | tf_op jit(solution)/shard_map/ppermute | solution.py:261
  66.8 12.8 %collective-permute-start.7 = (f32[192,384]{1,0:T(8,128)S(1)}, f32[192,384]{1,0:T(8,128)S(1)}, u32[]{:S(2)}, u32[]{:S(2)}) collective-permute-start(f32[192,384]{1,0:T(8,128)S(1)} %get-tuple-element.66.refs_2_.refs_4_), channel_id=1, source_target_pairs={{1,2},{3,4},{5,6},{2,1},{4,3},{6,5},{9,10},{11,12},{13,14},{10,9},... | collective-permute-start | bytes 884744 | tf_op jit(solution)/shard_map/ppermute | solution.py:261
  67.4 12.1 %collective-permute-start.8 = (f32[192,384]{1,0:T(8,128)S(1)}, f32[192,384]{1,0:T(8,128)S(1)}, u32[]{:S(2)}, u32[]{:S(2)}) collective-permute-start(f32[192,384]{1,0:T(8,128)S(1)} %get-tuple-element.67.refs_3_.refs_5_), channel_id=1, source_target_pairs={{0,1},{1,0},{2,3},{3,2},{4,5},{5,4},{6,7},{7,6},{8,9},{9,8},{10,11... | collective-permute-start | bytes 884744 | tf_op jit(solution)/shard_map/ppermute | solution.py:261
  84.0 13.6 %collective-permute-start.23 = (f32[192,384]{1,0:T(8,128)S(1)}, f32[192,384]{1,0:T(8,128)S(1)}, u32[]{:S(2)}, u32[]{:S(2)}) collective-permute-start(f32[192,384]{1,0:T(8,128)S(1)} %get-tuple-element.84.refs_2_), channel_id=1, source_target_pairs={{1,2},{3,4},{5,6},{2,1},{4,3},{6,5},{9,10},{11,12},{13,14},{10,9},... | collective-permute-start | bytes 884744 | tf_op jit(solution)/shard_map/ppermute | solution.py:261
  84.7 12.9 %collective-permute-start.24 = (f32[192,384]{1,0:T(8,128)S(1)}, f32[192,384]{1,0:T(8,128)S(1)}, u32[]{:S(2)}, u32[]{:S(2)}) collective-permute-start(f32[192,384]{1,0:T(8,128)S(1)} %get-tuple-element.85.refs_3_), channel_id=1, source_target_pairs={{0,1},{1,0},{2,3},{3,2},{4,5},{5,4},{6,7},{7,6},{8,9},{9,8},{10,11... | collective-permute-start | bytes 884744 | tf_op jit(solution)/shard_map/ppermute | solution.py:261
  91.3 11.6 %collective-permute-start.11 = (f32[192,384]{1,0:T(8,128)S(1)}, f32[192,384]{1,0:T(8,128)S(1)}, u32[]{:S(2)}, u32[]{:S(2)}) collective-permute-start(f32[192,384]{1,0:T(8,128)S(1)} %get-tuple-element.70.refs_2_), channel_id=1, source_target_pairs={{1,2},{3,4},{5,6},{2,1},{4,3},{6,5},{9,10},{11,12},{13,14},{10,9},... | collective-permute-start | bytes 884744 | tf_op jit(solution)/shard_map/ppermute | solution.py:261
  98.8 12.1 %collective-permute-start.28 = (f32[192,384]{1,0:T(8,128)S(1)}, f32[192,384]{1,0:T(8,128)S(1)}, u32[]{:S(2)}, u32[]{:S(2)}) collective-permute-start(f32[192,384]{1,0:T(8,128)S(1)} %get-tuple-element.87.refs_7_.refs_3_), channel_id=1, source_target_pairs={{0,1},{1,0},{2,3},{3,2},{4,5},{5,4},{6,7},{7,6},{8,9},{9,8},{10,11... | collective-permute-start | bytes 884744 | tf_op jit(solution)/shard_map/ppermute | solution.py:261
  102.0 13.1 %collective-permute-start.31 = (f32[192,384]{1,0:T(8,128)}, f32[192,384]{1,0:T(8,128)S(1)}, u32[]{:S(2)}, u32[]{:S(2)}) collective-permute-start(f32[192,384]{1,0:T(8,128)} %get-tuple-element.86.refs_6_.refs_2_), channel_id=1, source_target_pairs={{1,2},{3,4},{5,6},{2,1},{4,3},{6,5},{9,10},{11,12},{13,14},{10,9},... | collective-permute-start | bytes 884744 | tf_op jit(solution)/shard_map/ppermute | solution.py:261
  104.2 12.2 %collective-permute-start.26 = (f32[192,384]{1,0:T(8,128)S(1)}, f32[192,384]{1,0:T(8,128)S(1)}, u32[]{:S(2)}, u32[]{:S(2)}) collective-permute-start(f32[192,384]{1,0:T(8,128)S(1)} %get-tuple-element.73.refs_5_.refs_3_), channel_id=1, source_target_pairs={{0,1},{1,0},{2,3},{3,2},{4,5},{5,4},{6,7},{7,6},{8,9},{9,8},{10,11... | collective-permute-start | bytes 884744 | tf_op jit(solution)/shard_map/ppermute | solution.py:261
  108.5 15.2 %collective-permute-start.27 = (f32[192,384]{1,0:T(8,128)}, f32[192,384]{1,0:T(8,128)}, u32[]{:S(2)}, u32[]{:S(2)}) collective-permute-start(f32[192,384]{1,0:T(8,128)} %get-tuple-element.86.refs_6_.refs_2_), channel_id=1, source_target_pairs={{0,1},{1,0},{2,3},{3,2},{4,5},{5,4},{6,7},{7,6},{8,9},{9,8},{10,11... | collective-permute-start | bytes 884744 | tf_op jit(solution)/shard_map/ppermute | solution.py:277
  110.9 12.8 %collective-permute-start.25 = (f32[192,384]{1,0:T(8,128)}, f32[192,384]{1,0:T(8,128)}, u32[]{:S(2)}, u32[]{:S(2)}) collective-permute-start(f32[192,384]{1,0:T(8,128)} %get-tuple-element.72.refs_4_.refs_2_), channel_id=1, source_target_pairs={{0,1},{1,0},{2,3},{3,2},{4,5},{5,4},{6,7},{7,6},{8,9},{9,8},{10,11... | collective-permute-start | bytes 884744 | tf_op jit(solution)/shard_map/ppermute | solution.py:277
  115.9 15.1 %collective-permute-start.33 = (f32[192,768]{1,0:T(8,128)S(1)}, f32[192,768]{1,0:T(8,128)S(1)}, u32[]{:S(2)}, u32[]{:S(2)}) collective-permute-start(f32[192,768]{1,0:T(8,128)S(1)} %tail.27.refs_5_), channel_id=1, source_target_pairs={{0,1},{1,0},{2,3},{3,2},{4,5},{5,4},{6,7},{7,6},{8,9},{9,8},{10,11... | collective-permute-start | bytes 1769480 | tf_op jit(solution)/shard_map/ppermute | solution.py:278
  117.1 14.7 %collective-permute-start.32 = (f32[192,768]{1,0:T(8,128)S(1)}, f32[192,768]{1,0:T(8,128)S(1)}, u32[]{:S(2)}, u32[]{:S(2)}) collective-permute-start(f32[192,768]{1,0:T(8,128)S(1)} %tail.26.refs_4_), channel_id=1, source_target_pairs={{0,1},{1,0},{2,3},{3,2},{4,5},{5,4},{6,7},{7,6},{8,9},{9,8},{10,11... | collective-permute-start | bytes 1769480 | tf_op jit(solution)/shard_map/ppermute | solution.py:278
  129.8 11.5 %collective-permute-start.29 = (f32[2,128,384]{2,1,0:T(8,128)}, f32[2,128,384]{2,1,0:T(8,128)}, u32[]{:S(2)}, u32[]{:S(2)}) collective-permute-start(f32[2,128,384]{2,1,0:T(8,128)} %dynamic-slice_bitcast_fusion.1), channel_id=1, source_target_pairs={{0,2},{1,3},{2,0},{3,1},{4,6},{5,7},{6,4},{7,5},{8,10},{9,11},{10,... | collective-permute-start | bytes 1179656 | tf_op jit(solution)/shard_map/ppermute | solution.py:219
  144.4 22.5 %collective-permute-start.38 = (f32[128,384]{1,0:T(8,128)S(1)}, f32[128,384]{1,0:T(8,128)S(1)}, u32[]{:S(2)}, u32[]{:S(2)}) collective-permute-start(f32[128,384]{1,0:T(8,128)S(1)} %dynamic-slice_bitcast_fusion.3), channel_id=1, source_target_pairs={{0,4},{1,5},{2,6},{3,7},{4,0},{5,1},{6,2},{7,3},{8,12},{9,13},{10,... | collective-permute-start | bytes 589832 | tf_op jit(solution)/shard_map/ppermute | solution.py:219
  150.0 17.8 %collective-permute-start.34 = (f32[2,128,384]{2,1,0:T(8,128)S(1)}, f32[2,128,384]{2,1,0:T(8,128)S(1)}, u32[]{:S(2)}, u32[]{:S(2)}) collective-permute-start(f32[2,128,384]{2,1,0:T(8,128)S(1)} %dynamic-slice_bitcast_fusion), channel_id=1, source_target_pairs={{0,4},{1,5},{2,6},{3,7},{4,0},{5,1},{6,2},{7,3},{8,12},{9,13},{10,... | collective-permute-start | bytes 1179656 | tf_op jit(solution)/shard_map/ppermute | solution.py:219
  151.6 14.4 %collective-permute-start.36 = (f32[2,64,384]{2,1,0:T(8,128)S(1)}, f32[2,64,384]{2,1,0:T(8,128)S(1)}, u32[]{:S(2)}, u32[]{:S(2)}) collective-permute-start(f32[2,64,384]{2,1,0:T(8,128)S(1)} %dynamic-slice_bitcast_fusion.4), channel_id=1, source_target_pairs={{0,4},{1,5},{2,6},{3,7},{4,0},{5,1},{6,2},{7,3},{8,12},{9,13},{10,... | collective-permute-start | bytes 589832 | tf_op jit(solution)/shard_map/ppermute | solution.py:219
  155.5 11.5 %collective-permute-start.40 = (f32[64,384]{1,0:T(8,128)S(1)}, f32[64,384]{1,0:T(8,128)S(1)}, u32[]{:S(2)}, u32[]{:S(2)}) collective-permute-start(f32[64,384]{1,0:T(8,128)S(1)} %dynamic-slice_bitcast_fusion.6), channel_id=1, source_target_pairs={{0,4},{1,5},{2,6},{3,7},{4,0},{5,1},{6,2},{7,3},{8,12},{9,13},{10,... | collective-permute-start | bytes 294920 | tf_op jit(solution)/shard_map/ppermute | solution.py:219
  (50 other events, 234.1 us)
Sparse Core Ops, SparseCore 0:
  13.6 66.1 all-gather.6
  81.4 35.7 all-gather.4

commit v2 on v1

--- a/solution.py
+++ b/solution.py
@@ -20,26 +20,19 @@
 NN = ((1,), (0,))
 
 
-def call(kernel, out_shape, arrays, specs, name, mib, flops=0, scratch=(), after=()):
-    outs = list(out_shape)
+def call(kernel, out_shape, arrays, specs, name, mib, flops=0, scratch=()):
+    outs = out_shape if isinstance(out_shape, list) else [out_shape]
     moved = sum(a.size * a.dtype.itemsize for a in list(arrays) + outs)
-    count, made, late = len(arrays), len(outs), len(after)
-
-    def body(*refs):
-        inner = refs[count + late :]
-        kernel(*refs[:count], *inner[:made], *inner[made + late :])
-
-    return list(pl.pallas_call(
-        body,
-        out_shape=outs + [jax.ShapeDtypeStruct(a.shape, a.dtype) for a in after],
-        in_specs=[*specs] + [ANYWHERE] * late,
-        out_specs=[WHOLE] * made + [ANYWHERE] * late,
+    return pl.pallas_call(
+        kernel,
+        out_shape=out_shape,
+        in_specs=specs,
+        out_specs=[WHOLE] * len(outs) if isinstance(out_shape, list) else WHOLE,
         scratch_shapes=list(scratch),
-        input_output_aliases={count + i: made + i for i in range(late)},
         compiler_params=pltpu.CompilerParams(vmem_limit_bytes=mib * 1024 * 1024),
         cost_estimate=pl.CostEstimate(flops=int(flops), bytes_accessed=moved, transcendentals=0),
         name=name,
-    )(*arrays, *after))
+    )(*arrays)
 
 
 def f32(*shape):
@@ -89,7 +82,7 @@
     out = [f32(states // 2, atoms * size)] * 2 + [f32(states // PARTS, atoms // 2 * size)] * (2 * PARTS)
     kernel = functools.partial(arrange_kernel, states // (2 * width), width)
     by_atom = jnp.transpose(vectors, (1, 0, 2))
-    mine, theirs, *parts = call(kernel, out, [odd, by_atom], [SCALARS, WHOLE], "arrange", 8)
+    mine, theirs, *parts = call(kernel, out, [odd, by_atom], [SCALARS, WHOLE], "arrange", 16)
     return mine, theirs, [parts[2 * p : 2 * p + 2] for p in range(PARTS)]
 
 
@@ -129,7 +122,7 @@
     full, edge = atoms * size, REACH * size
     out = [bf16(full, full)] * 2 + [bf16(edge, edge)] * 4
     kernel = functools.partial(weights_kernel, atoms)
-    return call(kernel, out, [odd, coupling, hblocks], [SCALARS, SCALARS, WHOLE], "weights", 10)
+    return call(kernel, out, [odd, coupling, hblocks], [SCALARS, SCALARS, WHOLE], "weights", 16)
 
 
 def base_kernel(scales, high_ref, low_ref, *rest):
@@ -147,11 +140,11 @@
         out_ref[:, columns] = value
 
 
-def make_base(scales, weights, fields, after):
+def make_base(scales, weights, fields):
     arrays = list(weights[:2]) + [half for field in fields for half in field]
     rows, edge = fields[0][0].shape
     flops = 6 * rows * 4 * edge * edge
-    return call(functools.partial(base_kernel, scales), [f32(rows, 2 * edge)], arrays, [WHOLE] * len(arrays), "base", 10, flops, (), after)
+    return call(functools.partial(base_kernel, scales), f32(rows, 2 * edge), arrays, [WHOLE] * len(arrays), "base", 12, flops)
 
 
 def tail_kernel(scale, base, got_far, got_near, fh, fl, nh, nl, *outs):
@@ -165,36 +158,96 @@
             outs[0][:, columns] = value
 
 
-def make_tail(scale, base, got, weights, joined, after):
+def make_tail(scale, base, got, weights, joined):
     arrays = [base, *got, *weights[2:]]
     rows, edge = got[0].shape
     out = [f32(rows, 2 * edge)] if joined else [f32(rows, edge)] * 2
     flops = 6 * rows * 2 * edge * edge
-    return call(functools.partial(tail_kernel, scale), out, arrays, [WHOLE] * len(arrays), "tail", 8, flops, (), after)
-
-
-def assemble_kernel(all_ref, *outs):
-    planes, _, rows, depth = all_ref.shape
+    return call(functools.partial(tail_kernel, scale), out, arrays, [WHOLE] * len(arrays), "tail", 12, flops)
+
+
+def assemble_kernel(count, place_ref, *refs):
+    shards = refs[: 2 * count - 1]
+    outs = refs[2 * count - 1 : -2]
+    held, sems = refs[-2:]
+    place = place_ref[0]
+    rows, depth = shards[0].shape
+    half = rows // 2
+
+    def copies(plane, source):
+        return [
+            pltpu.make_async_copy(
+                source.at[pl.ds(side * half, half)],
+                held.at[pl.ds(plane * half, half), pl.ds(side * depth, depth)],
+                sems.at[plane, side],
+            )
+            for side in range(2)
+        ]
+
+    for plane in range(count):
+        for at in range(count):
+
+            @pl.when(place == at)
+            def _():
+                for copy in copies(plane, shards[plane - at + count - 1]):
+                    copy.start()
+
+    for plane in range(count):
+        for copy in copies(plane, shards[0]):
+            copy.wait()
     step = 128
-    for side in range(2):
-        for at in range(0, depth, step):
-            columns = [all_ref[plane, side, :, at : at + step] for plane in range(planes)]
-            term = split(jnp.concatenate(columns, axis=0).T)
+    for at in range(0, depth, step):
+        for side in range(2):
+            term = split(held[:, side * depth + at : side * depth + at + step].T)
             outs[2 * side][at : at + step], outs[2 * side + 1][at : at + step] = term
 
 
-def assemble(gathered, after):
-    planes, _, rows, depth = gathered.shape
-    out = [bf16(depth, planes * rows)] * 4
-    return call(assemble_kernel, out, [gathered], [WHOLE], "assemble", 10, 0, (), after)
-
-
-def product_kernel(own_h, own_l, other_h, other_l, *rest):
+def assemble(place, shards):
+    count = (len(shards) + 1) // 2
+    rows, depth = shards[0].shape
+    out = [bf16(depth, count * rows // 2)] * 4
+    scratch = [pltpu.VMEM((count * rows // 2, 2 * depth), jnp.float32), pltpu.SemaphoreType.DMA((count, 2))]
+    specs = [SCALARS] + [ANYWHERE] * len(shards)
+    return call(functools.partial(assemble_kernel, count), out, [place] + shards, specs, "assemble", 24, 0, scratch)
+
+
+def along_line(payload):
+    count = lax.axis_size("row")
+    before, after = [payload], [payload]
+    for d in range(1, count):
+        up = [(i, i + 1) for i in range(d - 1, count - 1)]
+        down = [(count - 1 - a, count - 1 - b) for a, b in up]
+        before.append(lax.ppermute(before[-1], "row", up))
+        after.append(lax.ppermute(after[-1], "row", down))
+    return before[:0:-1] + after
+
+
+def tiles(width):
+    step = 256 if width % 256 == 0 else width
+    return width // step, step
+
+
+def first_product_kernel(high_ref, low_ref, *rest):
     out_ref = rest[-1]
-    half = len(rest) // 2
-    value = dot3(split(joined(rest[:half])), (own_h[...], own_l[...]))
-    value = value + dot3(split(joined(rest[half:-1])), (other_h[...], other_l[...]))
-    out_ref[...] = value.T
+    operand = split(joined(rest[:-1]))
+    count, step = tiles(out_ref.shape[1])
+
+    @pl.loop(0, count)
+    def _(i):
+        columns = pl.ds(pl.multiple_of(i * step, step), step)
+        out_ref[:, columns] = dot3(operand, (high_ref[:, columns], low_ref[:, columns]))
+
+
+def second_product_kernel(high_ref, low_ref, acc_ref, *rest):
+    out_ref = rest[-1]
+    operand = split(joined(rest[:-1]))
+    count, step = tiles(out_ref.shape[0])
+
+    @pl.loop(0, count)
+    def _(i):
+        columns = pl.ds(pl.multiple_of(i * step, step), step)
+        value = acc_ref[:, columns] + dot3(operand, (high_ref[:, columns], low_ref[:, columns]))
+        out_ref[columns, :] = value.T
 
 
 def joined(refs):
@@ -207,10 +260,14 @@
 
 def product(everything, own, other):
     depth, width = everything[0].shape
-    arrays = [*everything] + [half for part in own + other for half in part]
     rows = sum(part[0].shape[0] for part in own)
-    flops = 12 * rows * depth * width
-    return call(product_kernel, [f32(width, rows)], arrays, [WHOLE] * len(arrays), "product", 14, flops)[0]
+    flops = 6 * rows * depth * width
+    mib = 24
+    arrays = [half for part in own for half in part]
+    arrays = [*everything[:2]] + [half for part in own for half in part]
+    acc = call(first_product_kernel, f32(rows, width), arrays, [WHOLE] * len(arrays), "own_product", mib, flops)
+    arrays = [*everything[2:], acc] + [half for part in other for half in part]
+    return call(second_product_kernel, f32(width, rows), arrays, [WHOLE] * len(arrays), "other_product", mib, flops)
 
 
 def halve(part, axis_at, mine, count, bit):
@@ -219,26 +276,25 @@
     return kept + lax.ppermute(other, "col", [(i, i ^ (1 << bit)) for i in range(count)])
 
 
-def reduce_step(part, step, low_first):
+def reduce_chips(part):
     count = lax.axis_size("col")
     me = lax.axis_index("col").astype(jnp.int32)
     bits = count.bit_length() - 1
-    if step == 1:
-        part = part.reshape((2,) * (bits - 1) + (part.shape[0] * 2 // count, part.shape[1]))
-    bit = step if low_first else bits - step
-    return halve(part, bits - 1 - step if low_first else 0, (me >> bit) % 2, count, bit)
-
-
-def reduce_rest(part, done, low_first):
-    bits = lax.axis_size("col").bit_length() - 1
-    for step in range(done + 1, bits):
-        part = reduce_step(part, step, low_first)
-    return part
+    width = part.shape[0] * 2 // count
+    part = part.reshape((2,) * (bits - 1) + (width, part.shape[1]))
+    cut = width // 2
+    first, second = part[..., :cut, :], part[..., cut:, :]
+    for step in range(1, bits):
+        low, high = step, bits - step
+        first = halve(first, bits - 1 - step, (me >> low) % 2, count, low)
+        second = halve(second, 0, (me >> high) % 2, count, high)
+    return jnp.concatenate([first, second], axis=0).T
 
 
 def per_device(vectors, hblocks, coupling):
     count = lax.axis_size("col")
     me = lax.axis_index("col").astype(jnp.int32)
+    place = lax.axis_index("row").astype(jnp.int32).reshape(1)
     odd = (me % 2).reshape(1)
     width = vectors.shape[0] * lax.axis_size("row") // count
     inner = [(i, i ^ 1) for i in range(count)]
@@ -247,15 +303,9 @@
 
     mine, theirs, start = arrange(odd, vectors, width)
     weights = make_weights(odd, coupling, hblocks)
-    groups = mine.shape[0] // width
-    cut = width // 24 * 16 or width
-    payload = [x.reshape(groups, width, -1) for x in (mine, lax.ppermute(theirs, "col", inner))]
-
-    def gather(at, to):
-        slab = jnp.stack([x[:, at:to].reshape(groups * (to - at), -1) for x in payload])
-        return lax.all_gather(slab, "row", axis=0)
-
-    gathered = [gather(0, cut), gather(cut, width)]
+    everything = assemble(
+        place, along_line(jnp.concatenate([mine, lax.ppermute(theirs, "col", inner)], axis=0))
+    )
 
     def send(now):
         return [lax.ppermute(now[0], "col", outer), lax.ppermute(now[1], "col", inner)]
@@ -266,26 +316,21 @@
     plans.append((1.0, 0.0))
     fields = [[part] for part in start]
     for at, plan in enumerate(plans):
-        got = [send(fields[p][-1]) for p in range(PARTS)]
+        last = at == len(plans) - 1
+        got = []
         for p in range(PARTS):
             now = fields[p][-1]
+            got.append(send(now))
             used = [now] + (fields[p][-2:-1] if len(plan) > 2 else []) + ([start[p]] if len(plan) > 3 else [])
-            (base,) = make_base(plan, weights, used, [])
-            fields[p].append(make_tail(plan[0], base, got[p], weights, at == len(plans) - 1, []))
+            base = make_base(plan, weights, used)
+            fields[p].append(make_tail(plan[0], base, got[p], weights, last))
     filtered = [field[-2] for field in fields]
     image = [field[-1] for field in fields]
-    other_filtered = [[lax.ppermute(filtered[p][0], "col", inner), got[p][1]] for p in range(PARTS)]
-    other_image = [[lax.ppermute(image[p][0], "col", inner)] for p in range(PARTS)]
-
-    everything = assemble(gathered[0], [])
-    sums = reduce_step(product(everything, filtered, other_filtered), 1, True)
-    image_sums = product(everything, image, other_image)
-    *everything, sums, image_sums = assemble(gathered[1], [sums, image_sums])
-    more = product(everything, filtered, other_filtered)
-    more_image = product(everything, image, other_image)
-    intersection = [reduce_rest(sums, 1, True), reduce_rest(more, 0, True)]
-    projected_ham = [reduce_rest(image_sums, 0, False), reduce_rest(more_image, 0, False)]
-    return jnp.concatenate(projected_ham, axis=0).T, jnp.concatenate(intersection, axis=0).T
+    other = [[lax.ppermute(filtered[p][0], "col", inner), got[p][1]] for p in range(PARTS)]
+    intersection = reduce_chips(product(everything, filtered, other))
+    other = [[lax.ppermute(image[p][0], "col", inner)] for p in range(PARTS)]
+    projected_ham = reduce_chips(product(everything, image, other))
+    return projected_ham, intersection
 
 
 def solution(mesh):

time: 184 us -> 152 us (0.83)
  starting transfers between devices: 64.8 us -> 84.8 us
  local copies, waits for them, and re-layouts: 22.4 us -> 3 us
  Pallas kernels: 56.5 us -> 43.1 us
  between operations: 14.9 us -> 1.54 us
  other arithmetic: 4.41 us -> 1.67 us
    unnamed x78 -> x27, local copies, waits for them, and re-layouts: 19.5 us -> 2.63 us
    pallas_call x36 -> x35, Pallas kernels: 56.5 us -> 43.1 us  [call(): pl.pallas_call(kernel, out_shape=out_shape, in_specs=specs, out_specs=[WH...]
    ppermute x14, starting transfers between devices: 37.9 us -> 50.8 us  [send(): lax.ppermute(now[1], 'col', inner)]
    ppermute x2 -> x8, starting transfers between devices: 4.24 us -> 15 us  [the longest x3 8.31 us: along_line(): before.append(lax.ppermute(before[-1], 'row', up))]
    ppermute x8, waiting for transfers between devices: 17.7 us -> 10.7 us  [halve(): lax.ppermute(other, 'col', [(i, i ^ 1 << bit) for i in range(count)])]
    ppermute x2 -> x8, waiting for transfers between devices: 0.01 us -> 5.91 us  [the longest x3 5.89 us: along_line(): after.append(lax.ppermute(after[-1], 'row', down))]
    ppermute x2, starting transfers between devices: 2.51 us -> 0.51 us  [per_device(): lax.ppermute(filtered[p][0], 'col', inner)]
  transfers between devices with their start and end apart: 43 -> 47, of which waited for: 6 -> 7; matrix products, arithmetic and copies ran while one was open for 3% -> 1% of each run, Pallas kernels for 30% -> 28%
where the time goes in v2:
time: 152 us
  starting transfers between devices  84.8 us (56%)
  Pallas kernels  43.1 us (28%)
  waiting for transfers between devices  17.5 us (12%)
  local copies, waits for them, and re-layouts  3 us (2%)
  other arithmetic  1.67 us (1%)
  between operations  1.54 us (1%)
    ppermute x14, starting transfers between devices, send(): lax.ppermute(now[1], 'col', inner)  50.8 us
    pallas_call x35, Pallas kernels, call(): pl.pallas_call(kernel, out_shape=out_shape, in_specs=specs, out_specs=[WH...  43.1 us
    ppermute x8, waiting for transfers between devices, halve(): lax.ppermute(other, 'col', [(i, i ^ 1 << bit) for i in range(count)])  10.7 us
    ppermute x14, starting transfers between devices, send(): lax.ppermute(now[0], 'col', outer)  10 us
    ppermute x3, starting transfers between devices, along_line(): before.append(lax.ppermute(before[-1], 'row', up))  8.31 us
    ppermute x8, starting transfers between devices, halve(): lax.ppermute(other, 'col', [(i, i ^ 1 << bit) for i in range(count)])  8 us
    ppermute x3, waiting for transfers between devices, along_line(): after.append(lax.ppermute(after[-1], 'row', down))  5.89 us
    ppermute x3, starting transfers between devices, along_line(): after.append(lax.ppermute(after[-1], 'row', down))  3.85 us
  transfers between devices with their start and end apart: 47, of which 7 were waited for; matrix products, arithmetic and copies ran while one was open for 1% of the time, Pallas kernels for 28%

profile of v2, /device:TPU:0, one launch (start us, length us, event | category | flops | bytes accessed | tf_op | source)
XLA Modules:
  0.0 151.6 jit_solution(13169792712566772137)
XLA Ops:
  4.3 4.9 %collective-permute-start.1 = (f32[384,768]{1,0:T(8,128)S(1)}, f32[384,768]{1,0:T(8,128)S(1)}, u32[]{:S(2)}, u32[]{:S(2)}) collective-permute-start(f32[384,768]{1,0:T(8,128)S(1)} %constant_dynamic-update-slice_fusion.refs_3_), channel_id=1, source_target_pairs={{0,8},{8,16},{16,24},{1,9},{9,17},{17,25},{2,10},{10,18},{18,26},{... | collective-permute-start | bytes 3538952 | tf_op jit(solution)/shard_map/ppermute | solution.py:220
  10.5 1.5 %collective-permute-start.8 = (f32[192,384]{1,0:T(8,128)S(1)}, f32[192,384]{1,0:T(8,128)S(1)}, u32[]{:S(2)}, u32[]{:S(2)}) collective-permute-start(f32[192,384]{1,0:T(8,128)S(1)} %get-tuple-element.51.rest_1_.rest_3_.rest_5_), channel_id=1, source_target_pairs={{0,1},{1,0},{2,3},{3,2},{4,5},{5,4},{6,7},{7,6},{8,9},{9,8},{10,11... | collective-permute-start | bytes 884744 | tf_op jit(solution)/shard_map/ppermute | solution.py:311
  12.7 2.9 %collective-permute-start.22 = (f32[192,384]{1,0:T(8,128)S(1)}, f32[192,384]{1,0:T(8,128)S(1)}, u32[]{:S(2)}, u32[]{:S(2)}) collective-permute-start(f32[192,384]{1,0:T(8,128)S(1)} %get-tuple-element.69.rest_1_.rest_3_.rest_5_), channel_id=1, source_target_pairs={{0,1},{1,0},{2,3},{3,2},{4,5},{5,4},{6,7},{7,6},{8,9},{9,8},{10,11... | collective-permute-start | bytes 884744 | tf_op jit(solution)/shard_map/ppermute | solution.py:311
  15.6 1.5 weights.1
  19.6 3.1 %collective-permute-start.10 = (f32[192,384]{1,0:T(8,128)S(1)}, f32[192,384]{1,0:T(8,128)S(1)}, u32[]{:S(2)}, u32[]{:S(2)}) collective-permute-start(f32[192,384]{1,0:T(8,128)S(1)} %get-tuple-element.57.rest_1_.rest_3_), channel_id=1, source_target_pairs={{0,1},{1,0},{2,3},{3,2},{4,5},{5,4},{6,7},{7,6},{8,9},{9,8},{10,11... | collective-permute-start | bytes 884744 | tf_op jit(solution)/shard_map/ppermute | solution.py:311
  25.3 5.0 %collective-permute-start.24 = (f32[192,384]{1,0:T(8,128)S(1)}, f32[192,384]{1,0:T(8,128)S(1)}, u32[]{:S(2)}, u32[]{:S(2)}) collective-permute-start(f32[192,384]{1,0:T(8,128)S(1)} %get-tuple-element.71.rest_1_.rest_3_), channel_id=1, source_target_pairs={{0,1},{1,0},{2,3},{3,2},{4,5},{5,4},{6,7},{7,6},{8,9},{9,8},{10,11... | collective-permute-start | bytes 884744 | tf_op jit(solution)/shard_map/ppermute | solution.py:311
  32.8 3.2 %collective-permute-start.12 = (f32[192,384]{1,0:T(8,128)S(1)}, f32[192,384]{1,0:T(8,128)S(1)}, u32[]{:S(2)}, u32[]{:S(2)}) collective-permute-start(f32[192,384]{1,0:T(8,128)S(1)} %get-tuple-element.59.rest_1_.rest_3_), channel_id=1, source_target_pairs={{0,1},{1,0},{2,3},{3,2},{4,5},{5,4},{6,7},{7,6},{8,9},{9,8},{10,11... | collective-permute-start | bytes 884744 | tf_op jit(solution)/shard_map/ppermute | solution.py:311
  39.7 3.3 %collective-permute-start.26 = (f32[192,384]{1,0:T(8,128)S(1)}, f32[192,384]{1,0:T(8,128)S(1)}, u32[]{:S(2)}, u32[]{:S(2)}) collective-permute-start(f32[192,384]{1,0:T(8,128)S(1)} %get-tuple-element.73.rest_1_.rest_3_), channel_id=1, source_target_pairs={{0,1},{1,0},{2,3},{3,2},{4,5},{5,4},{6,7},{7,6},{8,9},{9,8},{10,11... | collective-permute-start | bytes 884744 | tf_op jit(solution)/shard_map/ppermute | solution.py:311
  43.0 1.7 %collective-permute-start.2 = (f32[384,768]{1,0:T(8,128)S(1)}, f32[384,768]{1,0:T(8,128)}, u32[]{:S(2)}, u32[]{:S(2)}) collective-permute-start(f32[384,768]{1,0:T(8,128)S(1)} %collective-permute-done.1.refs_2_), channel_id=1, source_target_pairs={{8,16},{16,24},{9,17},{17,25},{10,18},{18,26},{11,19},{19,27},{12,... | collective-permute-start | bytes 3538952 | tf_op jit(solution)/shard_map/ppermute | solution.py:220
  47.6 3.4 %collective-permute-start.14 = (f32[192,384]{1,0:T(8,128)S(1)}, f32[192,384]{1,0:T(8,128)S(1)}, u32[]{:S(2)}, u32[]{:S(2)}) collective-permute-start(f32[192,384]{1,0:T(8,128)S(1)} %get-tuple-element.61.rest_1_.rest_3_), channel_id=1, source_target_pairs={{0,1},{1,0},{2,3},{3,2},{4,5},{5,4},{6,7},{7,6},{8,9},{9,8},{10,11... | collective-permute-start | bytes 884744 | tf_op jit(solution)/shard_map/ppermute | solution.py:311
  53.5 4.0 %collective-permute-start.28 = (f32[192,384]{1,0:T(8,128)S(1)}, f32[192,384]{1,0:T(8,128)S(1)}, u32[]{:S(2)}, u32[]{:S(2)}) collective-permute-start(f32[192,384]{1,0:T(8,128)S(1)} %get-tuple-element.75.rest_1_.rest_3_), channel_id=1, source_target_pairs={{0,1},{1,0},{2,3},{3,2},{4,5},{5,4},{6,7},{7,6},{8,9},{9,8},{10,11... | collective-permute-start | bytes 884744 | tf_op jit(solution)/shard_map/ppermute | solution.py:311
  61.2 4.1 %collective-permute-start.16 = (f32[192,384]{1,0:T(8,128)S(1)}, f32[192,384]{1,0:T(8,128)S(1)}, u32[]{:S(2)}, u32[]{:S(2)}) collective-permute-start(f32[192,384]{1,0:T(8,128)S(1)} %get-tuple-element.63.rest_1_.rest_3_), channel_id=1, source_target_pairs={{0,1},{1,0},{2,3},{3,2},{4,5},{5,4},{6,7},{7,6},{8,9},{9,8},{10,11... | collective-permute-start | bytes 884744 | tf_op jit(solution)/shard_map/ppermute | solution.py:311
  66.7 4.4 %collective-permute-start.30 = (f32[192,384]{1,0:T(8,128)S(1)}, f32[192,384]{1,0:T(8,128)S(1)}, u32[]{:S(2)}, u32[]{:S(2)}) collective-permute-start(f32[192,384]{1,0:T(8,128)S(1)} %get-tuple-element.77.rest_1_.rest_3_), channel_id=1, source_target_pairs={{0,1},{1,0},{2,3},{3,2},{4,5},{5,4},{6,7},{7,6},{8,9},{9,8},{10,11... | collective-permute-start | bytes 884744 | tf_op jit(solution)/shard_map/ppermute | solution.py:311
  73.6 4.1 %collective-permute-start.18 = (f32[192,384]{1,0:T(8,128)S(1)}, f32[192,384]{1,0:T(8,128)S(1)}, u32[]{:S(2)}, u32[]{:S(2)}) collective-permute-start(f32[192,384]{1,0:T(8,128)S(1)} %get-tuple-element.65.rest_1_), channel_id=1, source_target_pairs={{0,1},{1,0},{2,3},{3,2},{4,5},{5,4},{6,7},{7,6},{8,9},{9,8},{10,11... | collective-permute-start | bytes 884744 | tf_op jit(solution)/shard_map/ppermute | solution.py:311
  79.6 1.7 %collective-permute-start.3 = (f32[384,768]{1,0:T(8,128)}, f32[384,768]{1,0:T(8,128)}, u32[]{:S(2)}, u32[]{:S(2)}) collective-permute-start(f32[384,768]{1,0:T(8,128)} %collective-permute-done.2.refs_1_), channel_id=1, source_target_pairs={{16,24},{17,25},{18,26},{19,27},{20,28},{21,29},{22,30},{23,31}} | collective-permute-start | bytes 3538952 | tf_op jit(solution)/shard_map/ppermute | solution.py:220
  84.5 3.1 %collective-permute-start.32 = (f32[192,384]{1,0:T(8,128)S(1)}, f32[192,384]{1,0:T(8,128)S(1)}, u32[]{:S(2)}, u32[]{:S(2)}) collective-permute-start(f32[192,384]{1,0:T(8,128)S(1)} %get-tuple-element.79.rest_1_), channel_id=1, source_target_pairs={{0,1},{1,0},{2,3},{3,2},{4,5},{5,4},{6,7},{7,6},{8,9},{9,8},{10,11... | collective-permute-start | bytes 884744 | tf_op jit(solution)/shard_map/ppermute | solution.py:311
  90.4 3.9 %collective-permute-start.20 = (f32[192,384]{1,0:T(8,128)S(1)}, f32[192,384]{1,0:T(8,128)S(1)}, u32[]{:S(2)}, u32[]{:S(2)}) collective-permute-start(f32[192,384]{1,0:T(8,128)S(1)} %get-tuple-element.67.rest_1_), channel_id=1, source_target_pairs={{0,1},{1,0},{2,3},{3,2},{4,5},{5,4},{6,7},{7,6},{8,9},{9,8},{10,11... | collective-permute-start | bytes 884744 | tf_op jit(solution)/shard_map/ppermute | solution.py:311
  95.7 4.9 %collective-permute-start.34 = (f32[192,384]{1,0:T(8,128)S(1)}, f32[192,384]{1,0:T(8,128)S(1)}, u32[]{:S(2)}, u32[]{:S(2)}) collective-permute-start(f32[192,384]{1,0:T(8,128)S(1)} %get-tuple-element.81.rest_1_.rest_3_), channel_id=1, source_target_pairs={{0,1},{1,0},{2,3},{3,2},{4,5},{5,4},{6,7},{7,6},{8,9},{9,8},{10,11... | collective-permute-start | bytes 884744 | tf_op jit(solution)/shard_map/ppermute | solution.py:311
  102.8 1.5 tail.20.rest_0_
  104.4 1.5 %tail.27.rest_1_ = f32[192,768]{1,0:T(8,128)} custom-call(f32[192,768]{1,0:T(8,128)S(1)} %base.27, f32[192,384]{1,0:T(8,128)S(1)} %collective-permute-done.33.got_far, f32[192,384]{1,0:T(8,128)S(1)} %collective-permute-done.34.got_near.rest_3_, bf16[384,384]{1,0:T(8,128)(2,1)S(1)} %get-tuple-element.52.fh, bf16[384,384]{1,0:T(8,128)(2,1)S(1)} %get-tuple-element.53.fl, ...), custom_call_target="tpu_custom_call" | custom-call | flops 339738624 | bytes 2949120 | tf_op jit(solution)/shard_map/tail/pallas_call | solution.py:26
  105.9 2.8 %collective-permute-start.36 = (f32[192,768]{1,0:T(8,128)}, f32[192,768]{1,0:T(8,128)}, u32[]{:S(2)}, u32[]{:S(2)}) collective-permute-start(f32[192,768]{1,0:T(8,128)} %tail.27.rest_1_), channel_id=1, source_target_pairs={{0,1},{1,0},{2,3},{3,2},{4,5},{5,4},{6,7},{7,6},{8,9},{9,8},{10,11... | collective-permute-start | bytes 1769480 | tf_op jit(solution)/shard_map/ppermute | solution.py:331
  109.2 5.9 %collective-permute-done.6.refs_6_ = f32[384,768]{1,0:T(8,128)} collective-permute-done((f32[384,768]{1,0:T(8,128)}, f32[384,768]{1,0:T(8,128)}, u32[]{:S(2)}, u32[]{:S(2)}) %collective-permute-start.6) | collective-permute-done | bytes 1179680 | tf_op jit(solution)/shard_map/ppermute | solution.py:221
  116.4 3.1 %assemble.1 = (bf16[768,768]{1,0:T(8,128)(2,1)S(1)}, bf16[768,768]{1,0:T(8,128)(2,1)S(1)}, bf16[768,768]{1,0:T(8,128)(2,1)S(1)}, bf16[768,768]{1,0:T(8,128)(2,1)S(1)}) custom-call(s32[1]{0:T(128)} %bitcast.place_ref, f32[384,768]{1,0:T(8,128)} %collective-permute-done.3.refs_0_, f32[384,768]{1,0:T(8,128)} %collective-permute-done.2.refs_1_, ...), custom_call_target="tpu_custom_call" | custom-call | bytes 12976132 | tf_op jit(solution)/shard_map/assemble/pallas_call | solution.py:26
  119.5 3.3 %own_product.2.acc_ref = f32[384,768]{1,0:T(8,128)S(1)} custom-call(bf16[768,768]{1,0:T(8,128)(2,1)S(1)} %get-tuple-element.46.high_ref, bf16[768,768]{1,0:T(8,128)(2,1)S(1)} %get-tuple-element.47.low_ref, f32[192,768]{1,0:T(8,128)} %tail.20.rest_0_, f32[192,768]{1,0:T(8,128)} %tail.27.rest_1_), custom_call_target="tpu_custom_call" | custom-call | flops 1358954496 | bytes 4718592 | tf_op jit(solution)/shard_map/own_product/pallas_call | solution.py:26
  122.9 3.4 %other_product.2 = f32[768,384]{1,0:T(8,128)S(1)} custom-call(bf16[768,768]{1,0:T(8,128)(2,1)S(1)} %get-tuple-element.44.high_ref, bf16[768,768]{1,0:T(8,128)(2,1)S(1)} %get-tuple-element.45.low_ref, f32[384,768]{1,0:T(8,128)S(1)} %own_product.2.acc_ref, f32[192,768]{1,0:T(8,128)S(1)} %collective-permute-done.35.rest_0_, ...), custom_call_target="tpu_custom_call" | custom-call | flops 1358954496 | bytes 5898240 | tf_op jit(solution)/shard_map/other_product/pallas_call | solution.py:26
  126.4 2.4 %collective-permute-start.39 = (f32[2,96,384]{2,1,0:T(8,128)S(1)}, f32[2,96,384]{2,1,0:T(8,128)S(1)}, u32[]{:S(2)}, u32[]{:S(2)}) collective-permute-start(f32[2,96,384]{2,1,0:T(8,128)S(1)} %dynamic-slice_bitcast_fusion.2), channel_id=1, source_target_pairs={{0,4},{1,5},{2,6},{3,7},{4,0},{5,1},{6,2},{7,3},{8,12},{9,13},{10,... | collective-permute-start | bytes 884744 | tf_op jit(solution)/shard_map/ppermute | solution.py:276
  129.0 2.1 %own_product.3.acc_ref = f32[384,768]{1,0:T(8,128)S(1)} custom-call(bf16[768,768]{1,0:T(8,128)(2,1)S(1)} %get-tuple-element.46.high_ref, bf16[768,768]{1,0:T(8,128)(2,1)S(1)} %get-tuple-element.47.low_ref, f32[192,384]{1,0:T(8,128)S(1)} %copy-done.5, f32[192,384]{1,0:T(8,128)S(1)} %copy-done.7, f32[192,384]{1,0:T(8,128)S(1)} %copy-done.9, ...), custom_call_target="tpu_custom_call" | custom-call | flops 1358954496 | bytes 4718592 | tf_op jit(solution)/shard_map/own_product/pallas_call | solution.py:26
  131.1 2.3 %other_product.3 = f32[768,384]{1,0:T(8,128)S(1)} custom-call(bf16[768,768]{1,0:T(8,128)(2,1)S(1)} %get-tuple-element.44.high_ref, bf16[768,768]{1,0:T(8,128)(2,1)S(1)} %get-tuple-element.45.low_ref, f32[384,768]{1,0:T(8,128)S(1)} %own_product.3.acc_ref, f32[192,384]{1,0:T(8,128)S(1)} %collective-permute-done.41.rest_0_, ...), custom_call_target="tpu_custom_call" | custom-call | flops 1358954496 | bytes 5898240 | tf_op jit(solution)/shard_map/other_product/pallas_call | solution.py:26
  138.5 5.1 %collective-permute-done.45 = f32[2,96,384]{2,1,0:T(8,128)S(1)} collective-permute-done((f32[2,96,384]{2,1,0:T(8,128)S(1)}, f32[2,96,384]{2,1,0:T(8,128)S(1)}, u32[]{:S(2)}, u32[]{:S(2)}) %collective-permute-start.45) | collective-permute-done | bytes 294944 | tf_op jit(solution)/shard_map/ppermute | solution.py:276
  143.6 2.0 %collective-permute-start.46 = (f32[96,384]{1,0:T(8,128)S(1)}, f32[96,384]{1,0:T(8,128)S(1)}, u32[]{:S(2)}, u32[]{:S(2)}) collective-permute-start(f32[96,384]{1,0:T(8,128)S(1)} %dynamic-slice_bitcast_fusion.4), channel_id=1, source_target_pairs={{0,2},{1,3},{2,0},{3,1},{4,6},{5,7},{6,4},{7,5},{8,10},{9,11},{10,... | collective-permute-start | bytes 442376 | tf_op jit(solution)/shard_map/ppermute | solution.py:276
  145.8 1.9 %collective-permute-done.40 = f32[96,384]{1,0:T(8,128)S(1)} collective-permute-done((f32[96,384]{1,0:T(8,128)S(1)}, f32[96,384]{1,0:T(8,128)S(1)}, u32[]{:S(2)}, u32[]{:S(2)}) %collective-permute-start.40) | collective-permute-done | bytes 147488 | tf_op jit(solution)/shard_map/ppermute | solution.py:276
  147.8 2.3 %collective-permute-done.46 = f32[96,384]{1,0:T(8,128)S(1)} collective-permute-done((f32[96,384]{1,0:T(8,128)S(1)}, f32[96,384]{1,0:T(8,128)S(1)}, u32[]{:S(2)}, u32[]{:S(2)}) %collective-permute-start.46) | collective-permute-done | bytes 147488 | tf_op jit(solution)/shard_map/ppermute | solution.py:276
  (145 shorter events, 49.8 us)
Async XLA Ops:
  2.6 10.1 %collective-permute-start.7 = (f32[192,384]{1,0:T(8,128)S(1)}, f32[192,384]{1,0:T(8,128)S(1)}, u32[]{:S(2)}, u32[]{:S(2)}) collective-permute-start(f32[192,384]{1,0:T(8,128)S(1)} %get-tuple-element.50.rest_0_.rest_2_.rest_4_), channel_id=1, source_target_pairs={{1,2},{3,4},{5,6},{2,1},{4,3},{6,5},{9,10},{11,12},{13,14},{10,9},... | collective-permute-start | bytes 884744 | tf_op jit(solution)/shard_map/ppermute | solution.py:311
  4.3 38.7 %collective-permute-start.1 = (f32[384,768]{1,0:T(8,128)S(1)}, f32[384,768]{1,0:T(8,128)S(1)}, u32[]{:S(2)}, u32[]{:S(2)}) collective-permute-start(f32[384,768]{1,0:T(8,128)S(1)} %constant_dynamic-update-slice_fusion.refs_3_), channel_id=1, source_target_pairs={{0,8},{8,16},{16,24},{1,9},{9,17},{17,25},{2,10},{10,18},{18,26},{... | collective-permute-start | bytes 3538952 | tf_op jit(solution)/shard_map/ppermute | solution.py:220
  9.2 35.5 %collective-permute-start.4 = (f32[384,768]{1,0:T(8,128)S(1)}, f32[384,768]{1,0:T(8,128)S(1)}, u32[]{:S(2)}, u32[]{:S(2)}) collective-permute-start(f32[384,768]{1,0:T(8,128)S(1)} %constant_dynamic-update-slice_fusion.refs_3_), channel_id=1, source_target_pairs={{24,16},{16,8},{8,0},{25,17},{17,9},{9,1},{26,18},{18,10},{10,2},{... | collective-permute-start | bytes 3538952 | tf_op jit(solution)/shard_map/ppermute | solution.py:221
  12.7 11.1 %collective-permute-start.22 = (f32[192,384]{1,0:T(8,128)S(1)}, f32[192,384]{1,0:T(8,128)S(1)}, u32[]{:S(2)}, u32[]{:S(2)}) collective-permute-start(f32[192,384]{1,0:T(8,128)S(1)} %get-tuple-element.69.rest_1_.rest_3_.rest_5_), channel_id=1, source_target_pairs={{0,1},{1,0},{2,3},{3,2},{4,5},{5,4},{6,7},{7,6},{8,9},{9,8},{10,11... | collective-permute-start | bytes 884744 | tf_op jit(solution)/shard_map/ppermute | solution.py:311
  19.6 11.7 %collective-permute-start.10 = (f32[192,384]{1,0:T(8,128)S(1)}, f32[192,384]{1,0:T(8,128)S(1)}, u32[]{:S(2)}, u32[]{:S(2)}) collective-permute-start(f32[192,384]{1,0:T(8,128)S(1)} %get-tuple-element.57.rest_1_.rest_3_), channel_id=1, source_target_pairs={{0,1},{1,0},{2,3},{3,2},{4,5},{5,4},{6,7},{7,6},{8,9},{9,8},{10,11... | collective-permute-start | bytes 884744 | tf_op jit(solution)/shard_map/ppermute | solution.py:311
  25.3 11.9 %collective-permute-start.24 = (f32[192,384]{1,0:T(8,128)S(1)}, f32[192,384]{1,0:T(8,128)S(1)}, u32[]{:S(2)}, u32[]{:S(2)}) collective-permute-start(f32[192,384]{1,0:T(8,128)S(1)} %get-tuple-element.71.rest_1_.rest_3_), channel_id=1, source_target_pairs={{0,1},{1,0},{2,3},{3,2},{4,5},{5,4},{6,7},{7,6},{8,9},{9,8},{10,11... | collective-permute-start | bytes 884744 | tf_op jit(solution)/shard_map/ppermute | solution.py:311
  32.8 13.2 %collective-permute-start.12 = (f32[192,384]{1,0:T(8,128)S(1)}, f32[192,384]{1,0:T(8,128)S(1)}, u32[]{:S(2)}, u32[]{:S(2)}) collective-permute-start(f32[192,384]{1,0:T(8,128)S(1)} %get-tuple-element.59.rest_1_.rest_3_), channel_id=1, source_target_pairs={{0,1},{1,0},{2,3},{3,2},{4,5},{5,4},{6,7},{7,6},{8,9},{9,8},{10,11... | collective-permute-start | bytes 884744 | tf_op jit(solution)/shard_map/ppermute | solution.py:311
  37.9 9.7 %collective-permute-start.25 = (f32[192,384]{1,0:T(8,128)S(1)}, f32[192,384]{1,0:T(8,128)S(1)}, u32[]{:S(2)}, u32[]{:S(2)}) collective-permute-start(f32[192,384]{1,0:T(8,128)S(1)} %get-tuple-element.72.rest_0_.rest_2_), channel_id=1, source_target_pairs={{1,2},{3,4},{5,6},{2,1},{4,3},{6,5},{9,10},{11,12},{13,14},{10,9},... | collective-permute-start | bytes 884744 | tf_op jit(solution)/shard_map/ppermute | solution.py:311
  39.7 12.4 %collective-permute-start.26 = (f32[192,384]{1,0:T(8,128)S(1)}, f32[192,384]{1,0:T(8,128)S(1)}, u32[]{:S(2)}, u32[]{:S(2)}) collective-permute-start(f32[192,384]{1,0:T(8,128)S(1)} %get-tuple-element.73.rest_1_.rest_3_), channel_id=1, source_target_pairs={{0,1},{1,0},{2,3},{3,2},{4,5},{5,4},{6,7},{7,6},{8,9},{9,8},{10,11... | collective-permute-start | bytes 884744 | tf_op jit(solution)/shard_map/ppermute | solution.py:311
  43.0 36.6 %collective-permute-start.2 = (f32[384,768]{1,0:T(8,128)S(1)}, f32[384,768]{1,0:T(8,128)}, u32[]{:S(2)}, u32[]{:S(2)}) collective-permute-start(f32[384,768]{1,0:T(8,128)S(1)} %collective-permute-done.1.refs_2_), channel_id=1, source_target_pairs={{8,16},{16,24},{9,17},{17,25},{10,18},{18,26},{11,19},{19,27},{12,... | collective-permute-start | bytes 3538952 | tf_op jit(solution)/shard_map/ppermute | solution.py:220
  44.7 36.6 %collective-permute-start.5 = (f32[384,768]{1,0:T(8,128)S(1)}, f32[384,768]{1,0:T(8,128)}, u32[]{:S(2)}, u32[]{:S(2)}) collective-permute-start(f32[384,768]{1,0:T(8,128)S(1)} %collective-permute-done.4.refs_4_), channel_id=1, source_target_pairs={{16,8},{8,0},{17,9},{9,1},{18,10},{10,2},{19,11},{11,3},{20,12},{1... | collective-permute-start | bytes 3538952 | tf_op jit(solution)/shard_map/ppermute | solution.py:221
  47.6 11.1 %collective-permute-start.14 = (f32[192,384]{1,0:T(8,128)S(1)}, f32[192,384]{1,0:T(8,128)S(1)}, u32[]{:S(2)}, u32[]{:S(2)}) collective-permute-start(f32[192,384]{1,0:T(8,128)S(1)} %get-tuple-element.61.rest_1_.rest_3_), channel_id=1, source_target_pairs={{0,1},{1,0},{2,3},{3,2},{4,5},{5,4},{6,7},{7,6},{8,9},{9,8},{10,11... | collective-permute-start | bytes 884744 | tf_op jit(solution)/shard_map/ppermute | solution.py:311
  53.5 11.8 %collective-permute-start.28 = (f32[192,384]{1,0:T(8,128)S(1)}, f32[192,384]{1,0:T(8,128)S(1)}, u32[]{:S(2)}, u32[]{:S(2)}) collective-permute-start(f32[192,384]{1,0:T(8,128)S(1)} %get-tuple-element.75.rest_1_.rest_3_), channel_id=1, source_target_pairs={{0,1},{1,0},{2,3},{3,2},{4,5},{5,4},{6,7},{7,6},{8,9},{9,8},{10,11... | collective-permute-start | bytes 884744 | tf_op jit(solution)/shard_map/ppermute | solution.py:311
  61.2 11.0 %collective-permute-start.16 = (f32[192,384]{1,0:T(8,128)S(1)}, f32[192,384]{1,0:T(8,128)S(1)}, u32[]{:S(2)}, u32[]{:S(2)}) collective-permute-start(f32[192,384]{1,0:T(8,128)S(1)} %get-tuple-element.63.rest_1_.rest_3_), channel_id=1, source_target_pairs={{0,1},{1,0},{2,3},{3,2},{4,5},{5,4},{6,7},{7,6},{8,9},{9,8},{10,11... | collective-permute-start | bytes 884744 | tf_op jit(solution)/shard_map/ppermute | solution.py:311
  66.7 12.1 %collective-permute-start.30 = (f32[192,384]{1,0:T(8,128)S(1)}, f32[192,384]{1,0:T(8,128)S(1)}, u32[]{:S(2)}, u32[]{:S(2)}) collective-permute-start(f32[192,384]{1,0:T(8,128)S(1)} %get-tuple-element.77.rest_1_.rest_3_), channel_id=1, source_target_pairs={{0,1},{1,0},{2,3},{3,2},{4,5},{5,4},{6,7},{7,6},{8,9},{9,8},{10,11... | collective-permute-start | bytes 884744 | tf_op jit(solution)/shard_map/ppermute | solution.py:311
  73.0 11.5 %collective-permute-start.17 = (f32[192,384]{1,0:T(8,128)S(1)}, f32[192,384]{1,0:T(8,128)S(1)}, u32[]{:S(2)}, u32[]{:S(2)}) collective-permute-start(f32[192,384]{1,0:T(8,128)S(1)} %get-tuple-element.64.rest_0_), channel_id=1, source_target_pairs={{1,2},{3,4},{5,6},{2,1},{4,3},{6,5},{9,10},{11,12},{13,14},{10,9},... | collective-permute-start | bytes 884744 | tf_op jit(solution)/shard_map/ppermute | solution.py:311
  73.6 13.9 %collective-permute-start.18 = (f32[192,384]{1,0:T(8,128)S(1)}, f32[192,384]{1,0:T(8,128)S(1)}, u32[]{:S(2)}, u32[]{:S(2)}) collective-permute-start(f32[192,384]{1,0:T(8,128)S(1)} %get-tuple-element.65.rest_1_), channel_id=1, source_target_pairs={{0,1},{1,0},{2,3},{3,2},{4,5},{5,4},{6,7},{7,6},{8,9},{9,8},{10,11... | collective-permute-start | bytes 884744 | tf_op jit(solution)/shard_map/ppermute | solution.py:311
  79.6 29.1 %collective-permute-start.3 = (f32[384,768]{1,0:T(8,128)}, f32[384,768]{1,0:T(8,128)}, u32[]{:S(2)}, u32[]{:S(2)}) collective-permute-start(f32[384,768]{1,0:T(8,128)} %collective-permute-done.2.refs_1_), channel_id=1, source_target_pairs={{16,24},{17,25},{18,26},{19,27},{20,28},{21,29},{22,30},{23,31}} | collective-permute-start | bytes 3538952 | tf_op jit(solution)/shard_map/ppermute | solution.py:220
  81.3 33.8 %collective-permute-start.6 = (f32[384,768]{1,0:T(8,128)}, f32[384,768]{1,0:T(8,128)}, u32[]{:S(2)}, u32[]{:S(2)}) collective-permute-start(f32[384,768]{1,0:T(8,128)} %collective-permute-done.5.refs_5_), channel_id=1, source_target_pairs={{8,0},{9,1},{10,2},{11,3},{12,4},{13,5},{14,6},{15,7}} | collective-permute-start | bytes 3538952 | tf_op jit(solution)/shard_map/ppermute | solution.py:221
  84.5 9.8 %collective-permute-start.32 = (f32[192,384]{1,0:T(8,128)S(1)}, f32[192,384]{1,0:T(8,128)S(1)}, u32[]{:S(2)}, u32[]{:S(2)}) collective-permute-start(f32[192,384]{1,0:T(8,128)S(1)} %get-tuple-element.79.rest_1_), channel_id=1, source_target_pairs={{0,1},{1,0},{2,3},{3,2},{4,5},{5,4},{6,7},{7,6},{8,9},{9,8},{10,11... | collective-permute-start | bytes 884744 | tf_op jit(solution)/shard_map/ppermute | solution.py:311
  90.4 12.4 %collective-permute-start.20 = (f32[192,384]{1,0:T(8,128)S(1)}, f32[192,384]{1,0:T(8,128)S(1)}, u32[]{:S(2)}, u32[]{:S(2)}) collective-permute-start(f32[192,384]{1,0:T(8,128)S(1)} %get-tuple-element.67.rest_1_), channel_id=1, source_target_pairs={{0,1},{1,0},{2,3},{3,2},{4,5},{5,4},{6,7},{7,6},{8,9},{9,8},{10,11... | collective-permute-start | bytes 884744 | tf_op jit(solution)/shard_map/ppermute | solution.py:311
  95.0 9.3 %collective-permute-start.33 = (f32[192,384]{1,0:T(8,128)S(1)}, f32[192,384]{1,0:T(8,128)S(1)}, u32[]{:S(2)}, u32[]{:S(2)}) collective-permute-start(f32[192,384]{1,0:T(8,128)S(1)} %get-tuple-element.80.rest_0_.rest_2_), channel_id=1, source_target_pairs={{1,2},{3,4},{5,6},{2,1},{4,3},{6,5},{9,10},{11,12},{13,14},{10,9},... | collective-permute-start | bytes 884744 | tf_op jit(solution)/shard_map/ppermute | solution.py:311
  104.3 18.5 %collective-permute-start.35 = (f32[192,768]{1,0:T(8,128)}, f32[192,768]{1,0:T(8,128)S(1)}, u32[]{:S(2)}, u32[]{:S(2)}) collective-permute-start(f32[192,768]{1,0:T(8,128)} %tail.20.rest_0_), channel_id=1, source_target_pairs={{0,1},{1,0},{2,3},{3,2},{4,5},{5,4},{6,7},{7,6},{8,9},{9,8},{10,11... | collective-permute-start | bytes 1769480 | tf_op jit(solution)/shard_map/ppermute | solution.py:331
  105.9 17.0 %collective-permute-start.36 = (f32[192,768]{1,0:T(8,128)}, f32[192,768]{1,0:T(8,128)}, u32[]{:S(2)}, u32[]{:S(2)}) collective-permute-start(f32[192,768]{1,0:T(8,128)} %tail.27.rest_1_), channel_id=1, source_target_pairs={{0,1},{1,0},{2,3},{3,2},{4,5},{5,4},{6,7},{7,6},{8,9},{9,8},{10,11... | collective-permute-start | bytes 1769480 | tf_op jit(solution)/shard_map/ppermute | solution.py:331
  108.7 22.4 %collective-permute-start.41 = (f32[192,384]{1,0:T(8,128)}, f32[192,384]{1,0:T(8,128)S(1)}, u32[]{:S(2)}, u32[]{:S(2)}) collective-permute-start(f32[192,384]{1,0:T(8,128)} %copy-done.4), channel_id=1, source_target_pairs={{0,1},{1,0},{2,3},{3,2},{4,5},{5,4},{6,7},{7,6},{8,9},{9,8},{10,11... | collective-permute-start | bytes 884744 | tf_op jit(solution)/shard_map/ppermute | solution.py:329
  108.7 22.4 %collective-permute-start.42 = (f32[192,384]{1,0:T(8,128)}, f32[192,384]{1,0:T(8,128)S(1)}, u32[]{:S(2)}, u32[]{:S(2)}) collective-permute-start(f32[192,384]{1,0:T(8,128)} %copy-done.8), channel_id=1, source_target_pairs={{0,1},{1,0},{2,3},{3,2},{4,5},{5,4},{6,7},{7,6},{8,9},{9,8},{10,11... | collective-permute-start | bytes 884744 | tf_op jit(solution)/shard_map/ppermute | solution.py:329
  126.4 9.5 %collective-permute-start.39 = (f32[2,96,384]{2,1,0:T(8,128)S(1)}, f32[2,96,384]{2,1,0:T(8,128)S(1)}, u32[]{:S(2)}, u32[]{:S(2)}) collective-permute-start(f32[2,96,384]{2,1,0:T(8,128)S(1)} %dynamic-slice_bitcast_fusion.2), channel_id=1, source_target_pairs={{0,4},{1,5},{2,6},{3,7},{4,0},{5,1},{6,2},{7,3},{8,12},{9,13},{10,... | collective-permute-start | bytes 884744 | tf_op jit(solution)/shard_map/ppermute | solution.py:276
  128.9 9.1 %collective-permute-start.37 = (f32[2,96,384]{2,1,0:T(8,128)S(1)}, f32[2,96,384]{2,1,0:T(8,128)S(1)}, u32[]{:S(2)}, u32[]{:S(2)}) collective-permute-start(f32[2,96,384]{2,1,0:T(8,128)S(1)} %dynamic-slice_bitcast_fusion.3), channel_id=1, source_target_pairs={{0,2},{1,3},{2,0},{3,1},{4,6},{5,7},{6,4},{7,5},{8,10},{9,11},{10,... | collective-permute-start | bytes 884744 | tf_op jit(solution)/shard_map/ppermute | solution.py:276
  133.6 10.0 %collective-permute-start.45 = (f32[2,96,384]{2,1,0:T(8,128)S(1)}, f32[2,96,384]{2,1,0:T(8,128)S(1)}, u32[]{:S(2)}, u32[]{:S(2)}) collective-permute-start(f32[2,96,384]{2,1,0:T(8,128)S(1)} %dynamic-slice_bitcast_fusion), channel_id=1, source_target_pairs={{0,4},{1,5},{2,6},{3,7},{4,0},{5,1},{6,2},{7,3},{8,12},{9,13},{10,... | collective-permute-start | bytes 884744 | tf_op jit(solution)/shard_map/ppermute | solution.py:276
  134.6 11.0 %collective-permute-start.43 = (f32[2,96,384]{2,1,0:T(8,128)S(1)}, f32[2,96,384]{2,1,0:T(8,128)S(1)}, u32[]{:S(2)}, u32[]{:S(2)}) collective-permute-start(f32[2,96,384]{2,1,0:T(8,128)S(1)} %dynamic-slice_bitcast_fusion.1), channel_id=1, source_target_pairs={{0,2},{1,3},{2,0},{3,1},{4,6},{5,7},{6,4},{7,5},{8,10},{9,11},{10,... | collective-permute-start | bytes 884744 | tf_op jit(solution)/shard_map/ppermute | solution.py:276
  136.0 11.7 %collective-permute-start.40 = (f32[96,384]{1,0:T(8,128)S(1)}, f32[96,384]{1,0:T(8,128)S(1)}, u32[]{:S(2)}, u32[]{:S(2)}) collective-permute-start(f32[96,384]{1,0:T(8,128)S(1)} %dynamic-slice_bitcast_fusion.6), channel_id=1, source_target_pairs={{0,2},{1,3},{2,0},{3,1},{4,6},{5,7},{6,4},{7,5},{8,10},{9,11},{10,... | collective-permute-start | bytes 442376 | tf_op jit(solution)/shard_map/ppermute | solution.py:276
  138.1 9.7 %collective-permute-start.38 = (f32[96,384]{1,0:T(8,128)S(1)}, f32[96,384]{1,0:T(8,128)S(1)}, u32[]{:S(2)}, u32[]{:S(2)}) collective-permute-start(f32[96,384]{1,0:T(8,128)S(1)} %dynamic-slice_bitcast_fusion.7), channel_id=1, source_target_pairs={{0,4},{1,5},{2,6},{3,7},{4,0},{5,1},{6,2},{7,3},{8,12},{9,13},{10,... | collective-permute-start | bytes 442376 | tf_op jit(solution)/shard_map/ppermute | solution.py:276
  (28 other events, 183.2 us)

commit v3 on v2

--- a/solution.py
+++ b/solution.py
@@ -222,32 +222,15 @@
     return before[:0:-1] + after
 
 
-def tiles(width):
-    step = 256 if width % 256 == 0 else width
-    return width // step, step
-
-
 def first_product_kernel(high_ref, low_ref, *rest):
     out_ref = rest[-1]
-    operand = split(joined(rest[:-1]))
-    count, step = tiles(out_ref.shape[1])
-
-    @pl.loop(0, count)
-    def _(i):
-        columns = pl.ds(pl.multiple_of(i * step, step), step)
-        out_ref[:, columns] = dot3(operand, (high_ref[:, columns], low_ref[:, columns]))
+    out_ref[...] = dot3(split(joined(rest[:-1])), (high_ref[...], low_ref[...]))
 
 
 def second_product_kernel(high_ref, low_ref, acc_ref, *rest):
     out_ref = rest[-1]
-    operand = split(joined(rest[:-1]))
-    count, step = tiles(out_ref.shape[0])
-
-    @pl.loop(0, count)
-    def _(i):
-        columns = pl.ds(pl.multiple_of(i * step, step), step)
-        value = acc_ref[:, columns] + dot3(operand, (high_ref[:, columns], low_ref[:, columns]))
-        out_ref[columns, :] = value.T
+    value = acc_ref[...] + dot3(split(joined(rest[:-1])), (high_ref[...], low_ref[...]))
+    out_ref[...] = value.T
 
 
 def joined(refs):

time: 152 us -> 151 us (level)
  waiting for transfers between devices: 17.5 us -> 20.4 us
  Pallas kernels: 43.1 us -> 40.8 us
  starting transfers between devices: 84.8 us -> 83.1 us
    ppermute x8, waiting for transfers between devices: 10.7 us -> 13.6 us  [halve(): lax.ppermute(other, 'col', [(i, i ^ 1 << bit) for i in range(count)])]
    pallas_call x35, Pallas kernels: 43.1 us -> 40.8 us  [call(): pl.pallas_call(kernel, out_shape=out_shape, in_specs=specs, out_specs=[WH...]
    ppermute x8, starting transfers between devices: 8 us -> 6.28 us  [halve(): lax.ppermute(other, 'col', [(i, i ^ 1 << bit) for i in range(count)])]
  transfers between devices with their start and end apart: 47 -> 47, of which waited for: 7 -> 8; matrix products, arithmetic and copies ran while one was open for 1% -> 1% of each run, Pallas kernels for 28% -> 27%
where the time goes in v3:
time: 151 us; the launch traced here: 150 us
  starting transfers between devices  83.1 us (55%)
  Pallas kernels  40.8 us (27%)
  waiting for transfers between devices  20.4 us (14%)
  local copies, waits for them, and re-layouts  3 us (2%)
  other arithmetic  1.67 us (1%)
  between operations  1.55 us (1%)
    ppermute x14, starting transfers between devices, send(): lax.ppermute(now[1], 'col', inner)  50.8 us
    pallas_call x35, Pallas kernels, call(): pl.pallas_call(kernel, out_shape=out_shape, in_specs=specs, out_specs=[WH...  40.8 us
    ppermute x8, waiting for transfers between devices, halve(): lax.ppermute(other, 'col', [(i, i ^ 1 << bit) for i in range(count)])  13.6 us
    ppermute x14, starting transfers between devices, send(): lax.ppermute(now[0], 'col', outer)  10 us
    ppermute x3, starting transfers between devices, along_line(): before.append(lax.ppermute(before[-1], 'row', up))  8.31 us
    ppermute x8, starting transfers between devices, halve(): lax.ppermute(other, 'col', [(i, i ^ 1 << bit) for i in range(count)])  6.28 us
    ppermute x3, waiting for transfers between devices, along_line(): after.append(lax.ppermute(after[-1], 'row', down))  5.89 us
    ppermute x3, starting transfers between devices, along_line(): after.append(lax.ppermute(after[-1], 'row', down))  3.85 us
  transfers between devices with their start and end apart: 47, of which 8 were waited for; matrix products, arithmetic and copies ran while one was open for 1% of the time, Pallas kernels for 27%

profile of v3, /device:TPU:0, one launch (start us, length us, event | category | flops | bytes accessed | tf_op | source)
XLA Modules:
  0.0 150.5 jit_solution(13555838523912192410)
XLA Ops:
  4.3 4.9 %collective-permute-start.1 = (f32[384,768]{1,0:T(8,128)S(1)}, f32[384,768]{1,0:T(8,128)S(1)}, u32[]{:S(2)}, u32[]{:S(2)}) collective-permute-start(f32[384,768]{1,0:T(8,128)S(1)} %constant_dynamic-update-slice_fusion.refs_3_), channel_id=1, source_target_pairs={{0,8},{8,16},{16,24},{1,9},{9,17},{17,25},{2,10},{10,18},{18,26},{... | collective-permute-start | bytes 3538952 | tf_op jit(solution)/shard_map/ppermute | solution.py:220
  10.5 1.5 %collective-permute-start.8 = (f32[192,384]{1,0:T(8,128)S(1)}, f32[192,384]{1,0:T(8,128)S(1)}, u32[]{:S(2)}, u32[]{:S(2)}) collective-permute-start(f32[192,384]{1,0:T(8,128)S(1)} %get-tuple-element.51.rest_1_.rest_3_.rest_5_), channel_id=1, source_target_pairs={{0,1},{1,0},{2,3},{3,2},{4,5},{5,4},{6,7},{7,6},{8,9},{9,8},{10,11... | collective-permute-start | bytes 884744 | tf_op jit(solution)/shard_map/ppermute | solution.py:294
  12.7 2.9 %collective-permute-start.22 = (f32[192,384]{1,0:T(8,128)S(1)}, f32[192,384]{1,0:T(8,128)S(1)}, u32[]{:S(2)}, u32[]{:S(2)}) collective-permute-start(f32[192,384]{1,0:T(8,128)S(1)} %get-tuple-element.69.rest_1_.rest_3_.rest_5_), channel_id=1, source_target_pairs={{0,1},{1,0},{2,3},{3,2},{4,5},{5,4},{6,7},{7,6},{8,9},{9,8},{10,11... | collective-permute-start | bytes 884744 | tf_op jit(solution)/shard_map/ppermute | solution.py:294
  19.6 3.1 %collective-permute-start.10 = (f32[192,384]{1,0:T(8,128)S(1)}, f32[192,384]{1,0:T(8,128)S(1)}, u32[]{:S(2)}, u32[]{:S(2)}) collective-permute-start(f32[192,384]{1,0:T(8,128)S(1)} %get-tuple-element.57.rest_1_.rest_3_), channel_id=1, source_target_pairs={{0,1},{1,0},{2,3},{3,2},{4,5},{5,4},{6,7},{7,6},{8,9},{9,8},{10,11... | collective-permute-start | bytes 884744 | tf_op jit(solution)/shard_map/ppermute | solution.py:294
  25.3 5.0 %collective-permute-start.24 = (f32[192,384]{1,0:T(8,128)S(1)}, f32[192,384]{1,0:T(8,128)S(1)}, u32[]{:S(2)}, u32[]{:S(2)}) collective-permute-start(f32[192,384]{1,0:T(8,128)S(1)} %get-tuple-element.71.rest_1_.rest_3_), channel_id=1, source_target_pairs={{0,1},{1,0},{2,3},{3,2},{4,5},{5,4},{6,7},{7,6},{8,9},{9,8},{10,11... | collective-permute-start | bytes 884744 | tf_op jit(solution)/shard_map/ppermute | solution.py:294
  32.8 3.2 %collective-permute-start.12 = (f32[192,384]{1,0:T(8,128)S(1)}, f32[192,384]{1,0:T(8,128)S(1)}, u32[]{:S(2)}, u32[]{:S(2)}) collective-permute-start(f32[192,384]{1,0:T(8,128)S(1)} %get-tuple-element.59.rest_1_.rest_3_), channel_id=1, source_target_pairs={{0,1},{1,0},{2,3},{3,2},{4,5},{5,4},{6,7},{7,6},{8,9},{9,8},{10,11... | collective-permute-start | bytes 884744 | tf_op jit(solution)/shard_map/ppermute | solution.py:294
  39.7 3.3 %collective-permute-start.26 = (f32[192,384]{1,0:T(8,128)S(1)}, f32[192,384]{1,0:T(8,128)S(1)}, u32[]{:S(2)}, u32[]{:S(2)}) collective-permute-start(f32[192,384]{1,0:T(8,128)S(1)} %get-tuple-element.73.rest_1_.rest_3_), channel_id=1, source_target_pairs={{0,1},{1,0},{2,3},{3,2},{4,5},{5,4},{6,7},{7,6},{8,9},{9,8},{10,11... | collective-permute-start | bytes 884744 | tf_op jit(solution)/shard_map/ppermute | solution.py:294
  43.0 1.7 %collective-permute-start.2 = (f32[384,768]{1,0:T(8,128)S(1)}, f32[384,768]{1,0:T(8,128)}, u32[]{:S(2)}, u32[]{:S(2)}) collective-permute-start(f32[384,768]{1,0:T(8,128)S(1)} %collective-permute-done.1.refs_2_), channel_id=1, source_target_pairs={{8,16},{16,24},{9,17},{17,25},{10,18},{18,26},{11,19},{19,27},{12,... | collective-permute-start | bytes 3538952 | tf_op jit(solution)/shard_map/ppermute | solution.py:220
  47.6 3.4 %collective-permute-start.14 = (f32[192,384]{1,0:T(8,128)S(1)}, f32[192,384]{1,0:T(8,128)S(1)}, u32[]{:S(2)}, u32[]{:S(2)}) collective-permute-start(f32[192,384]{1,0:T(8,128)S(1)} %get-tuple-element.61.rest_1_.rest_3_), channel_id=1, source_target_pairs={{0,1},{1,0},{2,3},{3,2},{4,5},{5,4},{6,7},{7,6},{8,9},{9,8},{10,11... | collective-permute-start | bytes 884744 | tf_op jit(solution)/shard_map/ppermute | solution.py:294
  53.5 4.0 %collective-permute-start.28 = (f32[192,384]{1,0:T(8,128)S(1)}, f32[192,384]{1,0:T(8,128)S(1)}, u32[]{:S(2)}, u32[]{:S(2)}) collective-permute-start(f32[192,384]{1,0:T(8,128)S(1)} %get-tuple-element.75.rest_1_.rest_3_), channel_id=1, source_target_pairs={{0,1},{1,0},{2,3},{3,2},{4,5},{5,4},{6,7},{7,6},{8,9},{9,8},{10,11... | collective-permute-start | bytes 884744 | tf_op jit(solution)/shard_map/ppermute | solution.py:294
  61.2 4.1 %collective-permute-start.16 = (f32[192,384]{1,0:T(8,128)S(1)}, f32[192,384]{1,0:T(8,128)S(1)}, u32[]{:S(2)}, u32[]{:S(2)}) collective-permute-start(f32[192,384]{1,0:T(8,128)S(1)} %get-tuple-element.63.rest_1_.rest_3_), channel_id=1, source_target_pairs={{0,1},{1,0},{2,3},{3,2},{4,5},{5,4},{6,7},{7,6},{8,9},{9,8},{10,11... | collective-permute-start | bytes 884744 | tf_op jit(solution)/shard_map/ppermute | solution.py:294
  66.7 4.4 %collective-permute-start.30 = (f32[192,384]{1,0:T(8,128)S(1)}, f32[192,384]{1,0:T(8,128)S(1)}, u32[]{:S(2)}, u32[]{:S(2)}) collective-permute-start(f32[192,384]{1,0:T(8,128)S(1)} %get-tuple-element.77.rest_1_.rest_3_), channel_id=1, source_target_pairs={{0,1},{1,0},{2,3},{3,2},{4,5},{5,4},{6,7},{7,6},{8,9},{9,8},{10,11... | collective-permute-start | bytes 884744 | tf_op jit(solution)/shard_map/ppermute | solution.py:294
  73.6 4.1 %collective-permute-start.18 = (f32[192,384]{1,0:T(8,128)S(1)}, f32[192,384]{1,0:T(8,128)S(1)}, u32[]{:S(2)}, u32[]{:S(2)}) collective-permute-start(f32[192,384]{1,0:T(8,128)S(1)} %get-tuple-element.65.rest_1_), channel_id=1, source_target_pairs={{0,1},{1,0},{2,3},{3,2},{4,5},{5,4},{6,7},{7,6},{8,9},{9,8},{10,11... | collective-permute-start | bytes 884744 | tf_op jit(solution)/shard_map/ppermute | solution.py:294
  79.6 1.7 %collective-permute-start.3 = (f32[384,768]{1,0:T(8,128)}, f32[384,768]{1,0:T(8,128)}, u32[]{:S(2)}, u32[]{:S(2)}) collective-permute-start(f32[384,768]{1,0:T(8,128)} %collective-permute-done.2.refs_1_), channel_id=1, source_target_pairs={{16,24},{17,25},{18,26},{19,27},{20,28},{21,29},{22,30},{23,31}} | collective-permute-start | bytes 3538952 | tf_op jit(solution)/shard_map/ppermute | solution.py:220
  84.5 3.1 %collective-permute-start.32 = (f32[192,384]{1,0:T(8,128)S(1)}, f32[192,384]{1,0:T(8,128)S(1)}, u32[]{:S(2)}, u32[]{:S(2)}) collective-permute-start(f32[192,384]{1,0:T(8,128)S(1)} %get-tuple-element.79.rest_1_), channel_id=1, source_target_pairs={{0,1},{1,0},{2,3},{3,2},{4,5},{5,4},{6,7},{7,6},{8,9},{9,8},{10,11... | collective-permute-start | bytes 884744 | tf_op jit(solution)/shard_map/ppermute | solution.py:294
  90.4 3.9 %collective-permute-start.20 = (f32[192,384]{1,0:T(8,128)S(1)}, f32[192,384]{1,0:T(8,128)S(1)}, u32[]{:S(2)}, u32[]{:S(2)}) collective-permute-start(f32[192,384]{1,0:T(8,128)S(1)} %get-tuple-element.67.rest_1_), channel_id=1, source_target_pairs={{0,1},{1,0},{2,3},{3,2},{4,5},{5,4},{6,7},{7,6},{8,9},{9,8},{10,11... | collective-permute-start | bytes 884744 | tf_op jit(solution)/shard_map/ppermute | solution.py:294
  95.7 4.9 %collective-permute-start.34 = (f32[192,384]{1,0:T(8,128)S(1)}, f32[192,384]{1,0:T(8,128)S(1)}, u32[]{:S(2)}, u32[]{:S(2)}) collective-permute-start(f32[192,384]{1,0:T(8,128)S(1)} %get-tuple-element.81.rest_1_.rest_3_), channel_id=1, source_target_pairs={{0,1},{1,0},{2,3},{3,2},{4,5},{5,4},{6,7},{7,6},{8,9},{9,8},{10,11... | collective-permute-start | bytes 884744 | tf_op jit(solution)/shard_map/ppermute | solution.py:294
  102.8 1.5 %tail.20.rest_0_ = f32[192,768]{1,0:T(8,128)} custom-call(f32[192,768]{1,0:T(8,128)S(1)} %base.20, f32[192,384]{1,0:T(8,128)S(1)} %collective-permute-done.19.got_far, f32[192,384]{1,0:T(8,128)S(1)} %collective-permute-done.20.got_near.rest_1_, bf16[384,384]{1,0:T(8,128)(2,1)S(1)} %get-tuple-element.52.fh, bf16[384,384]{1,0:T(8,128)(2,1)S(1)} %get-tuple-element.53.fl, ...), custom_call_target="tpu_custom_call" | custom-call | flops 339738624 | bytes 2949120 | tf_op jit(solution)/shard_map/tail/pallas_call | solution.py:26
  104.4 1.5 %tail.27.rest_1_ = f32[192,768]{1,0:T(8,128)} custom-call(f32[192,768]{1,0:T(8,128)S(1)} %base.27, f32[192,384]{1,0:T(8,128)S(1)} %collective-permute-done.33.got_far, f32[192,384]{1,0:T(8,128)S(1)} %collective-permute-done.34.got_near.rest_3_, bf16[384,384]{1,0:T(8,128)(2,1)S(1)} %get-tuple-element.52.fh, bf16[384,384]{1,0:T(8,128)(2,1)S(1)} %get-tuple-element.53.fl, ...), custom_call_target="tpu_custom_call" | custom-call | flops 339738624 | bytes 2949120 | tf_op jit(solution)/shard_map/tail/pallas_call | solution.py:26
  105.9 2.8 %collective-permute-start.36 = (f32[192,768]{1,0:T(8,128)}, f32[192,768]{1,0:T(8,128)}, u32[]{:S(2)}, u32[]{:S(2)}) collective-permute-start(f32[192,768]{1,0:T(8,128)} %tail.27.rest_1_), channel_id=1, source_target_pairs={{0,1},{1,0},{2,3},{3,2},{4,5},{5,4},{6,7},{7,6},{8,9},{9,8},{10,11... | collective-permute-start | bytes 1769480 | tf_op jit(solution)/shard_map/ppermute | solution.py:314
  109.2 5.9 %collective-permute-done.6.refs_6_ = f32[384,768]{1,0:T(8,128)} collective-permute-done((f32[384,768]{1,0:T(8,128)}, f32[384,768]{1,0:T(8,128)}, u32[]{:S(2)}, u32[]{:S(2)}) %collective-permute-start.6) | collective-permute-done | bytes 1179680 | tf_op jit(solution)/shard_map/ppermute | solution.py:221
  116.4 3.1 %assemble.1 = (bf16[768,768]{1,0:T(8,128)(2,1)S(1)}, bf16[768,768]{1,0:T(8,128)(2,1)S(1)}, bf16[768,768]{1,0:T(8,128)(2,1)S(1)}, bf16[768,768]{1,0:T(8,128)(2,1)S(1)}) custom-call(s32[1]{0:T(128)} %bitcast.place_ref, f32[384,768]{1,0:T(8,128)} %collective-permute-done.3.refs_0_, f32[384,768]{1,0:T(8,128)} %collective-permute-done.2.refs_1_, ...), custom_call_target="tpu_custom_call" | custom-call | bytes 12976132 | tf_op jit(solution)/shard_map/assemble/pallas_call | solution.py:26
  119.5 2.8 %own_product.2.acc_ref = f32[384,768]{1,0:T(8,128)S(1)} custom-call(bf16[768,768]{1,0:T(8,128)(2,1)S(1)} %get-tuple-element.46.high_ref, bf16[768,768]{1,0:T(8,128)(2,1)S(1)} %get-tuple-element.47.low_ref, f32[192,768]{1,0:T(8,128)} %tail.20.rest_0_, f32[192,768]{1,0:T(8,128)} %tail.27.rest_1_), custom_call_target="tpu_custom_call" | custom-call | flops 1358954496 | bytes 4718592 | tf_op jit(solution)/shard_map/own_product/pallas_call | solution.py:26
  122.3 2.8 %other_product.2 = f32[768,384]{1,0:T(8,128)S(1)} custom-call(bf16[768,768]{1,0:T(8,128)(2,1)S(1)} %get-tuple-element.44.high_ref, bf16[768,768]{1,0:T(8,128)(2,1)S(1)} %get-tuple-element.45.low_ref, f32[384,768]{1,0:T(8,128)S(1)} %own_product.2.acc_ref, f32[192,768]{1,0:T(8,128)S(1)} %collective-permute-done.35.rest_0_, ...), custom_call_target="tpu_custom_call" | custom-call | flops 1358954496 | bytes 5898240 | tf_op jit(solution)/shard_map/other_product/pallas_call | solution.py:26
  125.2 2.4 %collective-permute-start.39 = (f32[2,96,384]{2,1,0:T(8,128)S(1)}, f32[2,96,384]{2,1,0:T(8,128)S(1)}, u32[]{:S(2)}, u32[]{:S(2)}) collective-permute-start(f32[2,96,384]{2,1,0:T(8,128)S(1)} %dynamic-slice_bitcast_fusion.2), channel_id=1, source_target_pairs={{0,4},{1,5},{2,6},{3,7},{4,0},{5,1},{6,2},{7,3},{8,12},{9,13},{10,... | collective-permute-start | bytes 884744 | tf_op jit(solution)/shard_map/ppermute | solution.py:259
  127.8 1.5 %own_product.3.acc_ref = f32[384,768]{1,0:T(8,128)S(1)} custom-call(bf16[768,768]{1,0:T(8,128)(2,1)S(1)} %get-tuple-element.46.high_ref, bf16[768,768]{1,0:T(8,128)(2,1)S(1)} %get-tuple-element.47.low_ref, f32[192,384]{1,0:T(8,128)S(1)} %copy-done.5, f32[192,384]{1,0:T(8,128)S(1)} %copy-done.7, f32[192,384]{1,0:T(8,128)S(1)} %copy-done.9, ...), custom_call_target="tpu_custom_call" | custom-call | flops 1358954496 | bytes 4718592 | tf_op jit(solution)/shard_map/own_product/pallas_call | solution.py:26
  129.4 1.7 %other_product.3 = f32[768,384]{1,0:T(8,128)S(1)} custom-call(bf16[768,768]{1,0:T(8,128)(2,1)S(1)} %get-tuple-element.44.high_ref, bf16[768,768]{1,0:T(8,128)(2,1)S(1)} %get-tuple-element.45.low_ref, f32[384,768]{1,0:T(8,128)S(1)} %own_product.3.acc_ref, f32[192,384]{1,0:T(8,128)S(1)} %collective-permute-done.41.rest_0_, ...), custom_call_target="tpu_custom_call" | custom-call | flops 1358954496 | bytes 5898240 | tf_op jit(solution)/shard_map/other_product/pallas_call | solution.py:26
  133.4 2.1 %collective-permute-done.39 = f32[2,96,384]{2,1,0:T(8,128)S(1)} collective-permute-done((f32[2,96,384]{2,1,0:T(8,128)S(1)}, f32[2,96,384]{2,1,0:T(8,128)S(1)}, u32[]{:S(2)}, u32[]{:S(2)}) %collective-permute-start.39) | collective-permute-done | bytes 294944 | tf_op jit(solution)/shard_map/ppermute | solution.py:259
  135.6 2.0 %collective-permute-done.37 = f32[2,96,384]{2,1,0:T(8,128)S(1)} collective-permute-done((f32[2,96,384]{2,1,0:T(8,128)S(1)}, f32[2,96,384]{2,1,0:T(8,128)S(1)}, u32[]{:S(2)}, u32[]{:S(2)}) %collective-permute-start.37) | collective-permute-done | bytes 294944 | tf_op jit(solution)/shard_map/ppermute | solution.py:259
  137.8 4.0 %collective-permute-done.45 = f32[2,96,384]{2,1,0:T(8,128)S(1)} collective-permute-done((f32[2,96,384]{2,1,0:T(8,128)S(1)}, f32[2,96,384]{2,1,0:T(8,128)S(1)}, u32[]{:S(2)}, u32[]{:S(2)}) %collective-permute-start.45) | collective-permute-done | bytes 294944 | tf_op jit(solution)/shard_map/ppermute | solution.py:259
  144.2 3.0 %collective-permute-done.40 = f32[96,384]{1,0:T(8,128)S(1)} collective-permute-done((f32[96,384]{1,0:T(8,128)S(1)}, f32[96,384]{1,0:T(8,128)S(1)}, u32[]{:S(2)}, u32[]{:S(2)}) %collective-permute-start.40) | collective-permute-done | bytes 147488 | tf_op jit(solution)/shard_map/ppermute | solution.py:259
  147.2 1.7 %collective-permute-done.46 = f32[96,384]{1,0:T(8,128)S(1)} collective-permute-done((f32[96,384]{1,0:T(8,128)S(1)}, f32[96,384]{1,0:T(8,128)S(1)}, u32[]{:S(2)}, u32[]{:S(2)}) %collective-permute-start.46) | collective-permute-done | bytes 147488 | tf_op jit(solution)/shard_map/ppermute | solution.py:259
  (145 shorter events, 50.9 us)
Async XLA Ops:
  2.6 10.1 %collective-permute-start.7 = (f32[192,384]{1,0:T(8,128)S(1)}, f32[192,384]{1,0:T(8,128)S(1)}, u32[]{:S(2)}, u32[]{:S(2)}) collective-permute-start(f32[192,384]{1,0:T(8,128)S(1)} %get-tuple-element.50.rest_0_.rest_2_.rest_4_), channel_id=1, source_target_pairs={{1,2},{3,4},{5,6},{2,1},{4,3},{6,5},{9,10},{11,12},{13,14},{10,9},... | collective-permute-start | bytes 884744 | tf_op jit(solution)/shard_map/ppermute | solution.py:294
  4.3 38.7 %collective-permute-start.1 = (f32[384,768]{1,0:T(8,128)S(1)}, f32[384,768]{1,0:T(8,128)S(1)}, u32[]{:S(2)}, u32[]{:S(2)}) collective-permute-start(f32[384,768]{1,0:T(8,128)S(1)} %constant_dynamic-update-slice_fusion.refs_3_), channel_id=1, source_target_pairs={{0,8},{8,16},{16,24},{1,9},{9,17},{17,25},{2,10},{10,18},{18,26},{... | collective-permute-start | bytes 3538952 | tf_op jit(solution)/shard_map/ppermute | solution.py:220
  9.2 35.5 %collective-permute-start.4 = (f32[384,768]{1,0:T(8,128)S(1)}, f32[384,768]{1,0:T(8,128)S(1)}, u32[]{:S(2)}, u32[]{:S(2)}) collective-permute-start(f32[384,768]{1,0:T(8,128)S(1)} %constant_dynamic-update-slice_fusion.refs_3_), channel_id=1, source_target_pairs={{24,16},{16,8},{8,0},{25,17},{17,9},{9,1},{26,18},{18,10},{10,2},{... | collective-permute-start | bytes 3538952 | tf_op jit(solution)/shard_map/ppermute | solution.py:221
  12.7 11.1 %collective-permute-start.22 = (f32[192,384]{1,0:T(8,128)S(1)}, f32[192,384]{1,0:T(8,128)S(1)}, u32[]{:S(2)}, u32[]{:S(2)}) collective-permute-start(f32[192,384]{1,0:T(8,128)S(1)} %get-tuple-element.69.rest_1_.rest_3_.rest_5_), channel_id=1, source_target_pairs={{0,1},{1,0},{2,3},{3,2},{4,5},{5,4},{6,7},{7,6},{8,9},{9,8},{10,11... | collective-permute-start | bytes 884744 | tf_op jit(solution)/shard_map/ppermute | solution.py:294
  19.6 11.7 %collective-permute-start.10 = (f32[192,384]{1,0:T(8,128)S(1)}, f32[192,384]{1,0:T(8,128)S(1)}, u32[]{:S(2)}, u32[]{:S(2)}) collective-permute-start(f32[192,384]{1,0:T(8,128)S(1)} %get-tuple-element.57.rest_1_.rest_3_), channel_id=1, source_target_pairs={{0,1},{1,0},{2,3},{3,2},{4,5},{5,4},{6,7},{7,6},{8,9},{9,8},{10,11... | collective-permute-start | bytes 884744 | tf_op jit(solution)/shard_map/ppermute | solution.py:294
  25.3 11.9 %collective-permute-start.24 = (f32[192,384]{1,0:T(8,128)S(1)}, f32[192,384]{1,0:T(8,128)S(1)}, u32[]{:S(2)}, u32[]{:S(2)}) collective-permute-start(f32[192,384]{1,0:T(8,128)S(1)} %get-tuple-element.71.rest_1_.rest_3_), channel_id=1, source_target_pairs={{0,1},{1,0},{2,3},{3,2},{4,5},{5,4},{6,7},{7,6},{8,9},{9,8},{10,11... | collective-permute-start | bytes 884744 | tf_op jit(solution)/shard_map/ppermute | solution.py:294
  32.8 13.2 %collective-permute-start.12 = (f32[192,384]{1,0:T(8,128)S(1)}, f32[192,384]{1,0:T(8,128)S(1)}, u32[]{:S(2)}, u32[]{:S(2)}) collective-permute-start(f32[192,384]{1,0:T(8,128)S(1)} %get-tuple-element.59.rest_1_.rest_3_), channel_id=1, source_target_pairs={{0,1},{1,0},{2,3},{3,2},{4,5},{5,4},{6,7},{7,6},{8,9},{9,8},{10,11... | collective-permute-start | bytes 884744 | tf_op jit(solution)/shard_map/ppermute | solution.py:294
  37.9 9.7 %collective-permute-start.25 = (f32[192,384]{1,0:T(8,128)S(1)}, f32[192,384]{1,0:T(8,128)S(1)}, u32[]{:S(2)}, u32[]{:S(2)}) collective-permute-start(f32[192,384]{1,0:T(8,128)S(1)} %get-tuple-element.72.rest_0_.rest_2_), channel_id=1, source_target_pairs={{1,2},{3,4},{5,6},{2,1},{4,3},{6,5},{9,10},{11,12},{13,14},{10,9},... | collective-permute-start | bytes 884744 | tf_op jit(solution)/shard_map/ppermute | solution.py:294
  39.7 12.4 %collective-permute-start.26 = (f32[192,384]{1,0:T(8,128)S(1)}, f32[192,384]{1,0:T(8,128)S(1)}, u32[]{:S(2)}, u32[]{:S(2)}) collective-permute-start(f32[192,384]{1,0:T(8,128)S(1)} %get-tuple-element.73.rest_1_.rest_3_), channel_id=1, source_target_pairs={{0,1},{1,0},{2,3},{3,2},{4,5},{5,4},{6,7},{7,6},{8,9},{9,8},{10,11... | collective-permute-start | bytes 884744 | tf_op jit(solution)/shard_map/ppermute | solution.py:294
  43.0 36.6 %collective-permute-start.2 = (f32[384,768]{1,0:T(8,128)S(1)}, f32[384,768]{1,0:T(8,128)}, u32[]{:S(2)}, u32[]{:S(2)}) collective-permute-start(f32[384,768]{1,0:T(8,128)S(1)} %collective-permute-done.1.refs_2_), channel_id=1, source_target_pairs={{8,16},{16,24},{9,17},{17,25},{10,18},{18,26},{11,19},{19,27},{12,... | collective-permute-start | bytes 3538952 | tf_op jit(solution)/shard_map/ppermute | solution.py:220
  44.7 36.6 %collective-permute-start.5 = (f32[384,768]{1,0:T(8,128)S(1)}, f32[384,768]{1,0:T(8,128)}, u32[]{:S(2)}, u32[]{:S(2)}) collective-permute-start(f32[384,768]{1,0:T(8,128)S(1)} %collective-permute-done.4.refs_4_), channel_id=1, source_target_pairs={{16,8},{8,0},{17,9},{9,1},{18,10},{10,2},{19,11},{11,3},{20,12},{1... | collective-permute-start | bytes 3538952 | tf_op jit(solution)/shard_map/ppermute | solution.py:221
  47.6 11.1 %collective-permute-start.14 = (f32[192,384]{1,0:T(8,128)S(1)}, f32[192,384]{1,0:T(8,128)S(1)}, u32[]{:S(2)}, u32[]{:S(2)}) collective-permute-start(f32[192,384]{1,0:T(8,128)S(1)} %get-tuple-element.61.rest_1_.rest_3_), channel_id=1, source_target_pairs={{0,1},{1,0},{2,3},{3,2},{4,5},{5,4},{6,7},{7,6},{8,9},{9,8},{10,11... | collective-permute-start | bytes 884744 | tf_op jit(solution)/shard_map/ppermute | solution.py:294
  53.5 11.8 %collective-permute-start.28 = (f32[192,384]{1,0:T(8,128)S(1)}, f32[192,384]{1,0:T(8,128)S(1)}, u32[]{:S(2)}, u32[]{:S(2)}) collective-permute-start(f32[192,384]{1,0:T(8,128)S(1)} %get-tuple-element.75.rest_1_.rest_3_), channel_id=1, source_target_pairs={{0,1},{1,0},{2,3},{3,2},{4,5},{5,4},{6,7},{7,6},{8,9},{9,8},{10,11... | collective-permute-start | bytes 884744 | tf_op jit(solution)/shard_map/ppermute | solution.py:294
  61.2 11.0 %collective-permute-start.16 = (f32[192,384]{1,0:T(8,128)S(1)}, f32[192,384]{1,0:T(8,128)S(1)}, u32[]{:S(2)}, u32[]{:S(2)}) collective-permute-start(f32[192,384]{1,0:T(8,128)S(1)} %get-tuple-element.63.rest_1_.rest_3_), channel_id=1, source_target_pairs={{0,1},{1,0},{2,3},{3,2},{4,5},{5,4},{6,7},{7,6},{8,9},{9,8},{10,11... | collective-permute-start | bytes 884744 | tf_op jit(solution)/shard_map/ppermute | solution.py:294
  66.7 12.1 %collective-permute-start.30 = (f32[192,384]{1,0:T(8,128)S(1)}, f32[192,384]{1,0:T(8,128)S(1)}, u32[]{:S(2)}, u32[]{:S(2)}) collective-permute-start(f32[192,384]{1,0:T(8,128)S(1)} %get-tuple-element.77.rest_1_.rest_3_), channel_id=1, source_target_pairs={{0,1},{1,0},{2,3},{3,2},{4,5},{5,4},{6,7},{7,6},{8,9},{9,8},{10,11... | collective-permute-start | bytes 884744 | tf_op jit(solution)/shard_map/ppermute | solution.py:294
  73.0 11.5 %collective-permute-start.17 = (f32[192,384]{1,0:T(8,128)S(1)}, f32[192,384]{1,0:T(8,128)S(1)}, u32[]{:S(2)}, u32[]{:S(2)}) collective-permute-start(f32[192,384]{1,0:T(8,128)S(1)} %get-tuple-element.64.rest_0_), channel_id=1, source_target_pairs={{1,2},{3,4},{5,6},{2,1},{4,3},{6,5},{9,10},{11,12},{13,14},{10,9},... | collective-permute-start | bytes 884744 | tf_op jit(solution)/shard_map/ppermute | solution.py:294
  73.6 13.9 %collective-permute-start.18 = (f32[192,384]{1,0:T(8,128)S(1)}, f32[192,384]{1,0:T(8,128)S(1)}, u32[]{:S(2)}, u32[]{:S(2)}) collective-permute-start(f32[192,384]{1,0:T(8,128)S(1)} %get-tuple-element.65.rest_1_), channel_id=1, source_target_pairs={{0,1},{1,0},{2,3},{3,2},{4,5},{5,4},{6,7},{7,6},{8,9},{9,8},{10,11... | collective-permute-start | bytes 884744 | tf_op jit(solution)/shard_map/ppermute | solution.py:294
  79.6 29.1 %collective-permute-start.3 = (f32[384,768]{1,0:T(8,128)}, f32[384,768]{1,0:T(8,128)}, u32[]{:S(2)}, u32[]{:S(2)}) collective-permute-start(f32[384,768]{1,0:T(8,128)} %collective-permute-done.2.refs_1_), channel_id=1, source_target_pairs={{16,24},{17,25},{18,26},{19,27},{20,28},{21,29},{22,30},{23,31}} | collective-permute-start | bytes 3538952 | tf_op jit(solution)/shard_map/ppermute | solution.py:220
  81.3 33.8 %collective-permute-start.6 = (f32[384,768]{1,0:T(8,128)}, f32[384,768]{1,0:T(8,128)}, u32[]{:S(2)}, u32[]{:S(2)}) collective-permute-start(f32[384,768]{1,0:T(8,128)} %collective-permute-done.5.refs_5_), channel_id=1, source_target_pairs={{8,0},{9,1},{10,2},{11,3},{12,4},{13,5},{14,6},{15,7}} | collective-permute-start | bytes 3538952 | tf_op jit(solution)/shard_map/ppermute | solution.py:221
  84.5 9.8 %collective-permute-start.32 = (f32[192,384]{1,0:T(8,128)S(1)}, f32[192,384]{1,0:T(8,128)S(1)}, u32[]{:S(2)}, u32[]{:S(2)}) collective-permute-start(f32[192,384]{1,0:T(8,128)S(1)} %get-tuple-element.79.rest_1_), channel_id=1, source_target_pairs={{0,1},{1,0},{2,3},{3,2},{4,5},{5,4},{6,7},{7,6},{8,9},{9,8},{10,11... | collective-permute-start | bytes 884744 | tf_op jit(solution)/shard_map/ppermute | solution.py:294
  90.4 12.4 %collective-permute-start.20 = (f32[192,384]{1,0:T(8,128)S(1)}, f32[192,384]{1,0:T(8,128)S(1)}, u32[]{:S(2)}, u32[]{:S(2)}) collective-permute-start(f32[192,384]{1,0:T(8,128)S(1)} %get-tuple-element.67.rest_1_), channel_id=1, source_target_pairs={{0,1},{1,0},{2,3},{3,2},{4,5},{5,4},{6,7},{7,6},{8,9},{9,8},{10,11... | collective-permute-start | bytes 884744 | tf_op jit(solution)/shard_map/ppermute | solution.py:294
  95.0 9.3 %collective-permute-start.33 = (f32[192,384]{1,0:T(8,128)S(1)}, f32[192,384]{1,0:T(8,128)S(1)}, u32[]{:S(2)}, u32[]{:S(2)}) collective-permute-start(f32[192,384]{1,0:T(8,128)S(1)} %get-tuple-element.80.rest_0_.rest_2_), channel_id=1, source_target_pairs={{1,2},{3,4},{5,6},{2,1},{4,3},{6,5},{9,10},{11,12},{13,14},{10,9},... | collective-permute-start | bytes 884744 | tf_op jit(solution)/shard_map/ppermute | solution.py:294
  104.3 17.9 %collective-permute-start.35 = (f32[192,768]{1,0:T(8,128)}, f32[192,768]{1,0:T(8,128)S(1)}, u32[]{:S(2)}, u32[]{:S(2)}) collective-permute-start(f32[192,768]{1,0:T(8,128)} %tail.20.rest_0_), channel_id=1, source_target_pairs={{0,1},{1,0},{2,3},{3,2},{4,5},{5,4},{6,7},{7,6},{8,9},{9,8},{10,11... | collective-permute-start | bytes 1769480 | tf_op jit(solution)/shard_map/ppermute | solution.py:314
  105.9 16.4 %collective-permute-start.36 = (f32[192,768]{1,0:T(8,128)}, f32[192,768]{1,0:T(8,128)}, u32[]{:S(2)}, u32[]{:S(2)}) collective-permute-start(f32[192,768]{1,0:T(8,128)} %tail.27.rest_1_), channel_id=1, source_target_pairs={{0,1},{1,0},{2,3},{3,2},{4,5},{5,4},{6,7},{7,6},{8,9},{9,8},{10,11... | collective-permute-start | bytes 1769480 | tf_op jit(solution)/shard_map/ppermute | solution.py:314
  108.7 20.7 %collective-permute-start.41 = (f32[192,384]{1,0:T(8,128)}, f32[192,384]{1,0:T(8,128)S(1)}, u32[]{:S(2)}, u32[]{:S(2)}) collective-permute-start(f32[192,384]{1,0:T(8,128)} %copy-done.4), channel_id=1, source_target_pairs={{0,1},{1,0},{2,3},{3,2},{4,5},{5,4},{6,7},{7,6},{8,9},{9,8},{10,11... | collective-permute-start | bytes 884744 | tf_op jit(solution)/shard_map/ppermute | solution.py:312
  108.7 20.7 %collective-permute-start.42 = (f32[192,384]{1,0:T(8,128)}, f32[192,384]{1,0:T(8,128)S(1)}, u32[]{:S(2)}, u32[]{:S(2)}) collective-permute-start(f32[192,384]{1,0:T(8,128)} %copy-done.8), channel_id=1, source_target_pairs={{0,1},{1,0},{2,3},{3,2},{4,5},{5,4},{6,7},{7,6},{8,9},{9,8},{10,11... | collective-permute-start | bytes 884744 | tf_op jit(solution)/shard_map/ppermute | solution.py:312
  125.2 10.3 %collective-permute-start.39 = (f32[2,96,384]{2,1,0:T(8,128)S(1)}, f32[2,96,384]{2,1,0:T(8,128)S(1)}, u32[]{:S(2)}, u32[]{:S(2)}) collective-permute-start(f32[2,96,384]{2,1,0:T(8,128)S(1)} %dynamic-slice_bitcast_fusion.2), channel_id=1, source_target_pairs={{0,4},{1,5},{2,6},{3,7},{4,0},{5,1},{6,2},{7,3},{8,12},{9,13},{10,... | collective-permute-start | bytes 884744 | tf_op jit(solution)/shard_map/ppermute | solution.py:259
  127.7 10.0 %collective-permute-start.37 = (f32[2,96,384]{2,1,0:T(8,128)S(1)}, f32[2,96,384]{2,1,0:T(8,128)S(1)}, u32[]{:S(2)}, u32[]{:S(2)}) collective-permute-start(f32[2,96,384]{2,1,0:T(8,128)S(1)} %dynamic-slice_bitcast_fusion.3), channel_id=1, source_target_pairs={{0,2},{1,3},{2,0},{3,1},{4,6},{5,7},{6,4},{7,5},{8,10},{9,11},{10,... | collective-permute-start | bytes 884744 | tf_op jit(solution)/shard_map/ppermute | solution.py:259
  131.2 10.6 %collective-permute-start.45 = (f32[2,96,384]{2,1,0:T(8,128)S(1)}, f32[2,96,384]{2,1,0:T(8,128)S(1)}, u32[]{:S(2)}, u32[]{:S(2)}) collective-permute-start(f32[2,96,384]{2,1,0:T(8,128)S(1)} %dynamic-slice_bitcast_fusion), channel_id=1, source_target_pairs={{0,4},{1,5},{2,6},{3,7},{4,0},{5,1},{6,2},{7,3},{8,12},{9,13},{10,... | collective-permute-start | bytes 884744 | tf_op jit(solution)/shard_map/ppermute | solution.py:259
  132.3 11.8 %collective-permute-start.43 = (f32[2,96,384]{2,1,0:T(8,128)S(1)}, f32[2,96,384]{2,1,0:T(8,128)S(1)}, u32[]{:S(2)}, u32[]{:S(2)}) collective-permute-start(f32[2,96,384]{2,1,0:T(8,128)S(1)} %dynamic-slice_bitcast_fusion.1), channel_id=1, source_target_pairs={{0,2},{1,3},{2,0},{3,1},{4,6},{5,7},{6,4},{7,5},{8,10},{9,11},{10,... | collective-permute-start | bytes 884744 | tf_op jit(solution)/shard_map/ppermute | solution.py:259
  135.6 11.6 %collective-permute-start.40 = (f32[96,384]{1,0:T(8,128)S(1)}, f32[96,384]{1,0:T(8,128)S(1)}, u32[]{:S(2)}, u32[]{:S(2)}) collective-permute-start(f32[96,384]{1,0:T(8,128)S(1)} %dynamic-slice_bitcast_fusion.6), channel_id=1, source_target_pairs={{0,2},{1,3},{2,0},{3,1},{4,6},{5,7},{6,4},{7,5},{8,10},{9,11},{10,... | collective-permute-start | bytes 442376 | tf_op jit(solution)/shard_map/ppermute | solution.py:259
  137.8 9.4 %collective-permute-start.38 = (f32[96,384]{1,0:T(8,128)S(1)}, f32[96,384]{1,0:T(8,128)S(1)}, u32[]{:S(2)}, u32[]{:S(2)}) collective-permute-start(f32[96,384]{1,0:T(8,128)S(1)} %dynamic-slice_bitcast_fusion.7), channel_id=1, source_target_pairs={{0,4},{1,5},{2,6},{3,7},{4,0},{5,1},{6,2},{7,3},{8,12},{9,13},{10,... | collective-permute-start | bytes 442376 | tf_op jit(solution)/shard_map/ppermute | solution.py:259
  (28 other events, 184.2 us)

commit v4 on v3

--- a/solution.py
+++ b/solution.py
@@ -167,8 +167,8 @@
 
 
 def assemble_kernel(count, place_ref, *refs):
-    shards = refs[: 2 * count - 1]
-    outs = refs[2 * count - 1 : -2]
+    shards = refs[: 2 * count - 3]
+    outs = refs[2 * count - 3 : -2]
     held, sems = refs[-2:]
     place = place_ref[0]
     rows, depth = shards[0].shape
@@ -184,17 +184,21 @@
             for side in range(2)
         ]
 
-    for plane in range(count):
-        for at in range(count):
-
-            @pl.when(place == at)
-            def _():
-                for copy in copies(plane, shards[plane - at + count - 1]):
-                    copy.start()
-
-    for plane in range(count):
-        for copy in copies(plane, shards[0]):
-            copy.wait()
+    for at in range(count):
+
+        @pl.when(place == at)
+        def _():
+            for plane in range(count):
+                if abs(plane - at) < count - 1:
+                    for copy in copies(plane, shards[plane - at + count - 2]):
+                        copy.start()
+                else:
+                    held[plane * half : (plane + 1) * half] = jnp.zeros((half, 2 * depth), jnp.float32)
+            for plane in range(count):
+                if abs(plane - at) < count - 1:
+                    for copy in copies(plane, shards[plane - at + count - 2]):
+                        copy.wait()
+
     step = 128
     for at in range(0, depth, step):
         for side in range(2):
@@ -202,13 +206,59 @@
             outs[2 * side][at : at + step], outs[2 * side + 1][at : at + step] = term
 
 
-def assemble(place, shards):
-    count = (len(shards) + 1) // 2
+def assemble(place, before, after):
+    count = len(before)
+    shards = before[count - 2 : 0 : -1] + after[: count - 1]
     rows, depth = shards[0].shape
     out = [bf16(depth, count * rows // 2)] * 4
     scratch = [pltpu.VMEM((count * rows // 2, 2 * depth), jnp.float32), pltpu.SemaphoreType.DMA((count, 2))]
     specs = [SCALARS] + [ANYWHERE] * len(shards)
     return call(functools.partial(assemble_kernel, count), out, [place] + shards, specs, "assemble", 24, 0, scratch)
+
+
+def late_kernel(before_ref, after_ref, *outs):
+    rows, depth = before_ref.shape
+    half = rows // 2
+    step = 128
+    for side in range(2):
+        here = slice(side * half, (side + 1) * half)
+        for at in range(0, depth, step):
+            columns = slice(at, at + step)
+            term = split((before_ref[here, columns] + after_ref[here, columns]).T)
+            outs[2 * side][columns], outs[2 * side + 1][columns] = term
+
+
+def assemble_late(before, after):
+    rows, depth = before[-1].shape
+    out = [bf16(depth, rows // 2)] * 4
+    return call(late_kernel, out, [before[-1], after[-1]], [WHOLE] * 2, "late", 16)
+
+
+def finish_kernel(count, place_ref, early_ref, own_h, own_l, other_h, other_l, *rest):
+    out_ref = rest[-1]
+    place = place_ref[0]
+    half = len(rest) // 2
+    value = dot3(split(joined(rest[:half])), (own_h[...], own_l[...]))
+    value = (value + dot3(split(joined(rest[half:-1])), (other_h[...], other_l[...]))).T
+    width = value.shape[0]
+    out_ref[...] = early_ref[...]
+
+    @pl.when(place == 0)
+    def _():
+        out_ref[(count - 1) * width :] = value
+
+    @pl.when(place == count - 1)
+    def _():
+        out_ref[:width] = value
+
+
+def finish(place, early, late, own, other):
+    depth, width = late[0].shape
+    count = early.shape[0] // width
+    arrays = [place, early, *late] + [half for part in own + other for half in part]
+    specs = [SCALARS] + [WHOLE] * (len(arrays) - 1)
+    flops = 12 * early.shape[1] * depth * width
+    return call(functools.partial(finish_kernel, count), f32(*early.shape), arrays, specs, "finish", 24, flops)
 
 
 def along_line(payload):
@@ -219,7 +269,7 @@
         down = [(count - 1 - a, count - 1 - b) for a, b in up]
         before.append(lax.ppermute(before[-1], "row", up))
         after.append(lax.ppermute(after[-1], "row", down))
-    return before[:0:-1] + after
+    return before, after
 
 
 def first_product_kernel(high_ref, low_ref, *rest):
@@ -286,9 +336,9 @@
 
     mine, theirs, start = arrange(odd, vectors, width)
     weights = make_weights(odd, coupling, hblocks)
-    everything = assemble(
-        place, along_line(jnp.concatenate([mine, lax.ppermute(theirs, "col", inner)], axis=0))
-    )
+    before, after = along_line(jnp.concatenate([mine, lax.ppermute(theirs, "col", inner)], axis=0))
+    everything = assemble(place, before, after)
+    late = assemble_late(before, after)
 
     def send(now):
         return [lax.ppermute(now[0], "col", outer), lax.ppermute(now[1], "col", inner)]
@@ -310,9 +360,11 @@
     filtered = [field[-2] for field in fields]
     image = [field[-1] for field in fields]
     other = [[lax.ppermute(filtered[p][0], "col", inner), got[p][1]] for p in range(PARTS)]
-    intersection = reduce_chips(product(everything, filtered, other))
-    other = [[lax.ppermute(image[p][0], "col", inner)] for p in range(PARTS)]
-    projected_ham = reduce_chips(product(everything, image, other))
+    sums = product(everything, filtered, other)
+    other_image = [[lax.ppermute(image[p][0], "col", inner)] for p in range(PARTS)]
+    image_sums = product(everything, image, other_image)
+    intersection = reduce_chips(finish(place, sums, late, filtered, other))
+    projected_ham = reduce_chips(finish(place, image_sums, late, image, other_image))
     return projected_ham, intersection
 
 

time: 151 us -> 180 us (1.19)
  the two profiles are of different devices: /device:TPU:0 before, /device:TPU:8 now
where the time goes in v4:
time: 180 us; the launch traced here: 177 us
  starting transfers between devices  103 us (57%)
  Pallas kernels  49.4 us (27%)
  waiting for transfers between devices  16.7 us (9%)
  local copies, waits for them, and re-layouts  4.99 us (3%)
    ppermute x14, starting transfers between devices, send(): lax.ppermute(now[1], 'col', inner)  50 us
    pallas_call x38, Pallas kernels, call(): pl.pallas_call(kernel, out_shape=out_shape, in_specs=specs, out_specs=[WH...  49.4 us
    ppermute x3, starting transfers between devices, along_line(): before.append(lax.ppermute(before[-1], 'row', up))  21.9 us
    ppermute x8, waiting for transfers between devices, halve(): lax.ppermute(other, 'col', [(i, i ^ 1 << bit) for i in range(count)])  16.6 us
    ppermute x14, starting transfers between devices, send(): lax.ppermute(now[0], 'col', outer)  9.63 us
    ppermute x3, starting transfers between devices, along_line(): after.append(lax.ppermute(after[-1], 'row', down))  7.12 us
    ppermute x8, starting transfers between devices, halve(): lax.ppermute(other, 'col', [(i, i ^ 1 << bit) for i in range(count)])  6.04 us
    ppermute x2, starting transfers between devices, per_device(): lax.ppermute(filtered[p][0], 'col', inner)  4.91 us
  transfers between devices with their start and end apart: 47, of which 6 were waited for; matrix products, arithmetic and copies ran while one was open for 1% of the time, Pallas kernels for 24%

profile of v4, /device:TPU:8, one launch (start us, length us, event | category | flops | bytes accessed | tf_op | source)
XLA Modules:
  0.0 177.1 jit_solution(15485900619309522286)
XLA Ops:
  3.0 2.9 %collective-permute-start.6 = (f32[192,384]{1,0:T(8,128)S(1)}, f32[192,384]{1,0:T(8,128)S(1)}, u32[]{:S(2)}, u32[]{:S(2)}) collective-permute-start(f32[192,384]{1,0:T(8,128)S(1)} %get-tuple-element.55.rest_1_.rest_3_.rest_5_), channel_id=1, source_target_pairs={{0,1},{1,0},{2,3},{3,2},{4,5},{5,4},{6,7},{7,6},{8,9},{9,8},{10,11... | collective-permute-start | bytes 884744 | tf_op jit(solution)/shard_map/ppermute | solution.py:344
  6.0 2.4 %collective-permute-start.3 = (f32[384,768]{1,0:T(8,128)S(1)}, f32[384,768]{1,0:T(8,128)S(1)}, u32[]{:S(2)}, u32[]{:S(2)}) collective-permute-start(f32[384,768]{1,0:T(8,128)S(1)} %constant_dynamic-update-slice_fusion.refs_2_), channel_id=1, source_target_pairs={{24,16},{16,8},{8,0},{25,17},{17,9},{9,1},{26,18},{18,10},{10,2},{... | collective-permute-start | bytes 3538952 | tf_op jit(solution)/shard_map/ppermute | solution.py:271
  8.3 3.5 %collective-permute-start.1 = (f32[384,768]{1,0:T(8,128)S(1)}, f32[384,768]{1,0:T(8,128)S(1)}, u32[]{:S(2)}, u32[]{:S(2)}) collective-permute-start(f32[384,768]{1,0:T(8,128)S(1)} %constant_dynamic-update-slice_fusion.refs_2_), channel_id=1, source_target_pairs={{0,8},{8,16},{16,24},{1,9},{9,17},{17,25},{2,10},{10,18},{18,26},{... | collective-permute-start | bytes 3538952 | tf_op jit(solution)/shard_map/ppermute | solution.py:270
  12.5 2.9 %collective-permute-start.20 = (f32[192,384]{1,0:T(8,128)S(1)}, f32[192,384]{1,0:T(8,128)S(1)}, u32[]{:S(2)}, u32[]{:S(2)}) collective-permute-start(f32[192,384]{1,0:T(8,128)S(1)} %get-tuple-element.73.rest_1_.rest_3_.rest_5_), channel_id=1, source_target_pairs={{0,1},{1,0},{2,3},{3,2},{4,5},{5,4},{6,7},{7,6},{8,9},{9,8},{10,11... | collective-permute-start | bytes 884744 | tf_op jit(solution)/shard_map/ppermute | solution.py:344
  20.6 2.9 %collective-permute-start.8 = (f32[192,384]{1,0:T(8,128)S(1)}, f32[192,384]{1,0:T(8,128)S(1)}, u32[]{:S(2)}, u32[]{:S(2)}) collective-permute-start(f32[192,384]{1,0:T(8,128)S(1)} %get-tuple-element.61.rest_1_.rest_3_), channel_id=1, source_target_pairs={{0,1},{1,0},{2,3},{3,2},{4,5},{5,4},{6,7},{7,6},{8,9},{9,8},{10,11... | collective-permute-start | bytes 884744 | tf_op jit(solution)/shard_map/ppermute | solution.py:344
  24.9 5.3 %collective-permute-start.22 = (f32[192,384]{1,0:T(8,128)S(1)}, f32[192,384]{1,0:T(8,128)S(1)}, u32[]{:S(2)}, u32[]{:S(2)}) collective-permute-start(f32[192,384]{1,0:T(8,128)S(1)} %get-tuple-element.75.rest_1_.rest_3_), channel_id=1, source_target_pairs={{0,1},{1,0},{2,3},{3,2},{4,5},{5,4},{6,7},{7,6},{8,9},{9,8},{10,11... | collective-permute-start | bytes 884744 | tf_op jit(solution)/shard_map/ppermute | solution.py:344
  32.8 3.5 %collective-permute-start.10 = (f32[192,384]{1,0:T(8,128)S(1)}, f32[192,384]{1,0:T(8,128)S(1)}, u32[]{:S(2)}, u32[]{:S(2)}) collective-permute-start(f32[192,384]{1,0:T(8,128)S(1)} %get-tuple-element.63.rest_1_.rest_3_), channel_id=1, source_target_pairs={{0,1},{1,0},{2,3},{3,2},{4,5},{5,4},{6,7},{7,6},{8,9},{9,8},{10,11... | collective-permute-start | bytes 884744 | tf_op jit(solution)/shard_map/ppermute | solution.py:344
  40.1 3.2 %collective-permute-start.24 = (f32[192,384]{1,0:T(8,128)S(1)}, f32[192,384]{1,0:T(8,128)S(1)}, u32[]{:S(2)}, u32[]{:S(2)}) collective-permute-start(f32[192,384]{1,0:T(8,128)S(1)} %get-tuple-element.77.rest_1_.rest_3_), channel_id=1, source_target_pairs={{0,1},{1,0},{2,3},{3,2},{4,5},{5,4},{6,7},{7,6},{8,9},{9,8},{10,11... | collective-permute-start | bytes 884744 | tf_op jit(solution)/shard_map/ppermute | solution.py:344
  44.7 4.7 %collective-permute-start.12 = (f32[192,384]{1,0:T(8,128)S(1)}, f32[192,384]{1,0:T(8,128)S(1)}, u32[]{:S(2)}, u32[]{:S(2)}) collective-permute-start(f32[192,384]{1,0:T(8,128)S(1)} %get-tuple-element.65.rest_1_.rest_3_), channel_id=1, source_target_pairs={{0,1},{1,0},{2,3},{3,2},{4,5},{5,4},{6,7},{7,6},{8,9},{9,8},{10,11... | collective-permute-start | bytes 884744 | tf_op jit(solution)/shard_map/ppermute | solution.py:344
  49.5 2.4 %collective-permute-start.4 = (f32[384,768]{1,0:T(8,128)S(1)}, f32[384,768]{1,0:T(8,128)}, u32[]{:S(2)}, u32[]{:S(2)}) collective-permute-start(f32[384,768]{1,0:T(8,128)S(1)} %collective-permute-done.3.refs_3_), channel_id=1, source_target_pairs={{16,8},{8,0},{17,9},{9,1},{18,10},{10,2},{19,11},{11,3},{20,12},{1... | collective-permute-start | bytes 3538952 | tf_op jit(solution)/shard_map/ppermute | solution.py:271
  51.9 5.7 %collective-permute-start.2 = (f32[384,768]{1,0:T(8,128)S(1)}, f32[384,768]{1,0:T(8,128)}, u32[]{:S(2)}, u32[]{:S(2)}) collective-permute-start(f32[384,768]{1,0:T(8,128)S(1)} %collective-permute-done.1.refs_1_), channel_id=1, source_target_pairs={{8,16},{16,24},{9,17},{17,25},{10,18},{18,26},{11,19},{19,27},{12,... | collective-permute-start | bytes 3538952 | tf_op jit(solution)/shard_map/ppermute | solution.py:270
  60.2 2.2 %collective-permute-start.26 = (f32[192,384]{1,0:T(8,128)S(1)}, f32[192,384]{1,0:T(8,128)S(1)}, u32[]{:S(2)}, u32[]{:S(2)}) collective-permute-start(f32[192,384]{1,0:T(8,128)S(1)} %get-tuple-element.79.rest_1_.rest_3_), channel_id=1, source_target_pairs={{0,1},{1,0},{2,3},{3,2},{4,5},{5,4},{6,7},{7,6},{8,9},{9,8},{10,11... | collective-permute-start | bytes 884744 | tf_op jit(solution)/shard_map/ppermute | solution.py:344
  66.1 4.2 %collective-permute-start.14 = (f32[192,384]{1,0:T(8,128)S(1)}, f32[192,384]{1,0:T(8,128)S(1)}, u32[]{:S(2)}, u32[]{:S(2)}) collective-permute-start(f32[192,384]{1,0:T(8,128)S(1)} %get-tuple-element.67.rest_1_.rest_3_), channel_id=1, source_target_pairs={{0,1},{1,0},{2,3},{3,2},{4,5},{5,4},{6,7},{7,6},{8,9},{9,8},{10,11... | collective-permute-start | bytes 884744 | tf_op jit(solution)/shard_map/ppermute | solution.py:344
  71.8 5.1 %collective-permute-start.28 = (f32[192,384]{1,0:T(8,128)S(1)}, f32[192,384]{1,0:T(8,128)S(1)}, u32[]{:S(2)}, u32[]{:S(2)}) collective-permute-start(f32[192,384]{1,0:T(8,128)S(1)} %get-tuple-element.81.rest_1_.rest_3_), channel_id=1, source_target_pairs={{0,1},{1,0},{2,3},{3,2},{4,5},{5,4},{6,7},{7,6},{8,9},{9,8},{10,11... | collective-permute-start | bytes 884744 | tf_op jit(solution)/shard_map/ppermute | solution.py:344
  79.5 3.7 %collective-permute-start.16 = (f32[192,384]{1,0:T(8,128)S(1)}, f32[192,384]{1,0:T(8,128)S(1)}, u32[]{:S(2)}, u32[]{:S(2)}) collective-permute-start(f32[192,384]{1,0:T(8,128)S(1)} %get-tuple-element.69.rest_1_), channel_id=1, source_target_pairs={{0,1},{1,0},{2,3},{3,2},{4,5},{5,4},{6,7},{7,6},{8,9},{9,8},{10,11... | collective-permute-start | bytes 884744 | tf_op jit(solution)/shard_map/ppermute | solution.py:344
  87.1 3.2 %collective-permute-start.30 = (f32[192,384]{1,0:T(8,128)S(1)}, f32[192,384]{1,0:T(8,128)S(1)}, u32[]{:S(2)}, u32[]{:S(2)}) collective-permute-start(f32[192,384]{1,0:T(8,128)S(1)} %get-tuple-element.83.rest_1_), channel_id=1, source_target_pairs={{0,1},{1,0},{2,3},{3,2},{4,5},{5,4},{6,7},{7,6},{8,9},{9,8},{10,11... | collective-permute-start | bytes 884744 | tf_op jit(solution)/shard_map/ppermute | solution.py:344
  92.3 2.4 %collective-permute-start.36 = (f32[384,768]{1,0:T(8,128)}, f32[384,768]{1,0:T(8,128)}, u32[]{:S(2)}, u32[]{:S(2)}) collective-permute-start(f32[384,768]{1,0:T(8,128)} %collective-permute-done.4.refs_4_), channel_id=1, source_target_pairs={{8,0},{9,1},{10,2},{11,3},{12,4},{13,5},{14,6},{15,7}} | collective-permute-start | bytes 3538952 | tf_op jit(solution)/shard_map/ppermute | solution.py:271
  94.6 12.7 %collective-permute-start.35 = (f32[384,768]{1,0:T(8,128)}, f32[384,768]{1,0:T(8,128)}, u32[]{:S(2)}, u32[]{:S(2)}) collective-permute-start(f32[384,768]{1,0:T(8,128)} %collective-permute-done.2.refs_0_), channel_id=1, source_target_pairs={{16,24},{17,25},{18,26},{19,27},{20,28},{21,29},{22,30},{23,31}} | collective-permute-start | bytes 3538952 | tf_op jit(solution)/shard_map/ppermute | solution.py:270
  109.4 6.1 %collective-permute-start.32 = (f32[192,384]{1,0:T(8,128)S(1)}, f32[192,384]{1,0:T(8,128)S(1)}, u32[]{:S(2)}, u32[]{:S(2)}) collective-permute-start(f32[192,384]{1,0:T(8,128)S(1)} %get-tuple-element.85.rest_1_.rest_3_), channel_id=1, source_target_pairs={{0,1},{1,0},{2,3},{3,2},{4,5},{5,4},{6,7},{7,6},{8,9},{9,8},{10,11... | collective-permute-start | bytes 884744 | tf_op jit(solution)/shard_map/ppermute | solution.py:344
  116.1 4.9 %collective-permute-start.42 = (f32[192,384]{1,0:T(8,128)S(1)}, f32[192,384]{1,0:T(8,128)S(1)}, u32[]{:S(2)}, u32[]{:S(2)}) collective-permute-start(f32[192,384]{1,0:T(8,128)S(1)} %get-tuple-element.84.rest_0_.rest_2_), channel_id=1, source_target_pairs={{0,1},{1,0},{2,3},{3,2},{4,5},{5,4},{6,7},{7,6},{8,9},{9,8},{10,11... | collective-permute-start | bytes 884744 | tf_op jit(solution)/shard_map/ppermute | solution.py:362
  122.2 2.1 %base.20 = f32[192,768]{1,0:T(8,128)S(1)} custom-call(bf16[768,768]{1,0:T(8,128)(2,1)S(1)} %get-tuple-element.52.high_ref, bf16[768,768]{1,0:T(8,128)(2,1)S(1)} %get-tuple-element.53.low_ref, f32[192,384]{1,0:T(8,128)} %get-tuple-element.70.rest_0_, f32[192,384]{1,0:T(8,128)S(1)} %get-tuple-element.71.rest_1_), custom_call_target="tpu_custom_call" | custom-call | flops 679477248 | bytes 3538944 | tf_op jit(solution)/shard_map/base/pallas_call | solution.py:26
  126.7 2.8 %collective-permute-start.34 = (f32[192,768]{1,0:T(8,128)}, f32[192,768]{1,0:T(8,128)S(1)}, u32[]{:S(2)}, u32[]{:S(2)}) collective-permute-start(f32[192,768]{1,0:T(8,128)} %tail.27.rest_1_), channel_id=1, source_target_pairs={{0,1},{1,0},{2,3},{3,2},{4,5},{5,4},{6,7},{7,6},{8,9},{9,8},{10,11... | collective-permute-start | bytes 1769480 | tf_op jit(solution)/shard_map/ppermute | solution.py:364
  132.7 2.8 %assemble.1 = (bf16[768,768]{1,0:T(8,128)(2,1)S(1)}, bf16[768,768]{1,0:T(8,128)(2,1)S(1)}, bf16[768,768]{1,0:T(8,128)(2,1)S(1)}, bf16[768,768]{1,0:T(8,128)(2,1)S(1)}) custom-call(s32[1]{0:T(128)} %bitcast.place_ref, f32[384,768]{1,0:T(8,128)} %collective-permute-done.2.refs_0_, f32[384,768]{1,0:T(8,128)S(1)} %copy-done.13, ...), custom_call_target="tpu_custom_call" | custom-call | bytes 10616836 | tf_op jit(solution)/shard_map/assemble/pallas_call | solution.py:26
  135.6 2.7 %own_product.2.acc_ref = f32[384,768]{1,0:T(8,128)S(1)} custom-call(bf16[768,768]{1,0:T(8,128)(2,1)S(1)} %get-tuple-element.50.high_ref, bf16[768,768]{1,0:T(8,128)(2,1)S(1)} %get-tuple-element.51.low_ref, f32[192,768]{1,0:T(8,128)S(1)} %tail.20.rest_0_, f32[192,768]{1,0:T(8,128)} %tail.27.rest_1_), custom_call_target="tpu_custom_call" | custom-call | flops 1358954496 | bytes 4718592 | tf_op jit(solution)/shard_map/own_product/pallas_call | solution.py:26
  138.3 2.6 %own_product.3.acc_ref = f32[384,768]{1,0:T(8,128)S(1)} custom-call(bf16[768,768]{1,0:T(8,128)(2,1)S(1)} %get-tuple-element.50.high_ref, bf16[768,768]{1,0:T(8,128)(2,1)S(1)} %get-tuple-element.51.low_ref, f32[192,384]{1,0:T(8,128)} %get-tuple-element.70.rest_0_, f32[192,384]{1,0:T(8,128)S(1)} %copy-done.2, f32[192,384]{1,0:T(8,128)S(1)} %copy-done.4, ...), custom_call_target="tpu_custom_call" | custom-call | flops 1358954496 | bytes 4718592 | tf_op jit(solution)/shard_map/own_product/pallas_call | solution.py:26
  140.9 2.7 %other_product.3.early_ref = f32[768,384]{1,0:T(8,128)S(1)} custom-call(bf16[768,768]{1,0:T(8,128)(2,1)S(1)} %get-tuple-element.48.high_ref, bf16[768,768]{1,0:T(8,128)(2,1)S(1)} %get-tuple-element.49.low_ref, f32[384,768]{1,0:T(8,128)S(1)} %own_product.3.acc_ref, f32[192,384]{1,0:T(8,128)} %collective-permute-done.41.rest_0_.rest_4_, ...), custom_call_target="tpu_custom_call" | custom-call | flops 1358954496 | bytes 5898240 | tf_op jit(solution)/shard_map/other_product/pallas_call | solution.py:26
  145.4 2.1 %late.1 = (bf16[768,192]{1,0:T(8,128)(2,1)S(1)}, bf16[768,192]{1,0:T(8,128)(2,1)S(1)}, bf16[768,192]{1,0:T(8,128)(2,1)S(1)}, bf16[768,192]{1,0:T(8,128)(2,1)S(1)}) custom-call(f32[384,768]{1,0:T(8,128)} %collective-permute-done.35.before_ref, f32[384,768]{1,0:T(8,128)} %collective-permute-done.36.after_ref), custom_call_target="tpu_custom_call" | custom-call | bytes 3538944 | tf_op jit(solution)/shard_map/late/pallas_call | solution.py:26
  147.5 2.3 %finish.2 = f32[768,384]{1,0:T(8,128)S(1)} custom-call(s32[1]{0:T(128)} %bitcast.place_ref, f32[768,384]{1,0:T(8,128)S(1)} %other_product.2.early_ref, bf16[768,192]{1,0:T(8,128)(2,1)S(1)} %get-tuple-element.86.own_h, bf16[768,192]{1,0:T(8,128)(2,1)S(1)} %get-tuple-element.87.own_l, bf16[768,192]{1,0:T(8,128)(2,1)S(1)} %get-tuple-element.88.other_h, ...), custom_call_target="tpu_custom_call" | custom-call | flops 679477248 | bytes 5898244 | tf_op jit(solution)/shard_map/finish/pallas_call | solution.py:26
  149.9 2.3 %finish.3 = f32[768,384]{1,0:T(8,128)S(1)} custom-call(s32[1]{0:T(128)} %bitcast.place_ref, f32[768,384]{1,0:T(8,128)S(1)} %other_product.3.early_ref, bf16[768,192]{1,0:T(8,128)(2,1)S(1)} %get-tuple-element.86.own_h, bf16[768,192]{1,0:T(8,128)(2,1)S(1)} %get-tuple-element.87.own_l, bf16[768,192]{1,0:T(8,128)(2,1)S(1)} %get-tuple-element.88.other_h, ...), custom_call_target="tpu_custom_call" | custom-call | flops 679477248 | bytes 5898244 | tf_op jit(solution)/shard_map/finish/pallas_call | solution.py:26
  156.8 5.5 %collective-permute-done.39 = f32[2,96,384]{2,1,0:T(8,128)S(1)} collective-permute-done((f32[2,96,384]{2,1,0:T(8,128)S(1)}, f32[2,96,384]{2,1,0:T(8,128)S(1)}, u32[]{:S(2)}, u32[]{:S(2)}) %collective-permute-start.39) | collective-permute-done | bytes 294944 | tf_op jit(solution)/shard_map/ppermute | solution.py:309
  164.5 4.0 %collective-permute-done.45 = f32[2,96,384]{2,1,0:T(8,128)S(1)} collective-permute-done((f32[2,96,384]{2,1,0:T(8,128)S(1)}, f32[2,96,384]{2,1,0:T(8,128)S(1)}, u32[]{:S(2)}, u32[]{:S(2)}) %collective-permute-start.45) | collective-permute-done | bytes 294944 | tf_op jit(solution)/shard_map/ppermute | solution.py:309
  170.9 2.7 %collective-permute-done.40 = f32[96,384]{1,0:T(8,128)S(1)} collective-permute-done((f32[96,384]{1,0:T(8,128)S(1)}, f32[96,384]{1,0:T(8,128)S(1)}, u32[]{:S(2)}, u32[]{:S(2)}) %collective-permute-start.40) | collective-permute-done | bytes 147488 | tf_op jit(solution)/shard_map/ppermute | solution.py:309
  (152 shorter events, 56.9 us)
Async XLA Ops:
  2.2 10.4 %collective-permute-start.5 = (f32[192,384]{1,0:T(8,128)S(1)}, f32[192,384]{1,0:T(8,128)S(1)}, u32[]{:S(2)}, u32[]{:S(2)}) collective-permute-start(f32[192,384]{1,0:T(8,128)S(1)} %get-tuple-element.54.rest_0_.rest_2_.rest_4_), channel_id=1, source_target_pairs={{1,2},{3,4},{5,6},{2,1},{4,3},{6,5},{9,10},{11,12},{13,14},{10,9},... | collective-permute-start | bytes 884744 | tf_op jit(solution)/shard_map/ppermute | solution.py:344
  3.0 15.1 %collective-permute-start.6 = (f32[192,384]{1,0:T(8,128)S(1)}, f32[192,384]{1,0:T(8,128)S(1)}, u32[]{:S(2)}, u32[]{:S(2)}) collective-permute-start(f32[192,384]{1,0:T(8,128)S(1)} %get-tuple-element.55.rest_1_.rest_3_.rest_5_), channel_id=1, source_target_pairs={{0,1},{1,0},{2,3},{3,2},{4,5},{5,4},{6,7},{7,6},{8,9},{9,8},{10,11... | collective-permute-start | bytes 884744 | tf_op jit(solution)/shard_map/ppermute | solution.py:344
  6.0 43.5 %collective-permute-start.3 = (f32[384,768]{1,0:T(8,128)S(1)}, f32[384,768]{1,0:T(8,128)S(1)}, u32[]{:S(2)}, u32[]{:S(2)}) collective-permute-start(f32[384,768]{1,0:T(8,128)S(1)} %constant_dynamic-update-slice_fusion.refs_2_), channel_id=1, source_target_pairs={{24,16},{16,8},{8,0},{25,17},{17,9},{9,1},{26,18},{18,10},{10,2},{... | collective-permute-start | bytes 3538952 | tf_op jit(solution)/shard_map/ppermute | solution.py:271
  8.3 43.5 %collective-permute-start.1 = (f32[384,768]{1,0:T(8,128)S(1)}, f32[384,768]{1,0:T(8,128)S(1)}, u32[]{:S(2)}, u32[]{:S(2)}) collective-permute-start(f32[384,768]{1,0:T(8,128)S(1)} %constant_dynamic-update-slice_fusion.refs_2_), channel_id=1, source_target_pairs={{0,8},{8,16},{16,24},{1,9},{9,17},{17,25},{2,10},{10,18},{18,26},{... | collective-permute-start | bytes 3538952 | tf_op jit(solution)/shard_map/ppermute | solution.py:270
  12.5 11.0 %collective-permute-start.20 = (f32[192,384]{1,0:T(8,128)S(1)}, f32[192,384]{1,0:T(8,128)S(1)}, u32[]{:S(2)}, u32[]{:S(2)}) collective-permute-start(f32[192,384]{1,0:T(8,128)S(1)} %get-tuple-element.73.rest_1_.rest_3_.rest_5_), channel_id=1, source_target_pairs={{0,1},{1,0},{2,3},{3,2},{4,5},{5,4},{6,7},{7,6},{8,9},{9,8},{10,11... | collective-permute-start | bytes 884744 | tf_op jit(solution)/shard_map/ppermute | solution.py:344
  20.6 10.8 %collective-permute-start.8 = (f32[192,384]{1,0:T(8,128)S(1)}, f32[192,384]{1,0:T(8,128)S(1)}, u32[]{:S(2)}, u32[]{:S(2)}) collective-permute-start(f32[192,384]{1,0:T(8,128)S(1)} %get-tuple-element.61.rest_1_.rest_3_), channel_id=1, source_target_pairs={{0,1},{1,0},{2,3},{3,2},{4,5},{5,4},{6,7},{7,6},{8,9},{9,8},{10,11... | collective-permute-start | bytes 884744 | tf_op jit(solution)/shard_map/ppermute | solution.py:344
  24.9 12.6 %collective-permute-start.22 = (f32[192,384]{1,0:T(8,128)S(1)}, f32[192,384]{1,0:T(8,128)S(1)}, u32[]{:S(2)}, u32[]{:S(2)}) collective-permute-start(f32[192,384]{1,0:T(8,128)S(1)} %get-tuple-element.75.rest_1_.rest_3_), channel_id=1, source_target_pairs={{0,1},{1,0},{2,3},{3,2},{4,5},{5,4},{6,7},{7,6},{8,9},{9,8},{10,11... | collective-permute-start | bytes 884744 | tf_op jit(solution)/shard_map/ppermute | solution.py:344
  32.8 10.5 %collective-permute-start.10 = (f32[192,384]{1,0:T(8,128)S(1)}, f32[192,384]{1,0:T(8,128)S(1)}, u32[]{:S(2)}, u32[]{:S(2)}) collective-permute-start(f32[192,384]{1,0:T(8,128)S(1)} %get-tuple-element.63.rest_1_.rest_3_), channel_id=1, source_target_pairs={{0,1},{1,0},{2,3},{3,2},{4,5},{5,4},{6,7},{7,6},{8,9},{9,8},{10,11... | collective-permute-start | bytes 884744 | tf_op jit(solution)/shard_map/ppermute | solution.py:344
  40.1 18.7 %collective-permute-start.24 = (f32[192,384]{1,0:T(8,128)S(1)}, f32[192,384]{1,0:T(8,128)S(1)}, u32[]{:S(2)}, u32[]{:S(2)}) collective-permute-start(f32[192,384]{1,0:T(8,128)S(1)} %get-tuple-element.77.rest_1_.rest_3_), channel_id=1, source_target_pairs={{0,1},{1,0},{2,3},{3,2},{4,5},{5,4},{6,7},{7,6},{8,9},{9,8},{10,11... | collective-permute-start | bytes 884744 | tf_op jit(solution)/shard_map/ppermute | solution.py:344
  44.0 16.2 %collective-permute-start.11 = (f32[192,384]{1,0:T(8,128)S(1)}, f32[192,384]{1,0:T(8,128)S(1)}, u32[]{:S(2)}, u32[]{:S(2)}) collective-permute-start(f32[192,384]{1,0:T(8,128)S(1)} %get-tuple-element.64.rest_0_.rest_2_), channel_id=1, source_target_pairs={{1,2},{3,4},{5,6},{2,1},{4,3},{6,5},{9,10},{11,12},{13,14},{10,9},... | collective-permute-start | bytes 884744 | tf_op jit(solution)/shard_map/ppermute | solution.py:344
  44.7 18.8 %collective-permute-start.12 = (f32[192,384]{1,0:T(8,128)S(1)}, f32[192,384]{1,0:T(8,128)S(1)}, u32[]{:S(2)}, u32[]{:S(2)}) collective-permute-start(f32[192,384]{1,0:T(8,128)S(1)} %get-tuple-element.65.rest_1_.rest_3_), channel_id=1, source_target_pairs={{0,1},{1,0},{2,3},{3,2},{4,5},{5,4},{6,7},{7,6},{8,9},{9,8},{10,11... | collective-permute-start | bytes 884744 | tf_op jit(solution)/shard_map/ppermute | solution.py:344
  49.5 42.8 %collective-permute-start.4 = (f32[384,768]{1,0:T(8,128)S(1)}, f32[384,768]{1,0:T(8,128)}, u32[]{:S(2)}, u32[]{:S(2)}) collective-permute-start(f32[384,768]{1,0:T(8,128)S(1)} %collective-permute-done.3.refs_3_), channel_id=1, source_target_pairs={{16,8},{8,0},{17,9},{9,1},{18,10},{10,2},{19,11},{11,3},{20,12},{1... | collective-permute-start | bytes 3538952 | tf_op jit(solution)/shard_map/ppermute | solution.py:271
  51.9 42.7 %collective-permute-start.2 = (f32[384,768]{1,0:T(8,128)S(1)}, f32[384,768]{1,0:T(8,128)}, u32[]{:S(2)}, u32[]{:S(2)}) collective-permute-start(f32[384,768]{1,0:T(8,128)S(1)} %collective-permute-done.1.refs_1_), channel_id=1, source_target_pairs={{8,16},{16,24},{9,17},{17,25},{10,18},{18,26},{11,19},{19,27},{12,... | collective-permute-start | bytes 3538952 | tf_op jit(solution)/shard_map/ppermute | solution.py:270
  60.2 10.1 %collective-permute-start.26 = (f32[192,384]{1,0:T(8,128)S(1)}, f32[192,384]{1,0:T(8,128)S(1)}, u32[]{:S(2)}, u32[]{:S(2)}) collective-permute-start(f32[192,384]{1,0:T(8,128)S(1)} %get-tuple-element.79.rest_1_.rest_3_), channel_id=1, source_target_pairs={{0,1},{1,0},{2,3},{3,2},{4,5},{5,4},{6,7},{7,6},{8,9},{9,8},{10,11... | collective-permute-start | bytes 884744 | tf_op jit(solution)/shard_map/ppermute | solution.py:344
  66.1 11.9 %collective-permute-start.14 = (f32[192,384]{1,0:T(8,128)S(1)}, f32[192,384]{1,0:T(8,128)S(1)}, u32[]{:S(2)}, u32[]{:S(2)}) collective-permute-start(f32[192,384]{1,0:T(8,128)S(1)} %get-tuple-element.67.rest_1_.rest_3_), channel_id=1, source_target_pairs={{0,1},{1,0},{2,3},{3,2},{4,5},{5,4},{6,7},{7,6},{8,9},{9,8},{10,11... | collective-permute-start | bytes 884744 | tf_op jit(solution)/shard_map/ppermute | solution.py:344
  71.8 12.6 %collective-permute-start.28 = (f32[192,384]{1,0:T(8,128)S(1)}, f32[192,384]{1,0:T(8,128)S(1)}, u32[]{:S(2)}, u32[]{:S(2)}) collective-permute-start(f32[192,384]{1,0:T(8,128)S(1)} %get-tuple-element.81.rest_1_.rest_3_), channel_id=1, source_target_pairs={{0,1},{1,0},{2,3},{3,2},{4,5},{5,4},{6,7},{7,6},{8,9},{9,8},{10,11... | collective-permute-start | bytes 884744 | tf_op jit(solution)/shard_map/ppermute | solution.py:344
  79.5 10.8 %collective-permute-start.16 = (f32[192,384]{1,0:T(8,128)S(1)}, f32[192,384]{1,0:T(8,128)S(1)}, u32[]{:S(2)}, u32[]{:S(2)}) collective-permute-start(f32[192,384]{1,0:T(8,128)S(1)} %get-tuple-element.69.rest_1_), channel_id=1, source_target_pairs={{0,1},{1,0},{2,3},{3,2},{4,5},{5,4},{6,7},{7,6},{8,9},{9,8},{10,11... | collective-permute-start | bytes 884744 | tf_op jit(solution)/shard_map/ppermute | solution.py:344
  87.1 21.5 %collective-permute-start.30 = (f32[192,384]{1,0:T(8,128)S(1)}, f32[192,384]{1,0:T(8,128)S(1)}, u32[]{:S(2)}, u32[]{:S(2)}) collective-permute-start(f32[192,384]{1,0:T(8,128)S(1)} %get-tuple-element.83.rest_1_), channel_id=1, source_target_pairs={{0,1},{1,0},{2,3},{3,2},{4,5},{5,4},{6,7},{7,6},{8,9},{9,8},{10,11... | collective-permute-start | bytes 884744 | tf_op jit(solution)/shard_map/ppermute | solution.py:344
  91.6 23.9 %collective-permute-start.18 = (f32[192,384]{1,0:T(8,128)S(1)}, f32[192,384]{1,0:T(8,128)S(1)}, u32[]{:S(2)}, u32[]{:S(2)}) collective-permute-start(f32[192,384]{1,0:T(8,128)S(1)} %get-tuple-element.71.rest_1_), channel_id=1, source_target_pairs={{0,1},{1,0},{2,3},{3,2},{4,5},{5,4},{6,7},{7,6},{8,9},{9,8},{10,11... | collective-permute-start | bytes 884744 | tf_op jit(solution)/shard_map/ppermute | solution.py:344
  91.6 24.5 %collective-permute-start.17 = (f32[192,384]{1,0:T(8,128)}, f32[192,384]{1,0:T(8,128)S(1)}, u32[]{:S(2)}, u32[]{:S(2)}) collective-permute-start(f32[192,384]{1,0:T(8,128)} %get-tuple-element.70.rest_0_), channel_id=1, source_target_pairs={{1,2},{3,4},{5,6},{2,1},{4,3},{6,5},{9,10},{11,12},{13,14},{10,9},... | collective-permute-start | bytes 884744 | tf_op jit(solution)/shard_map/ppermute | solution.py:344
  92.3 53.1 %collective-permute-start.36 = (f32[384,768]{1,0:T(8,128)}, f32[384,768]{1,0:T(8,128)}, u32[]{:S(2)}, u32[]{:S(2)}) collective-permute-start(f32[384,768]{1,0:T(8,128)} %collective-permute-done.4.refs_4_), channel_id=1, source_target_pairs={{8,0},{9,1},{10,2},{11,3},{12,4},{13,5},{14,6},{15,7}} | collective-permute-start | bytes 3538952 | tf_op jit(solution)/shard_map/ppermute | solution.py:271
  94.6 50.8 %collective-permute-start.35 = (f32[384,768]{1,0:T(8,128)}, f32[384,768]{1,0:T(8,128)}, u32[]{:S(2)}, u32[]{:S(2)}) collective-permute-start(f32[384,768]{1,0:T(8,128)} %collective-permute-done.2.refs_0_), channel_id=1, source_target_pairs={{16,24},{17,25},{18,26},{19,27},{20,28},{21,29},{22,30},{23,31}} | collective-permute-start | bytes 3538952 | tf_op jit(solution)/shard_map/ppermute | solution.py:270
  109.4 15.6 %collective-permute-start.32 = (f32[192,384]{1,0:T(8,128)S(1)}, f32[192,384]{1,0:T(8,128)S(1)}, u32[]{:S(2)}, u32[]{:S(2)}) collective-permute-start(f32[192,384]{1,0:T(8,128)S(1)} %get-tuple-element.85.rest_1_.rest_3_), channel_id=1, source_target_pairs={{0,1},{1,0},{2,3},{3,2},{4,5},{5,4},{6,7},{7,6},{8,9},{9,8},{10,11... | collective-permute-start | bytes 884744 | tf_op jit(solution)/shard_map/ppermute | solution.py:344
  116.1 13.3 %collective-permute-start.42 = (f32[192,384]{1,0:T(8,128)S(1)}, f32[192,384]{1,0:T(8,128)S(1)}, u32[]{:S(2)}, u32[]{:S(2)}) collective-permute-start(f32[192,384]{1,0:T(8,128)S(1)} %get-tuple-element.84.rest_0_.rest_2_), channel_id=1, source_target_pairs={{0,1},{1,0},{2,3},{3,2},{4,5},{5,4},{6,7},{7,6},{8,9},{9,8},{10,11... | collective-permute-start | bytes 884744 | tf_op jit(solution)/shard_map/ppermute | solution.py:362
  125.0 18.7 %collective-permute-start.33 = (f32[192,768]{1,0:T(8,128)S(1)}, f32[192,768]{1,0:T(8,128)S(1)}, u32[]{:S(2)}, u32[]{:S(2)}) collective-permute-start(f32[192,768]{1,0:T(8,128)S(1)} %tail.20.rest_0_), channel_id=1, source_target_pairs={{0,1},{1,0},{2,3},{3,2},{4,5},{5,4},{6,7},{7,6},{8,9},{9,8},{10,11... | collective-permute-start | bytes 1769480 | tf_op jit(solution)/shard_map/ppermute | solution.py:364
  126.7 17.0 %collective-permute-start.34 = (f32[192,768]{1,0:T(8,128)}, f32[192,768]{1,0:T(8,128)S(1)}, u32[]{:S(2)}, u32[]{:S(2)}) collective-permute-start(f32[192,768]{1,0:T(8,128)} %tail.27.rest_1_), channel_id=1, source_target_pairs={{0,1},{1,0},{2,3},{3,2},{4,5},{5,4},{6,7},{7,6},{8,9},{9,8},{10,11... | collective-permute-start | bytes 1769480 | tf_op jit(solution)/shard_map/ppermute | solution.py:364
  130.2 10.7 %collective-permute-start.41 = (f32[192,384]{1,0:T(8,128)}, f32[192,384]{1,0:T(8,128)}, u32[]{:S(2)}, u32[]{:S(2)}) collective-permute-start(f32[192,384]{1,0:T(8,128)} %get-tuple-element.70.rest_0_), channel_id=1, source_target_pairs={{0,1},{1,0},{2,3},{3,2},{4,5},{5,4},{6,7},{7,6},{8,9},{9,8},{10,11... | collective-permute-start | bytes 884744 | tf_op jit(solution)/shard_map/ppermute | solution.py:362
  152.4 9.9 %collective-permute-start.39 = (f32[2,96,384]{2,1,0:T(8,128)S(1)}, f32[2,96,384]{2,1,0:T(8,128)S(1)}, u32[]{:S(2)}, u32[]{:S(2)}) collective-permute-start(f32[2,96,384]{2,1,0:T(8,128)S(1)} %dynamic-slice_bitcast_fusion.2), channel_id=1, source_target_pairs={{0,4},{1,5},{2,6},{3,7},{4,0},{5,1},{6,2},{7,3},{8,12},{9,13},{10,... | collective-permute-start | bytes 884744 | tf_op jit(solution)/shard_map/ppermute | solution.py:309
  154.1 10.0 %collective-permute-start.37 = (f32[2,96,384]{2,1,0:T(8,128)S(1)}, f32[2,96,384]{2,1,0:T(8,128)S(1)}, u32[]{:S(2)}, u32[]{:S(2)}) collective-permute-start(f32[2,96,384]{2,1,0:T(8,128)S(1)} %dynamic-slice_bitcast_fusion.3), channel_id=1, source_target_pairs={{0,2},{1,3},{2,0},{3,1},{4,6},{5,7},{6,4},{7,5},{8,10},{9,11},{10,... | collective-permute-start | bytes 884744 | tf_op jit(solution)/shard_map/ppermute | solution.py:309
  154.2 14.4 %collective-permute-start.45 = (f32[2,96,384]{2,1,0:T(8,128)S(1)}, f32[2,96,384]{2,1,0:T(8,128)S(1)}, u32[]{:S(2)}, u32[]{:S(2)}) collective-permute-start(f32[2,96,384]{2,1,0:T(8,128)S(1)} %dynamic-slice_bitcast_fusion), channel_id=1, source_target_pairs={{0,4},{1,5},{2,6},{3,7},{4,0},{5,1},{6,2},{7,3},{8,12},{9,13},{10,... | collective-permute-start | bytes 884744 | tf_op jit(solution)/shard_map/ppermute | solution.py:309
  155.1 15.3 %collective-permute-start.43 = (f32[2,96,384]{2,1,0:T(8,128)S(1)}, f32[2,96,384]{2,1,0:T(8,128)S(1)}, u32[]{:S(2)}, u32[]{:S(2)}) collective-permute-start(f32[2,96,384]{2,1,0:T(8,128)S(1)} %dynamic-slice_bitcast_fusion.1), channel_id=1, source_target_pairs={{0,2},{1,3},{2,0},{3,1},{4,6},{5,7},{6,4},{7,5},{8,10},{9,11},{10,... | collective-permute-start | bytes 884744 | tf_op jit(solution)/shard_map/ppermute | solution.py:309
  162.3 11.2 %collective-permute-start.40 = (f32[96,384]{1,0:T(8,128)S(1)}, f32[96,384]{1,0:T(8,128)S(1)}, u32[]{:S(2)}, u32[]{:S(2)}) collective-permute-start(f32[96,384]{1,0:T(8,128)S(1)} %dynamic-slice_bitcast_fusion.6), channel_id=1, source_target_pairs={{0,2},{1,3},{2,0},{3,1},{4,6},{5,7},{6,4},{7,5},{8,10},{9,11},{10,... | collective-permute-start | bytes 442376 | tf_op jit(solution)/shard_map/ppermute | solution.py:309
  (30 other events, 221.3 us)
